TPU v7x, 128 devices: a whole 4x4x4 slice. The times are simulated.
128 devices in a mesh: brick: 16 (over y, x), sub: 8 (over z, core).
Axes of the slice: x: 4, y: 4, z: 4, core: 2. Of those that a mesh axis runs over, the one named last changes fastest.
Arguments:
- atom_features: bfloat16 [16, 8, 1024, 256], P('brick', 'sub'), may hold values from -6 to 6
- positions: float32 [3, 16, 8, 1024], P(None, 'brick', 'sub')
- charges: float32 [16, 8, 1024], P('brick', 'sub'), may hold values from -0.8 to 0.8
- slot_index: int32 [6144, 64], P(('brick', 'sub')), may hold values from 0 to 9215, as said below
- atom_count: int32 [6144], P(('brick', 'sub')), may hold values from 12 to 60
- cap_weight: float32 [6144, 64], P(('brick', 'sub')), may hold values from 0.25 to 1
- tile_pairs: int32 [2, 16, 8, 128], P(None, 'brick', 'sub'), may hold values from 0 to 71, as said below
- tile_count: int32 [16, 8], P('brick', 'sub'), may hold values from 16 to 128
- w_qkv: bfloat16 [2, 256, 768], replicated, may hold values from -0.375 to 0.375
- w_out: bfloat16 [2, 256, 256], replicated, may hold values from -0.375 to 0.375
- gains: float32 [3, 256], replicated, may hold values from 0.5 to 1.5
- rates: float32 [2, 8], replicated, may hold values from 0.05 to 1
- w_read: bfloat16 [256, 128], replicated, may hold values from -0.375 to 0.375
- w_energy: float32 [128], replicated, may hold values from -0.5 to 0.5
Outputs:
- forces: float32 [3, 16, 8, 1024], P(None, 'brick', 'sub')
- total_energy: float32 [], replicated
Inputs may be any that keep to these rules, and one draw needn't show every extreme that they name: `slot_index`: A fragment's slots name distinct rows, all from the blocks of two devices that are adjacent to each other, each within one step along brick and along sub of the fragment's own device and inside the mesh. `tile_pairs`: row 0 names an own tile below 8, row 1 a neighbourhood tile.
All inputs are finite; a program needn't handle non-finite values.
Results may differ from a plain program's by a relative error of at most 0.009.
Values may be sent and summed in bfloat16 or wider, within the bound.
A program may use at most 64 MiB of HBM per device.

v0:
```python
import math

import jax
import jax.numpy as jnp
from jax import lax
from jax.sharding import PartitionSpec as P

LAYERS = 2
BLOCK_FRAGS = 8
TILE = 128
TILE_BLOCK = 16
TILE_CAP = 128


NORM_EPS = 1e-05
PAIR_SOFTEN = 0.01
SCREEN_RATE = 0.1
COULOMB_UNIT = 14.4
CHARGE_SOFTEN = 1.0


def with_halo(x, sides, width):
    for axis, dim in sides:
        devices, length = (lax.axis_size(axis), x.shape[dim])
        up = [(i, (i + 1) % devices) for i in range(devices - 1)]
        down = [(j, i) for i, j in up]
        last = lax.slice_in_dim(x, length - width, length, axis=dim)
        initial = lax.slice_in_dim(x, 0, width, axis=dim)
        before = lax.ppermute(last, axis, up)
        after = lax.ppermute(initial, axis, down)
        x = jnp.concatenate([before, x, after], axis=dim)
    return x


def norm_rows(hidden, gain_row):
    centre = jnp.mean(hidden, axis=-1, keepdims=True)
    spread = jnp.mean((hidden - centre) ** 2, axis=-1, keepdims=True)
    return (hidden - centre) * lax.rsqrt(spread + NORM_EPS) * gain_row


def block_energy(coords, features, living, weight, w_qkv, w_out, gains, rates, w_read, w_energy):
    pair_count, block_rows, feature_width = features.shape
    head_count = rates.shape[1]
    head_dim = feature_width // head_count
    offset = coords[:, :, :, None] - coords[:, :, None, :]
    distance = jnp.sqrt(jnp.sum(offset * offset, axis=1) + PAIR_SOFTEN)
    halves = jnp.arange(block_rows, dtype=jnp.int32) // (block_rows // 2)
    same_frag = (halves[:, None] == halves[None, :]).astype(jnp.float32)
    pair_mask = living[:, :, None] * living[:, None, :] * same_frag
    hidden = features.astype(jnp.float32).reshape(pair_count * block_rows, feature_width)
    for layer_index in range(LAYERS):
        normed = norm_rows(hidden, gains[layer_index]).astype(jnp.bfloat16)
        project = jnp.dot(normed, w_qkv[layer_index], preferred_element_type=jnp.float32).astype(
            jnp.bfloat16
        )
        project = project.reshape(pair_count, block_rows, 3, head_count, head_dim)
        queries = project[:, :, 0]
        key_rows = project[:, :, 1]
        values = project[:, :, 2]
        scores = jnp.einsum(
            "pihd,pjhd->phij", queries, key_rows, preferred_element_type=jnp.float32
        ) / math.sqrt(head_dim)
        damping = 1.0 / (1.0 + rates[layer_index][None, :, None, None] * distance[:, None])
        attend = (jax.nn.silu(scores) * damping * pair_mask[:, None]).astype(jnp.bfloat16)
        message = jnp.einsum("phij,pjhd->pihd", attend, values, preferred_element_type=jnp.float32)
        message = message.astype(jnp.bfloat16).reshape(pair_count * block_rows, feature_width)
        hidden = hidden + jnp.dot(message, w_out[layer_index], preferred_element_type=jnp.float32)
    normed = norm_rows(hidden, gains[LAYERS]).astype(jnp.bfloat16)
    readout = jax.nn.silu(jnp.dot(normed, w_read, preferred_element_type=jnp.float32))
    energy = jnp.dot(readout, w_energy, precision=lax.Precision.HIGHEST)
    return jnp.sum(energy * (living * weight).reshape(-1))


def fragment_model(
    received,
    places,
    slot_index,
    atom_count,
    cap_weight,
    w_qkv,
    w_out,
    gains,
    rates,
    w_read,
    w_energy,
):
    frag_count, slot_count = slot_index.shape
    feature_width = received.shape[1]
    blocks = frag_count // BLOCK_FRAGS
    pair_count = BLOCK_FRAGS // 2
    slot_rows = slot_index.reshape(-1)
    living = (jnp.arange(slot_count, dtype=jnp.int32)[None, :] < atom_count[:, None]).astype(
        jnp.float32
    )
    features = received[slot_rows].reshape(blocks, pair_count, 2 * slot_count, feature_width)
    coords = (
        places[:, slot_rows].reshape(3, blocks, pair_count, 2 * slot_count).transpose(1, 2, 0, 3)
    )
    alive_blocks = living.reshape(blocks, pair_count, 2 * slot_count)
    weight_blocks = cap_weight.reshape(blocks, pair_count, 2 * slot_count)

    def one_block(inputs):
        coord_block, feature_block, alive_block, weight_block = inputs

        def energy_of(coord_value):
            return block_energy(
                coord_value,
                feature_block,
                alive_block,
                weight_block,
                w_qkv,
                w_out,
                gains,
                rates,
                w_read,
                w_energy,
            )

        energy, pullback = jax.vjp(energy_of, coord_block)
        gradient = pullback(jnp.ones_like(energy))[0]
        return (energy, -gradient)

    energies, slot_force = lax.map(one_block, (coords, features, alive_blocks, weight_blocks))
    slot_force = slot_force.transpose(2, 0, 1, 3).reshape(3, -1) * living.reshape(-1)
    row_force = jnp.zeros((3, received.shape[0]), jnp.float32).at[:, slot_rows].add(slot_force)
    return (jnp.sum(energies), row_force)


def solvent_pairs(own_atoms, neighbours, own_list, near_list, tile_live, loop_count):
    tile_size = TILE
    own_tiles = own_atoms.reshape(4, -1, tile_size)
    near_tiles = neighbours.reshape(4, -1, tile_size)
    centre = 4 * own_atoms.shape[1]
    lane_ids = jnp.arange(tile_size, dtype=jnp.int32)
    gauss_slope = 2.0 * SCREEN_RATE / math.sqrt(math.pi)

    def visit_block(index, state_now):
        tile_force, energy = state_now
        start = index * TILE_BLOCK
        own_pick = lax.dynamic_slice_in_dim(own_list, start, TILE_BLOCK)
        near_pick = lax.dynamic_slice_in_dim(near_list, start, TILE_BLOCK)
        active = (start + jnp.arange(TILE_BLOCK, dtype=jnp.int32) < tile_live).astype(jnp.float32)
        own_block = own_tiles[:, own_pick]
        near_block = near_tiles[:, near_pick]
        offset = own_block[:3, :, :, None] - near_block[:3, :, None, :]
        square = jnp.sum(offset * offset, axis=0) + CHARGE_SOFTEN
        radius = jnp.sqrt(square)
        own_ids = centre + own_pick[:, None] * tile_size + lane_ids[None, :]
        near_ids = near_pick[:, None] * tile_size + lane_ids[None, :]
        distinct = (own_ids[:, :, None] != near_ids[:, None, :]).astype(jnp.float32)
        charge = (
            own_block[3][:, :, None] * near_block[3][:, None, :] * distinct * active[:, None, None]
        )
        screened = jax.scipy.special.erfc(SCREEN_RATE * radius) / radius
        energy = energy + 0.5 * COULOMB_UNIT * jnp.sum(charge * screened)
        strength = (
            COULOMB_UNIT
            * charge
            * (screened + gauss_slope * jnp.exp(-SCREEN_RATE * SCREEN_RATE * square))
            / square
        )
        pull_force = jnp.sum(strength[None] * offset, axis=3)
        tile_force = tile_force.at[:, own_pick].add(pull_force)
        return (tile_force, energy)

    start_state = (
        jnp.zeros((3, own_tiles.shape[1], tile_size), jnp.float32),
        jnp.zeros((), jnp.float32),
    )
    tile_force, energy = lax.fori_loop(0, loop_count, visit_block, start_state)
    return (energy, tile_force.reshape(3, -1))


def body(
    atom_features,
    positions,
    charges,
    slot_index,
    atom_count,
    cap_weight,
    tile_pairs,
    tile_count,
    w_qkv,
    w_out,
    gains,
    rates,
    w_read,
    w_energy,
):
    own_size = atom_features.shape[2]
    feature_width = atom_features.shape[3]
    atom_table = jnp.concatenate([positions, charges[None]], axis=0)
    neighbours = with_halo(atom_table, (("brick", 1), ("sub", 2)), 1).reshape(4, -1)
    near_features = with_halo(atom_features, (("brick", 0), ("sub", 1)), 1)
    ml_energy, row_force = fragment_model(
        near_features.reshape(-1, feature_width),
        neighbours[:3],
        slot_index,
        atom_count,
        cap_weight,
        w_qkv,
        w_out,
        gains,
        rates,
        w_read,
        w_energy,
    )
    tile_live = tile_count[0, 0]
    loop_count = TILE_CAP // TILE_BLOCK
    mm_energy, mm_force = solvent_pairs(
        atom_table.reshape(4, -1),
        neighbours,
        tile_pairs[0, 0, 0],
        tile_pairs[1, 0, 0],
        tile_live,
        loop_count,
    )
    returned = with_halo(
        row_force.reshape(3, 3, 3, own_size).astype(jnp.bfloat16), (("brick", 1), ("sub", 2)), 1
    ).astype(jnp.float32)
    ml_force = jnp.sum(returned[:, ::2, ::2], axis=(1, 2))
    energy_sum = lax.psum(ml_energy + mm_energy, ("brick", "sub"))
    return ((ml_force + mm_force).reshape(3, 1, 1, own_size), energy_sum)


def solution(mesh):
    in_specs = (
        P("brick", "sub", None, None),
        P(None, "brick", "sub", None),
        P("brick", "sub", None),
        P(("brick", "sub"), None),
        P(("brick", "sub")),
        P(("brick", "sub"), None),
        P(None, "brick", "sub", None),
        P("brick", "sub"),
        P(),
        P(),
        P(),
        P(),
        P(),
        P(),
    )
    out_specs = (P(None, "brick", "sub", None), P())
    return jax.shard_map(body, mesh=mesh, in_specs=in_specs, out_specs=out_specs, check_vma=False)
```

profile of v0, /device:TPU:1, one launch (start us, length us, event | category | flops | bytes accessed | tf_op | source)
XLA Modules:
  0.0 504.4 jit_solution(9763239967571849462)
XLA Ops:
  0.7 4.1 collective-permute-start
  6.8 4.0 collective-permute-start.4
  16.8 2.6 collective-permute-done.1
  19.4 5.5 %collective-permute-start.2 = (bf16[3,1,1024,256]{3,2,1,0:T(8,128)(2,1)S(1)}, bf16[3,1,1024,256]{3,2,1,0:T(8,128)(2,1)}, u32[]{:S(2)}, u32[]{:S(2)}) collective-permute-start(bf16[3,1,1024,256]{3,2,1,0:T(8,128)(2,1)S(1)} %constant_dynamic-update-slice_fusion), channel_id=1, source_target_pairs={{0,1},{1,2},{2,3},{3,4},{4,5},{5,6},{6,7},{8,9},{9,10},{10,11},{11... | collective-permute-start | bytes 4718600 | tf_op jit(solution)/shard_map/ppermute | solution.py:29
  27.5 3.6 collective-permute-start.6
  34.4 8.4 %collective-permute-done.6 = f32[4,3,1,1024]{3,2,1,0:T(1,128)S(1)} collective-permute-done((f32[4,3,1,1024]{3,2,1,0:T(1,128)S(1)}, f32[4,3,1,1024]{3,2,1,0:T(1,128)S(1)}, u32[]{:S(2)}, u32[]{:S(2)}) %collective-permute-start.6) | collective-permute-done | bytes 49184 | tf_op jit(solution)/shard_map/ppermute | solution.py:29
  42.8 4.4 collective-permute-done.7
  48.0 2.9 copy.128
  50.9 10.4 %gather_fusion.3 = f32[3072,3]{1,0:T(8,128)S(1)} fusion(f32[3,9216]{0,1:T(8,128)} %bitcast.300, s32[3072]{0:T(1024)S(1)} %broadcast_clamp_fusion), kind=kCustom, calls=%fused_computation.3 | custom fusion | bytes 86016 | tf_op jit(solution)/shard_map/gather | solution.py:97
  62.4 3.8 pad_maximum_fusion
  66.2 15.2 %gather_fusion.2 = bf16[3072,256]{1,0:T(8,128)(2,1)} fusion(bf16[9216,256]{1,0:T(8,128)(2,1)} %bitcast.289, s32[3072]{0:T(1024)S(1)} %broadcast_clamp_fusion), kind=kCustom, calls=%fused_computation.2 | custom fusion | bytes 3158016 | tf_op jit(solution)/shard_map/gather | solution.py:95
  81.4 222.6 %while.32 = (s32[]{:T(128)}, f32[6]{0:T(128)}, f32[6,4,3,128]{3,2,1,0:T(4,128)}, bf16[6,4,128,256]{3,2,1,0:T(8,128)(2,1)}, f32[3,256]{1,0:T(4,128)S(1)}, /*index...) while((s32[]{:T(128)}, f32[6]{0:T(128)}, ...), condition=%wide.region_19.20_spmd, body=%wide.region_0.19_spmd.sunk | while | flops 1292415488 | bytes 95351416 | solution.py:123
  90.1 2.4 multiply_convert_fusion.17
  96.3 1.9 convolution_convert_fusion.19
  103.1 4.1 multiply_reduce_fusion.30
  113.6 2.7 multiply_reduce_fusion.33
  127.1 2.4 multiply_convert_fusion.17
  133.3 1.9 convolution_convert_fusion.19
  140.1 4.1 multiply_reduce_fusion.30
  150.6 2.7 multiply_reduce_fusion.33
  164.1 2.4 multiply_convert_fusion.17
  177.2 4.1 multiply_reduce_fusion.30
  187.6 2.7 multiply_reduce_fusion.33
  201.2 2.4 multiply_convert_fusion.17
  214.2 4.1 multiply_reduce_fusion.30
  224.6 2.7 multiply_reduce_fusion.33
  238.2 2.4 multiply_convert_fusion.17
  251.2 4.1 multiply_reduce_fusion.30
  261.7 2.7 multiply_reduce_fusion.33
  275.2 2.4 multiply_convert_fusion.17
  281.5 1.9 convolution_convert_fusion.19
  288.3 4.1 multiply_reduce_fusion.30
  298.7 2.7 multiply_reduce_fusion.33
  305.4 19.4 %scatter_custom_fusion.1 = f32[3,9216]{0,1:T(8,128)} fusion(s32[3072]{0:T(1024)} %bitcast.325, f32[3072,3]{1,0:T(8,128)S(1)} %copy.131, f32[]{:T(128)} %constant.405.clone.1), kind=kCustom, calls=%fused_computation.196 | custom fusion | flops 9216 | bytes 111104 | tf_op jit(solution)/shard_map/scatter-add | solution.py:125
  324.8 2.5 convert_element_type.245
  329.8 3.1 collective-permute-start.8
  335.9 2.0 collective-permute-done.9
  338.0 3.2 collective-permute-start.10
  343.1 89.6 %while.33 = (s32[]{:T(128)}, f32[3,8,128]{2,0,1:T(4,128)S(1)}, f32[]{:T(128)}, s32[128]{0:T(128)S(1)}, s32[128]{0:T(128)S(1)}, /*index=5*/f32[4,8,128]{2,0,1:T(4...) while((s32[]{:T(128)}, f32[3,8,128]{2,0,1:T(4,128)S(1)}, ...), condition=%wide.region_27.28_spmd.clone.clone, body=%wide.region_22.27_spmd.clone.clone.sunk | while | flops 25434308 | bytes 7939283 | solution.py:170
  346.3 3.5 multiply_reduce_fusion.34
  357.5 3.5 multiply_reduce_fusion.34
  368.8 3.5 multiply_reduce_fusion.34
  380.0 3.5 multiply_reduce_fusion.34
  391.2 3.5 multiply_reduce_fusion.34
  402.4 3.5 multiply_reduce_fusion.34
  413.6 3.5 multiply_reduce_fusion.34
  424.8 3.5 multiply_reduce_fusion.34
  434.3 68.9 %psum.7 = f32[]{:T(128)} all-reduce(f32[]{:T(128)S(6)} %add.328), channel_id=1, replica_groups=mesh['brick'=16,'sub'=8] {'brick','sub'}, use_global_device_ids=true, to_apply=%region_29.30 | all-reduce | flops 1 | bytes 8 | tf_op jit(solution)/shard_map/psum | solution.py:222
  (805 shorter events, 240.3 us)
Async XLA Ops:
  0.6 26.8 %copy-start.17 = (f32[1,1,1024]{2,1,0:T(1,128)S(1)}, f32[1,1,1024]{2,1,0:T(1,128)}, u32[]{:S(2)}) copy-start(f32[1,1,1024]{2,1,0:T(1,128)} %param.20) | copy-start | bytes 12292
  0.6 26.8 %copy-start.15 = (f32[3,1,1,1024]{3,2,1,0:T(1,128)S(1)}, f32[3,1,1,1024]{3,2,1,0:T(1,128)}, u32[]{:S(2)}) copy-start(f32[3,1,1,1024]{3,2,1,0:T(1,128)} %param.19) | copy-start | bytes 36868
  0.7 32.5 %copy-start.28 = (s32[2,1,1,128]{3,2,1,0:T(1,128)S(1)}, s32[2,1,1,128]{3,2,1,0:T(1,128)}, u32[]{:S(2)}) copy-start(s32[2,1,1,128]{3,2,1,0:T(1,128)} %param.24) | copy-start | bytes 3076
  0.7 33.0 %copy-start.25 = (f32[48,64]{1,0:T(8,128)S(1)}, f32[48,64]{1,0:T(8,128)}, u32[]{:S(2)}) copy-start(f32[48,64]{1,0:T(8,128)} %param.23) | copy-start | bytes 36868
  0.7 15.0 %collective-permute-start = (bf16[1,1,1024,256]{3,2,1,0:T(8,128)(2,1)}, bf16[1,1,1024,256]{3,2,1,0:T(8,128)(2,1)S(1)}, u32[]{:S(2)}, u32[]{:S(2)}) collective-permute-start(bf16[1,1,1024,256]{3,2,1,0:T(8,128)(2,1)} %param.18), channel_id=1, source_target_pairs={{0,8},{8,16},{16,24},{24,32},{32,40},{40,48},{48,56},{56,64},{64,7... | collective-permute-start | bytes 1572872 | tf_op jit(solution)/shard_map/ppermute | solution.py:29
  4.8 14.6 %collective-permute-start.1 = (bf16[1,1,1024,256]{3,2,1,0:T(8,128)(2,1)}, bf16[1,1,1024,256]{3,2,1,0:T(8,128)(2,1)S(1)}, u32[]{:S(2)}, u32[]{:S(2)}) collective-permute-start(bf16[1,1,1024,256]{3,2,1,0:T(8,128)(2,1)} %param.18), channel_id=1, source_target_pairs={{8,0},{16,8},{24,16},{32,24},{40,32},{48,40},{56,48},{64,56},{72,6... | collective-permute-start | bytes 1572872 | tf_op jit(solution)/shard_map/ppermute | solution.py:30
  6.8 20.0 %collective-permute-start.4 = (f32[4,1,1,1024]{3,2,1,0:T(1,128)S(1)}, f32[4,1,1,1024]{3,2,1,0:T(1,128)S(1)}, u32[]{:S(2)}, u32[]{:S(2)}) collective-permute-start(f32[4,1,1,1024]{3,2,1,0:T(1,128)S(1)} %pad_maximum_fusion.7), channel_id=1, source_target_pairs={{0,8},{8,16},{16,24},{24,32},{32,40},{40,48},{48,56},{56,64},{64,7... | collective-permute-start | bytes 49160 | tf_op jit(solution)/shard_map/ppermute | solution.py:29
  10.8 16.6 %collective-permute-start.5 = (f32[4,1,1,1024]{3,2,1,0:T(1,128)S(1)}, f32[4,1,1,1024]{3,2,1,0:T(1,128)S(1)}, u32[]{:S(2)}, u32[]{:S(2)}) collective-permute-start(f32[4,1,1,1024]{3,2,1,0:T(1,128)S(1)} %pad_maximum_fusion.7), channel_id=1, source_target_pairs={{8,0},{16,8},{24,16},{32,24},{40,32},{48,40},{56,48},{64,56},{72,6... | collective-permute-start | bytes 49160 | tf_op jit(solution)/shard_map/ppermute | solution.py:30
  19.4 43.0 %collective-permute-start.2 = (bf16[3,1,1024,256]{3,2,1,0:T(8,128)(2,1)S(1)}, bf16[3,1,1024,256]{3,2,1,0:T(8,128)(2,1)}, u32[]{:S(2)}, u32[]{:S(2)}) collective-permute-start(bf16[3,1,1024,256]{3,2,1,0:T(8,128)(2,1)S(1)} %constant_dynamic-update-slice_fusion), channel_id=1, source_target_pairs={{0,1},{1,2},{2,3},{3,4},{4,5},{5,6},{6,7},{8,9},{9,10},{10,11},{11... | collective-permute-start | bytes 4718600 | tf_op jit(solution)/shard_map/ppermute | solution.py:29
  24.9 37.5 %collective-permute-start.3 = (bf16[3,1,1024,256]{3,2,1,0:T(8,128)(2,1)S(1)}, bf16[3,1,1024,256]{3,2,1,0:T(8,128)(2,1)}, u32[]{:S(2)}, u32[]{:S(2)}) collective-permute-start(bf16[3,1,1024,256]{3,2,1,0:T(8,128)(2,1)S(1)} %constant_dynamic-update-slice_fusion), channel_id=1, source_target_pairs={{1,0},{2,1},{3,2},{4,3},{5,4},{6,5},{7,6},{9,8},{10,9},{11,10},{12... | collective-permute-start | bytes 4718600 | tf_op jit(solution)/shard_map/ppermute | solution.py:30
  27.5 15.2 %collective-permute-start.6 = (f32[4,3,1,1024]{3,2,1,0:T(1,128)S(1)}, f32[4,3,1,1024]{3,2,1,0:T(1,128)S(1)}, u32[]{:S(2)}, u32[]{:S(2)}) collective-permute-start(f32[4,3,1,1024]{3,2,1,0:T(1,128)S(1)} %pad_maximum_fusion.3), channel_id=1, source_target_pairs={{0,1},{1,2},{2,3},{3,4},{4,5},{5,6},{6,7},{8,9},{9,10},{10,11},{11... | collective-permute-start | bytes 147464 | tf_op jit(solution)/shard_map/ppermute | solution.py:29
  31.2 16.0 %collective-permute-start.7 = (f32[4,3,1,1024]{3,2,1,0:T(1,128)S(1)}, f32[4,3,1,1024]{3,2,1,0:T(1,128)S(1)}, u32[]{:S(2)}, u32[]{:S(2)}) collective-permute-start(f32[4,3,1,1024]{3,2,1,0:T(1,128)S(1)} %pad_maximum_fusion.3), channel_id=1, source_target_pairs={{1,0},{2,1},{3,2},{4,3},{5,4},{6,5},{7,6},{9,8},{10,9},{11,10},{12... | collective-permute-start | bytes 147464 | tf_op jit(solution)/shard_map/ppermute | solution.py:30
  66.2 15.2 %copy-start.6 = (bf16[2,256,256]{2,1,0:T(8,128)(2,1)S(1)}, bf16[2,256,256]{2,1,0:T(8,128)(2,1)}, u32[]{:S(2)}) copy-start(bf16[2,256,256]{2,1,0:T(8,128)(2,1)} %param.27) | copy-start | bytes 786436
  66.2 15.2 %copy-start.8 = (bf16[2,256,768]{2,1,0:T(8,128)(2,1)S(1)}, bf16[2,256,768]{2,1,0:T(8,128)(2,1)}, u32[]{:S(2)}) copy-start(bf16[2,256,768]{2,1,0:T(8,128)(2,1)} %param.26) | copy-start | bytes 2359300
  66.2 15.2 %copy-start.12 = (bf16[256,128]{1,0:T(8,128)(2,1)S(1)}, bf16[256,128]{1,0:T(8,128)(2,1)}, u32[]{:S(2)}) copy-start(bf16[256,128]{1,0:T(8,128)(2,1)} %param.30) | copy-start | bytes 196612
  66.2 15.2 %copy-start.19 = (f32[3,256]{1,0:T(4,128)S(1)}, f32[3,256]{1,0:T(4,128)}, u32[]{:S(2)}) copy-start(f32[3,256]{1,0:T(4,128)} %param.28) | copy-start | bytes 9220
  66.2 15.2 %copy-start.24 = (f32[2,8]{1,0:T(2,128)S(1)}, f32[2,8]{1,0:T(2,128)}, u32[]{:S(2)}) copy-start(f32[2,8]{1,0:T(2,128)} %param.29) | copy-start | bytes 196
  66.2 15.2 %copy-start.29 = (f32[128]{0:T(128)S(1)}, f32[128]{0:T(128)}, u32[]{:S(2)}) copy-start(f32[128]{0:T(128)} %param.31) | copy-start | bytes 1540
  81.4 222.6 %copy-start.21 = (f32[3072]{0:T(1024)S(1)}, f32[3072]{0:T(1024)}, u32[]{:S(2)}) copy-start(f32[3072]{0:T(1024)} %reshape.545) | copy-start | bytes 36868
  81.6 12.9 %copy-start.22 = (f32[6,4,128]{2,1,0:T(4,128)}, f32[6,4,128]{2,1,0:T(4,128)S(1)}, u32[]{:S(2)}) copy-start(f32[6,4,128]{2,1,0:T(4,128)S(1)} %get-tuple-element.865) | copy-start | bytes 36868 | tf_op jit(solution)/shard_map/while
  113.5 5.1 %copy-start.7 = (bf16[2,256,256]{2,1,0:T(8,128)(2,1)S(1)}, bf16[2,256,256]{2,1,0:T(8,128)(2,1)}, u32[]{:S(2)}) copy-start(bf16[2,256,256]{2,1,0:T(8,128)(2,1)} %get-tuple-element.881) | copy-start | bytes 786436 | tf_op jit(solution)/shard_map/while
  113.5 5.1 %copy-start.9 = (bf16[2,256,768]{2,1,0:T(8,128)(2,1)S(1)}, bf16[2,256,768]{2,1,0:T(8,128)(2,1)}, u32[]{:S(2)}) copy-start(bf16[2,256,768]{2,1,0:T(8,128)(2,1)} %get-tuple-element.897) | copy-start | bytes 2359300 | tf_op jit(solution)/shard_map/while
  118.7 12.9 %copy-start.22 = (f32[6,4,128]{2,1,0:T(4,128)}, f32[6,4,128]{2,1,0:T(4,128)S(1)}, u32[]{:S(2)}) copy-start(f32[6,4,128]{2,1,0:T(4,128)S(1)} %get-tuple-element.865) | copy-start | bytes 36868 | tf_op jit(solution)/shard_map/while
  150.5 5.1 %copy-start.7 = (bf16[2,256,256]{2,1,0:T(8,128)(2,1)S(1)}, bf16[2,256,256]{2,1,0:T(8,128)(2,1)}, u32[]{:S(2)}) copy-start(bf16[2,256,256]{2,1,0:T(8,128)(2,1)} %get-tuple-element.881) | copy-start | bytes 786436 | tf_op jit(solution)/shard_map/while
  150.5 5.1 %copy-start.9 = (bf16[2,256,768]{2,1,0:T(8,128)(2,1)S(1)}, bf16[2,256,768]{2,1,0:T(8,128)(2,1)}, u32[]{:S(2)}) copy-start(bf16[2,256,768]{2,1,0:T(8,128)(2,1)} %get-tuple-element.897) | copy-start | bytes 2359300 | tf_op jit(solution)/shard_map/while
  155.7 12.9 %copy-start.22 = (f32[6,4,128]{2,1,0:T(4,128)}, f32[6,4,128]{2,1,0:T(4,128)S(1)}, u32[]{:S(2)}) copy-start(f32[6,4,128]{2,1,0:T(4,128)S(1)} %get-tuple-element.865) | copy-start | bytes 36868 | tf_op jit(solution)/shard_map/while
  187.6 5.1 %copy-start.7 = (bf16[2,256,256]{2,1,0:T(8,128)(2,1)S(1)}, bf16[2,256,256]{2,1,0:T(8,128)(2,1)}, u32[]{:S(2)}) copy-start(bf16[2,256,256]{2,1,0:T(8,128)(2,1)} %get-tuple-element.881) | copy-start | bytes 786436 | tf_op jit(solution)/shard_map/while
  187.6 5.1 %copy-start.9 = (bf16[2,256,768]{2,1,0:T(8,128)(2,1)S(1)}, bf16[2,256,768]{2,1,0:T(8,128)(2,1)}, u32[]{:S(2)}) copy-start(bf16[2,256,768]{2,1,0:T(8,128)(2,1)} %get-tuple-element.897) | copy-start | bytes 2359300 | tf_op jit(solution)/shard_map/while
  187.6 5.1 %copy-start.23 = (f32[6,4,128]{2,1,0:T(4,128)S(1)}, f32[6,4,128]{2,1,0:T(4,128)}, u32[]{:S(2)}) copy-start(f32[6,4,128]{2,1,0:T(4,128)} %copy-done.22) | copy-start | bytes 36868 | tf_op jit(solution)/shard_map/while
  192.7 12.9 %copy-start.22 = (f32[6,4,128]{2,1,0:T(4,128)}, f32[6,4,128]{2,1,0:T(4,128)S(1)}, u32[]{:S(2)}) copy-start(f32[6,4,128]{2,1,0:T(4,128)S(1)} %get-tuple-element.865) | copy-start | bytes 36868 | tf_op jit(solution)/shard_map/while
  224.6 5.1 %copy-start.7 = (bf16[2,256,256]{2,1,0:T(8,128)(2,1)S(1)}, bf16[2,256,256]{2,1,0:T(8,128)(2,1)}, u32[]{:S(2)}) copy-start(bf16[2,256,256]{2,1,0:T(8,128)(2,1)} %get-tuple-element.881) | copy-start | bytes 786436 | tf_op jit(solution)/shard_map/while
  224.6 5.1 %copy-start.9 = (bf16[2,256,768]{2,1,0:T(8,128)(2,1)S(1)}, bf16[2,256,768]{2,1,0:T(8,128)(2,1)}, u32[]{:S(2)}) copy-start(bf16[2,256,768]{2,1,0:T(8,128)(2,1)} %get-tuple-element.897) | copy-start | bytes 2359300 | tf_op jit(solution)/shard_map/while
  224.6 5.1 %copy-start.23 = (f32[6,4,128]{2,1,0:T(4,128)S(1)}, f32[6,4,128]{2,1,0:T(4,128)}, u32[]{:S(2)}) copy-start(f32[6,4,128]{2,1,0:T(4,128)} %copy-done.22) | copy-start | bytes 36868 | tf_op jit(solution)/shard_map/while
  229.8 12.9 %copy-start.22 = (f32[6,4,128]{2,1,0:T(4,128)}, f32[6,4,128]{2,1,0:T(4,128)S(1)}, u32[]{:S(2)}) copy-start(f32[6,4,128]{2,1,0:T(4,128)S(1)} %get-tuple-element.865) | copy-start | bytes 36868 | tf_op jit(solution)/shard_map/while
  261.6 5.1 %copy-start.7 = (bf16[2,256,256]{2,1,0:T(8,128)(2,1)S(1)}, bf16[2,256,256]{2,1,0:T(8,128)(2,1)}, u32[]{:S(2)}) copy-start(bf16[2,256,256]{2,1,0:T(8,128)(2,1)} %get-tuple-element.881) | copy-start | bytes 786436 | tf_op jit(solution)/shard_map/while
  261.7 5.1 %copy-start.9 = (bf16[2,256,768]{2,1,0:T(8,128)(2,1)S(1)}, bf16[2,256,768]{2,1,0:T(8,128)(2,1)}, u32[]{:S(2)}) copy-start(bf16[2,256,768]{2,1,0:T(8,128)(2,1)} %get-tuple-element.897) | copy-start | bytes 2359300 | tf_op jit(solution)/shard_map/while
  266.8 12.9 %copy-start.22 = (f32[6,4,128]{2,1,0:T(4,128)}, f32[6,4,128]{2,1,0:T(4,128)S(1)}, u32[]{:S(2)}) copy-start(f32[6,4,128]{2,1,0:T(4,128)S(1)} %get-tuple-element.865) | copy-start | bytes 36868 | tf_op jit(solution)/shard_map/while
  298.7 5.1 %copy-start.7 = (bf16[2,256,256]{2,1,0:T(8,128)(2,1)S(1)}, bf16[2,256,256]{2,1,0:T(8,128)(2,1)}, u32[]{:S(2)}) copy-start(bf16[2,256,256]{2,1,0:T(8,128)(2,1)} %get-tuple-element.881) | copy-start | bytes 786436 | tf_op jit(solution)/shard_map/while
  327.3 7.3 %copy-start.16 = (f32[3,1,1,1024]{3,2,1,0:T(1,128)S(1)}, f32[3,1,1,1024]{3,2,1,0:T(1,128)}, u32[]{:S(2)}) copy-start(f32[3,1,1,1024]{3,2,1,0:T(1,128)} %param.19) | copy-start | bytes 36868
  327.3 7.3 %copy-start.18 = (f32[1,1,1024]{2,1,0:T(1,128)S(1)}, f32[1,1,1024]{2,1,0:T(1,128)}, u32[]{:S(2)}) copy-start(f32[1,1,1024]{2,1,0:T(1,128)} %param.20) | copy-start | bytes 12292
  327.3 7.3 %copy-start.14 = (f32[4,3,3,1024]{3,2,1,0:T(4,128)S(1)}, f32[4,3,3,1024]{3,2,1,0:T(4,128)}, u32[]{:S(2)}) copy-start(f32[4,3,3,1024]{3,2,1,0:T(4,128)} %copy-done.13) | copy-start | bytes 442372
  329.8 6.0 %collective-permute-start.8 = (bf16[3,1,3,1024]{3,2,1,0:T(4,128)(2,1)S(1)}, bf16[3,1,3,1024]{3,2,1,0:T(4,128)(2,1)S(1)}, u32[]{:S(2)}, u32[]{:S(2)}) collective-permute-start(bf16[3,1,3,1024]{3,2,1,0:T(4,128)(2,1)S(1)} %copy.150), channel_id=1, source_target_pairs={{0,8},{8,16},{16,24},{24,32},{32,40},{40,48},{48,56},{56,64},{64,7... | collective-permute-start | bytes 55304 | tf_op jit(solution)/shard_map/ppermute | solution.py:29
  332.9 10.2 %copy-start.26 = (s32[128]{0:T(128)S(1)}, s32[128]{0:T(128)}, u32[]{:S(2)}) copy-start(s32[128]{0:T(128)} %get-tuple-element.790) | copy-start | bytes 1540
  332.9 10.2 %copy-start.27 = (s32[128]{0:T(128)S(1)}, s32[128]{0:T(128)}, u32[]{:S(2)}) copy-start(s32[128]{0:T(128)} %get-tuple-element.789) | copy-start | bytes 1540
  333.3 4.6 collective-permute-start.9
  338.0 165.1 %collective-permute-start.10 = (bf16[3,5,1,1024]{3,0,2,1:T(4,128)(2,1)S(1)}, bf16[3,5,1,1024]{3,0,2,1:T(4,128)(2,1)S(1)}, u32[]{:S(2)}, u32[]{:S(2)}) collective-permute-start(bf16[3,5,1,1024]{3,0,2,1:T(4,128)(2,1)S(1)} %get-tuple-element.580), channel_id=1, source_target_pairs={{0,1},{1,2},{2,3},{3,4},{4,5},{5,6},{6,7},{8,9},{9,10},{10,11},{11... | collective-permute-start | bytes 92168 | tf_op jit(solution)/shard_map/ppermute | solution.py:29
  341.2 162.0 %collective-permute-start.11 = (bf16[3,5,1,1024]{3,0,2,1:T(4,128)(2,1)S(1)}, bf16[3,5,1,1024]{3,0,2,1:T(4,128)(2,1)S(1)}, u32[]{:S(2)}, u32[]{:S(2)}) collective-permute-start(bf16[3,5,1,1024]{3,0,2,1:T(4,128)(2,1)S(1)} %get-tuple-element.581), channel_id=1, source_target_pairs={{1,0},{2,1},{3,2},{4,3},{5,4},{6,5},{7,6},{9,8},{10,9},{11,10},{12... | collective-permute-start | bytes 92168 | tf_op jit(solution)/shard_map/ppermute | solution.py:30
  343.1 89.6 %copy-start.33 = (f32[6]{0:T(128)S(1)}, f32[6]{0:T(128)}, u32[]{:S(2)}) copy-start(f32[6]{0:T(128)} %get-tuple-element.921) | copy-start | bytes 76
  (79 other events, 213.9 us)
where the time goes:
time: 507 us; the launch traced here: 504 us
  other arithmetic  134 us (26%)
  matrix products  130 us (26%)
  local copies, waits for them, and re-layouts  109 us (21%)
  blocking collectives  68.9 us (14%)
  starting transfers between devices  33.1 us (7%)
  waiting for transfers between devices  18.3 us (4%)
  loops' own time  9.28 us (2%)
    psum x1, blocking collectives, body(): energy_sum = lax.psum(ml_energy + mm_energy, ('brick', 'sub'))  68.9 us
    dot_general x30, matrix products, block_energy(): jnp.einsum('phij,pjhd->pihd', attend, values, preferred_element_type=jnp....  57.3 us
    reduce_sum x8, other arithmetic, visit_block(): energy = energy + 0.5 * COULOMB_UNIT * jnp.sum(charge * screened)  27.9 us
    dot_general x24, matrix products, block_energy(): jnp.einsum('pihd,pjhd->phij', queries, key_rows, preferred_element_type=j...  25.4 us
    ppermute x6, starting transfers between devices, with_halo(): before = lax.ppermute(last, axis, up)  23.5 us
    dot_general x24, matrix products, block_energy(): jnp.dot(message, w_out[layer_index], preferred_element_type=jnp.float32)  23.1 us
    scatter-add x1, other arithmetic, fragment_model(): jnp.zeros((3, received.shape[0]), jnp.float32).at[:, slot_rows]  19.4 us
    reduce_sum x8, other arithmetic, visit_block(): pull_force = jnp.sum(strength[None] * offset, axis=3)  15.4 us
  transfers between devices with their start and end apart: 12, of which 5 were waited for; matrix products, arithmetic and copies ran while one was open for 21% of the time, Pallas kernels for 0%

commit v1 on v0

v1 whole, which is shorter than its diff:
```python
import math

import jax
import jax.numpy as jnp
from jax import lax
from jax.experimental import pallas as pl
from jax.experimental.pallas import tpu as pltpu
from jax.sharding import PartitionSpec as P

F = 256
HEADS = 8
LAYERS = 2
SLOTS = 64
TILE = 128
GROUP = 4
ROWS = GROUP * SLOTS
QUAD = 128

NORM_EPS = 1e-05
PAIR_SOFTEN = 0.01
SCREEN_RATE = 0.1
COULOMB_UNIT = 14.4
CHARGE_SOFTEN = 1.0
FAR = 1e30
GAUSS = 2.0 * SCREEN_RATE / math.sqrt(math.pi)
ERFC_P = 0.6
ERFC_C = (
    0.33858295223558404,
    0.33681896467541816,
    0.2948193558779553,
    0.06093701313639673,
    0.3109940554359323,
    -0.6781244471753995,
    0.4339317702022656,
    -0.0979638654555287,
)
MIB = 1024 * 1024


def dot(a, b):
    return lax.dot_general(a, b, (((1,), (0,)), ((), ())), preferred_element_type=jnp.float32)


def dot_nt(a, b):
    return lax.dot_general(a, b, (((1,), (1,)), ((), ())), preferred_element_type=jnp.float32)


def dot_tn(a, b):
    return lax.dot_general(a, b, (((0,), (0,)), ((), ())), preferred_element_type=jnp.float32)


def recip(x):
    return pl.reciprocal(x, approx=True)


def pair_body(pairs_ref, count_ref, own_ref, near_ref, force_ref, energy_ref):
    force_ref[...] = jnp.zeros_like(force_ref)
    energy_ref[...] = jnp.zeros_like(energy_ref)
    chunk = 32
    lane = lax.broadcasted_iota(jnp.int32, (chunk, TILE), 1)
    row = lax.broadcasted_iota(jnp.int32, (chunk, TILE), 0)
    rel = lane - row

    def one_pair(p, carry):
        own = pairs_ref[0, p]
        near = pairs_ref[1, p]
        o = own_ref[own]
        n = jnp.transpose(near_ref[near])
        xi, yi, zi, qi = (o[c : c + 1, :] for c in range(4))
        same = jnp.where(near - 4 * own_ref.shape[0] == own, 0, 4 * TILE)
        fx = jnp.zeros((8, TILE), jnp.float32)
        fy = jnp.zeros((8, TILE), jnp.float32)
        fz = jnp.zeros((8, TILE), jnp.float32)
        en = jnp.zeros((8, TILE), jnp.float32)
        for start in range(0, TILE, chunk):
            part = n[start : start + chunk]
            dx = xi - part[:, 0:1]
            dy = yi - part[:, 1:2]
            dz = zi - part[:, 2:3]
            qq = jnp.where(rel == same + start, 0.0, qi * part[:, 3:4])
            s = dx * dx + dy * dy + dz * dz + CHARGE_SOFTEN
            s = jnp.minimum(s, 1e6)
            rinv = lax.rsqrt(s)
            t = recip(1.0 + (ERFC_P * SCREEN_RATE) * (s * rinv))
            g = ERFC_C[-1]
            for coef in ERFC_C[-2::-1]:
                g = g * t + coef
            gauss = qq * jnp.exp((-SCREEN_RATE * SCREEN_RATE) * s)
            screened = gauss * (g * t) * rinv
            en += jnp.sum(screened.reshape(chunk // 8, 8, TILE), axis=0)
            w = (screened + GAUSS * gauss) * (rinv * rinv)
            fx += jnp.sum((w * dx).reshape(chunk // 8, 8, TILE), axis=0)
            fy += jnp.sum((w * dy).reshape(chunk // 8, 8, TILE), axis=0)
            fz += jnp.sum((w * dz).reshape(chunk // 8, 8, TILE), axis=0)
        energy_ref[...] += en
        force_ref[own, 0] += fx
        force_ref[own, 1] += fy
        force_ref[own, 2] += fz
        return carry

    lax.fori_loop(0, count_ref[0], one_pair, 0)


def solvent_pairs(own8, near8, pairs, count):
    tiles = own8.shape[0]
    smem = pl.BlockSpec(memory_space=pltpu.SMEM)
    vmem = pl.BlockSpec(memory_space=pltpu.VMEM)
    force, energy = pl.pallas_call(
        pair_body,
        out_shape=(
            jax.ShapeDtypeStruct((tiles, 3, 8, TILE), jnp.float32),
            jax.ShapeDtypeStruct((8, TILE), jnp.float32),
        ),
        in_specs=[smem, smem, vmem, vmem],
        out_specs=(vmem, vmem),
        name="pair_tiles",
    )(pairs, count, own8, near8)
    force = COULOMB_UNIT * jnp.sum(force, axis=2)
    return 0.5 * COULOMB_UNIT * jnp.sum(energy), force.transpose(1, 0, 2).reshape(3, -1)


def norm_parts(hidden):
    centre = jnp.mean(hidden, axis=-1, keepdims=True)
    shifted = hidden - centre
    spread = jnp.mean(shifted * shifted, axis=-1, keepdims=True)
    scale = lax.rsqrt(spread + NORM_EPS)
    return shifted * scale, scale


def norm_back(grad, gain, unit, scale):
    g = grad * gain
    mean_g = jnp.mean(g, axis=-1, keepdims=True)
    mean_gu = jnp.mean(g * unit, axis=-1, keepdims=True)
    return scale * (g - mean_g - unit * mean_gu)


def sigmoid(x):
    return 0.5 * jnp.tanh(0.5 * x) + 0.5


def fragment_body(
    slot_ref,
    count_ref,
    near_ref,
    feat_ref,
    cap_ref,
    wqkv_ref,
    wout_ref,
    gains_ref,
    rates_ref,
    wread_ref,
    wen_ref,
    force_ref,
    energy_ref,
    table,
    atoms,
    slot_feat,
    slot_atom,
    slot_force,
):
    tiles = near_ref.shape[0]
    blocks = slot_ref.shape[0] // GROUP

    def widen(i, carry):
        at = pl.multiple_of(i * TILE, TILE)
        table[pl.ds(at, TILE), :] = feat_ref[pl.ds(at, TILE), :].astype(jnp.float32)
        n = jnp.transpose(near_ref[i])
        atoms[pl.ds(at, TILE), :] = jnp.concatenate(
            [n, jnp.zeros((TILE, TILE - 8), jnp.float32)], axis=1
        )
        return carry

    lax.fori_loop(0, tiles, widen, 0)
    slot_feat[...] = jnp.zeros_like(slot_feat)
    slot_atom[...] = jnp.zeros_like(slot_atom)
    slot_force[...] = jnp.zeros_like(slot_force)
    energy_ref[...] = jnp.zeros_like(energy_ref)

    lane = lax.broadcasted_iota(jnp.int32, (1, QUAD), 1)
    head_mask = [(lane // 32 == h).astype(jnp.bfloat16) for h in range(4)]
    head_pick = [lane // 32 == h for h in range(4)]
    slot_row = lax.broadcasted_iota(jnp.int32, (SLOTS, 1), 0)
    slot_lane = lane % SLOTS
    frag_lane = lax.broadcasted_iota(jnp.int32, (SLOTS, cap_ref.shape[1]), 1)

    def spread_heads(x):
        return jnp.concatenate([x * head_mask[h] for h in range(4)], axis=0)

    def fold_heads(x):
        out = jnp.where(head_pick[0], x[0:SLOTS], 0.0)
        for h in range(1, 4):
            out = jnp.where(head_pick[h], x[h * SLOTS : (h + 1) * SLOTS], out)
        return out

    def rate_of(layer, quad):
        return rates_ref[layer : layer + 1, quad * 256 : (quad + 1) * 256]

    def one_block(b, carry):
        for f in range(GROUP):
            frag = b * GROUP + f

            def pull(j8, c, frag=frag, f=f):
                for k in range(8):
                    j = j8 * 8 + k
                    r = slot_ref[frag, j]
                    slot_feat[pl.ds(f * SLOTS + j, 1), :] = table[pl.ds(r, 1), :]
                    slot_atom[pl.ds(f * SLOTS + j, 1), :] = atoms[pl.ds(r, 1), :]
                return c

            lax.fori_loop(0, (count_ref[frag] + 7) // 8, pull, 0)

        atom_rows = jnp.transpose(slot_atom[...])
        dists, offsets, weights = [], [], []
        for f in range(GROUP):
            count = count_ref[b * GROUP + f]
            col = slot_atom[f * SLOTS : (f + 1) * SLOTS, :]
            row = atom_rows[0:8, f * SLOTS : (f + 1) * SLOTS]
            row = jnp.concatenate([row, row], axis=1)
            off = [col[:, c : c + 1] - row[c : c + 1, :] for c in range(3)]
            square = off[0] * off[0] + off[1] * off[1] + off[2] * off[2]
            live = jnp.logical_and(slot_row < count, slot_lane < count)
            dists.append(jnp.where(live, jnp.sqrt(square + PAIR_SOFTEN), FAR))
            offsets.append(off)
            cap = jnp.sum(
                jnp.where(frag_lane == b * GROUP + f, cap_ref[...], 0.0), axis=1, keepdims=True
            )
            weights.append(jnp.where(slot_row < count, cap, 0.0))
        weight = jnp.concatenate(weights, axis=0)

        def attention(layer, project):
            messages, kept = [], []
            for f in range(GROUP):
                dist = jnp.concatenate([dists[f], dists[f]], axis=1)
                parts = []
                for quad in range(2):
                    rows = slice(f * SLOTS, (f + 1) * SLOTS)
                    q, k, v = (
                        project[rows, part * F + quad * QUAD : part * F + (quad + 1) * QUAD]
                        for part in range(3)
                    )
                    kb = spread_heads(k)
                    vb = spread_heads(v)
                    s = dot_nt(q, kb) * (1.0 / math.sqrt(32.0))
                    sig = sigmoid(s)
                    rate = rate_of(layer, quad)
                    damp = recip(1.0 + rate * dist)
                    silu = s * sig
                    att = silu * damp
                    att16 = att.astype(jnp.bfloat16)
                    parts.append(dot(att16, vb).astype(jnp.bfloat16))
                    by_dist = att * (rate * damp)
                    by_score = None
                    if layer == 1:
                        by_score = (damp * (1.0 / math.sqrt(32.0))) * (sig + silu * (1.0 - sig))
                    kept.append((q, kb, vb, att16, by_dist, by_score))
                messages.append(jnp.concatenate(parts, axis=1))
            return jnp.concatenate(messages, axis=0), kept

        gain = [gains_ref[i : i + 1, :] for i in range(LAYERS + 1)]
        h0 = slot_feat[...]
        unit0, _ = norm_parts(h0)
        project0 = dot((unit0 * gain[0]).astype(jnp.bfloat16), wqkv_ref[0]).astype(jnp.bfloat16)
        message0, kept0 = attention(0, project0)
        h1 = h0 + dot(message0, wout_ref[0])
        unit1, scale1 = norm_parts(h1)
        project1 = dot((unit1 * gain[1]).astype(jnp.bfloat16), wqkv_ref[1]).astype(jnp.bfloat16)
        message1, kept1 = attention(1, project1)
        h2 = h1 + dot(message1, wout_ref[1])
        unit2, scale2 = norm_parts(h2)
        read = dot((unit2 * gain[2]).astype(jnp.bfloat16), wread_ref[...])
        sig = sigmoid(read)
        silu = read * sig
        wen = wen_ref[...]
        contrib = weight * (silu * wen)
        energy_ref[...] += jnp.sum(contrib.reshape(ROWS // 8, 8, QUAD), axis=0)

        dread = ((weight * wen) * (sig + silu * (1.0 - sig))).astype(jnp.bfloat16)
        dh2 = norm_back(dot_nt(dread, wread_ref[...]), gain[2], unit2, scale2)
        dmsg1 = dot_nt(dh2.astype(jnp.bfloat16), wout_ref[1]).astype(jnp.bfloat16)
        pulls = []
        dqkv = []
        for f in range(GROUP):
            rows = slice(f * SLOTS, (f + 1) * SLOTS)
            total = None
            cols = [[], [], []]
            for quad in range(2):
                q, kb, vb, att16, by_dist, by_score = kept1[2 * f + quad]
                dm = dmsg1[rows, quad * QUAD : (quad + 1) * QUAD]
                datt = dot_nt(dm, vb)
                ds = (datt * by_score).astype(jnp.bfloat16)
                cols[0].append(dot(ds, kb))
                cols[1].append(fold_heads(dot_tn(ds, q)))
                cols[2].append(fold_heads(dot_tn(att16, dm)))
                pull = datt * by_dist
                pull = pull[:, :QUAD] + pull[:, QUAD:]
                total = pull if total is None else total + pull
            pulls.append(total)
            dqkv.append(
                jnp.concatenate([x.astype(jnp.bfloat16) for part in cols for x in part], axis=1)
            )
        dproject = jnp.concatenate(dqkv, axis=0)
        dh1 = dh2 + norm_back(dot_nt(dproject, wqkv_ref[1]), gain[1], unit1, scale1)
        dmsg0 = dot_nt(dh1.astype(jnp.bfloat16), wout_ref[0]).astype(jnp.bfloat16)
        force_rows = []
        for f in range(GROUP):
            rows = slice(f * SLOTS, (f + 1) * SLOTS)
            total = pulls[f]
            for quad in range(2):
                q, kb, vb, att16, by_dist, by_score = kept0[2 * f + quad]
                datt = dot_nt(dmsg0[rows, quad * QUAD : (quad + 1) * QUAD], vb)
                pull = datt * by_dist
                total = total + (pull[:, :QUAD] + pull[:, QUAD:])
            pull = total / dists[f]
            pull = pull[:, :SLOTS] + pull[:, SLOTS:]
            pull = pull + jnp.transpose(pull)
            for c in range(3):
                force_rows.append(
                    -jnp.sum(pull * offsets[f][c][:, :SLOTS], axis=0, keepdims=True)
                )
        packed = jnp.concatenate(
            [
                jnp.concatenate([force_rows[3 * f + c] for f in range(GROUP)], axis=1)
                for c in range(3)
            ]
            + [jnp.zeros((5, ROWS), jnp.float32)],
            axis=0,
        )
        slot_force[:, 8:16] = jnp.transpose(packed)

        for f in range(GROUP):
            frag = b * GROUP + f
            count = count_ref[frag]

            def push(j8, c, frag=frag, f=f, count=count):
                rs = [slot_ref[frag, j8 * 8 + k] for k in range(8)]
                old = [atoms[pl.ds(r, 1), :] for r in rs]
                add = [slot_force[pl.ds(f * SLOTS + j8 * 8 + k, 1), :] for k in range(8)]
                for k in range(8):
                    atoms[pl.ds(rs[k], 1), :] = old[k] + add[k]
                return c

            lax.fori_loop(0, (count + 7) // 8, push, 0)
        return carry

    lax.fori_loop(0, blocks, one_block, 0)

    pick = (
        lax.broadcasted_iota(jnp.int32, (16, TILE), 0) + 8
        == lax.broadcasted_iota(jnp.int32, (16, TILE), 1)
    ).astype(jnp.bfloat16)
    for i in range(tiles // 8):
        force_ref[i] = dot_nt(pick, atoms[i * 1024 : (i + 1) * 1024, :].astype(jnp.bfloat16))[:8]


def fragment_model(near8, near_features, slot_index, atom_count, cap_weight, weights):
    w_qkv, w_out, gains, rates, w_read, w_energy = weights
    tiles = near8.shape[0]
    smem = pl.BlockSpec(memory_space=pltpu.SMEM)
    vmem = pl.BlockSpec(memory_space=pltpu.VMEM)
    lane_rates = jnp.repeat(rates, SLOTS, axis=1)
    force, energy = pl.pallas_call(
        fragment_body,
        out_shape=(
            jax.ShapeDtypeStruct((tiles // 8, 8, 1024), jnp.float32),
            jax.ShapeDtypeStruct((8, TILE), jnp.float32),
        ),
        in_specs=[smem, smem] + [vmem] * 9,
        out_specs=(vmem, vmem),
        scratch_shapes=[
            pltpu.VMEM((tiles * TILE, F), jnp.float32),
            pltpu.VMEM((tiles * TILE, TILE), jnp.float32),
            pltpu.VMEM((ROWS, F), jnp.float32),
            pltpu.VMEM((ROWS, TILE), jnp.float32),
            pltpu.VMEM((ROWS, TILE), jnp.float32),
        ],
        compiler_params=pltpu.CompilerParams(vmem_limit_bytes=56 * MIB),
        name="fragments",
    )(
        slot_index,
        atom_count,
        near8,
        near_features,
        cap_weight.T,
        w_qkv,
        w_out,
        gains,
        lane_rates,
        w_read,
        w_energy.reshape(1, -1),
    )
    return jnp.sum(energy), force


def with_halo(x, sides, width):
    for axis, dim in sides:
        devices, length = (lax.axis_size(axis), x.shape[dim])
        up = [(i, (i + 1) % devices) for i in range(devices - 1)]
        down = [(j, i) for i, j in up]
        last = lax.slice_in_dim(x, length - width, length, axis=dim)
        initial = lax.slice_in_dim(x, 0, width, axis=dim)
        before = lax.ppermute(last, axis, up)
        after = lax.ppermute(initial, axis, down)
        x = jnp.concatenate([before, x, after], axis=dim)
    return x


def body(
    atom_features,
    positions,
    charges,
    slot_index,
    atom_count,
    cap_weight,
    tile_pairs,
    tile_count,
    w_qkv,
    w_out,
    gains,
    rates,
    w_read,
    w_energy,
):
    own_size = atom_features.shape[2]
    own_tiles = own_size // TILE
    own8 = jnp.concatenate([positions.reshape(3, -1), charges.reshape(1, -1)], axis=0)
    own8 = jnp.pad(own8, ((0, 4), (0, 0))).reshape(8, own_tiles, TILE).transpose(1, 0, 2)
    near8 = with_halo(own8[None, None], (("brick", 0), ("sub", 1)), 1).reshape(-1, 8, TILE)
    near_features = with_halo(atom_features, (("brick", 0), ("sub", 1)), 1)
    mm_energy, mm_force = solvent_pairs(
        own8, near8, tile_pairs.reshape(2, -1), tile_count.reshape(1)
    )
    ml_energy, row_force = fragment_model(
        near8,
        near_features.reshape(-1, F),
        slot_index,
        atom_count,
        cap_weight,
        (w_qkv, w_out, gains, rates, w_read, w_energy),
    )
    row_force = row_force[:, :3].astype(jnp.bfloat16).transpose(1, 0, 2).reshape(3, 3, 3, own_size)
    returned = with_halo(row_force, (("brick", 1), ("sub", 2)), 1).astype(jnp.float32)
    ml_force = jnp.sum(returned[:, ::2, ::2], axis=(1, 2))
    energy_sum = lax.psum(ml_energy + mm_energy, ("brick", "sub"))
    return ((ml_force + mm_force).reshape(3, 1, 1, own_size), energy_sum)


def solution(mesh):
    in_specs = (
        P("brick", "sub", None, None),
        P(None, "brick", "sub", None),
        P("brick", "sub", None),
        P(("brick", "sub"), None),
        P(("brick", "sub")),
        P(("brick", "sub"), None),
        P(None, "brick", "sub", None),
        P("brick", "sub"),
        P(),
        P(),
        P(),
        P(),
        P(),
        P(),
    )
    out_specs = (P(None, "brick", "sub", None), P())
    return jax.shard_map(body, mesh=mesh, in_specs=in_specs, out_specs=out_specs, check_vma=False)
```

time: 507 us -> 296 us (0.58)
  matrix products: 130 us -> 0 us
  other arithmetic: 134 us -> 8.65 us
  Pallas kernels: 0 us -> 123 us
  local copies, waits for them, and re-layouts: 109 us -> 4.95 us
  blocking collectives: 68.9 us -> 99.4 us
  loops' own time: 9.28 us -> 0 us
    dot_general x114 -> x0, matrix products: 130 us -> none  [the longest x30 57.3 us: block_energy(): jnp.einsum('phij,pjhd->pihd', attend, values, preferred_element_type=jnp....]
    pallas_call x0 -> x2, Pallas kernels: none -> 123 us  [the longest x1 115 us: fragment_model(): pl.pallas_call(fragment_body, out_shape=(jax.ShapeDtypeStruct((tiles // 8...]
    reduce_sum x79 -> x3, other arithmetic: 66.3 us -> 3.5 us  [the longest x1 1.29 us: solvent_pairs(): jnp.sum(energy)]
    gather x18 -> x0, local copies, waits for them, and re-layouts: 35 us -> none  [the longest x1 15.2 us: fragment_model(): received[slot_rows]]
    psum x1, blocking collectives: 68.9 us -> 99.4 us  [body(): energy_sum = lax.psum(ml_energy + mm_energy, ('brick', 'sub'))]
    scatter-add x9 -> x0, other arithmetic: 28.3 us -> none  [the longest x1 19.4 us: fragment_model(): jnp.zeros((3, received.shape[0]), jnp.float32).at[:, slot_rows]]
    convert_element_type x38 -> x0, local copies, waits for them, and re-layouts: 19.4 us -> none  [the longest x12 11.7 us: block_energy(): jnp.dot(message, w_out[layer_index], preferred_element_type=jnp.float32)]
    div x44 -> x0, other arithmetic: 14.3 us -> none  [the longest x6 8.25 us: block_energy(): jnp.einsum('pihd,pjhd->phij', queries, key_rows, preferred_element_type=j...]
  transfers between devices with their start and end apart: 12 -> 12, of which waited for: 5 -> 5; matrix products, arithmetic and copies ran while one was open for 21% -> 3% of each run, Pallas kernels for 0% -> 3%
where the time goes in v1:
time: 296 us; the launch traced here: 295 us
  Pallas kernels  123 us (42%)
  blocking collectives  99.4 us (34%)
  starting transfers between devices  33.3 us (11%)
  waiting for transfers between devices  22.4 us (8%)
  other arithmetic  8.65 us (3%)
  local copies, waits for them, and re-layouts  4.95 us (2%)
    pallas_call x1, Pallas kernels, fragment_model(): pl.pallas_call(fragment_body, out_shape=(jax.ShapeDtypeStruct((tiles // 8...  115 us
    psum x1, blocking collectives, body(): energy_sum = lax.psum(ml_energy + mm_energy, ('brick', 'sub'))  99.4 us
    ppermute x6, starting transfers between devices, with_halo(): before = lax.ppermute(last, axis, up)  23.7 us
    ppermute x6, waiting for transfers between devices, with_halo(): after = lax.ppermute(initial, axis, down)  12.9 us
    ppermute x6, starting transfers between devices, with_halo(): after = lax.ppermute(initial, axis, down)  9.64 us
    ppermute x6, waiting for transfers between devices, with_halo(): before = lax.ppermute(last, axis, up)  9.57 us
    pallas_call x1, Pallas kernels, solvent_pairs(): pl.pallas_call(pair_body, out_shape=(jax.ShapeDtypeStruct((tiles, 3, 8, T...  8.12 us
  transfers between devices with their start and end apart: 12, of which 5 were waited for; matrix products, arithmetic and copies ran while one was open for 3% of the time, Pallas kernels for 3%

profile of v1, /device:TPU:1, one launch (start us, length us, event | category | flops | bytes accessed | tf_op | source)
XLA Modules:
  0.0 295.0 jit_solution(5943022823543864017)
XLA Ops:
  0.6 0.0 copy-start
  0.6 0.0 copy-start.1
  0.7 0.0 copy-start.2
  0.7 4.1 %collective-permute-start.4 = (bf16[1,1,1024,256]{3,2,1,0:T(8,128)(2,1)}, bf16[1,1,1024,256]{3,2,1,0:T(8,128)(2,1)S(1)}, u32[]{:S(2)}, u32[]{:S(2)}) collective-permute-start(bf16[1,1,1024,256]{3,2,1,0:T(8,128)(2,1)} %param.14), channel_id=1, source_target_pairs={{0,8},{8,16},{16,24},{24,32},{32,40},{40,48},{48,56},{56,64},{64,7... | collective-permute-start | bytes 1572872 | tf_op jit(solution)/shard_map/ppermute | solution.py:401
  4.8 1.3 collective-permute-start.5
  6.1 9.6 %collective-permute-done.4 = bf16[1,1,1024,256]{3,2,1,0:T(8,128)(2,1)S(1)} collective-permute-done((bf16[1,1,1024,256]{3,2,1,0:T(8,128)(2,1)}, bf16[1,1,1024,256]{3,2,1,0:T(8,128)(2,1)S(1)}, u32[]{:S(2)}, u32[]{:S(2)}) %collective-permute-start.4) | collective-permute-done | bytes 524320 | tf_op jit(solution)/shard_map/ppermute | solution.py:401
  15.7 1.1 constant_dynamic-update-slice_fusion.1
  16.8 2.6 collective-permute-done.5
  19.4 5.3 %collective-permute-start.6 = (bf16[3,1,1024,256]{3,2,1,0:T(8,128)(2,1)S(1)}, bf16[3,1,1024,256]{3,2,1,0:T(8,128)(2,1)S(1)}, u32[]{:S(2)}, u32[]{:S(2)}) collective-permute-start(bf16[3,1,1024,256]{3,2,1,0:T(8,128)(2,1)S(1)} %constant_dynamic-update-slice_fusion), channel_id=1, source_target_pairs={{0,1},{1,2},{2,3},{3,4},{4,5},{5,6},{6,7},{8,9},{9,10},{10,11},{11... | collective-permute-start | bytes 4718600 | tf_op jit(solution)/shard_map/ppermute | solution.py:401
  24.7 1.9 collective-permute-start.7
  26.6 0.0 copy-done
  26.7 0.0 copy-done.1
  26.7 0.6 fusion
  27.3 3.1 %collective-permute-start = (f32[1,1,8,8,128]{4,3,2,1,0:T(8,128)S(1)}, f32[1,1,8,8,128]{4,3,2,1,0:T(8,128)S(1)}, u32[]{:S(2)}, u32[]{:S(2)}) collective-permute-start(f32[1,1,8,8,128]{4,3,2,1,0:T(8,128)S(1)} %get-tuple-element.17), channel_id=1, source_target_pairs={{0,8},{8,16},{16,24},{24,32},{32,40},{40,48},{48,56},{56,64},{64,7... | collective-permute-start | bytes 98312 | tf_op jit(solution)/shard_map/ppermute | solution.py:401
  30.4 1.3 collective-permute-start.1
  31.7 0.0 collective-permute-done
  31.7 3.3 %collective-permute-done.1 = f32[1,1,8,8,128]{4,3,2,1,0:T(8,128)S(1)} collective-permute-done((f32[1,1,8,8,128]{4,3,2,1,0:T(8,128)S(1)}, f32[1,1,8,8,128]{4,3,2,1,0:T(8,128)S(1)}, u32[]{:S(2)}, u32[]{:S(2)}) %collective-permute-start.1) | collective-permute-done | bytes 32800 | tf_op jit(solution)/shard_map/ppermute | solution.py:402
  35.0 5.1 %collective-permute-start.2 = (f32[3,1,8,8,128]{4,3,2,1,0:T(8,128)S(1)}, f32[3,1,8,8,128]{4,3,2,1,0:T(8,128)S(1)}, u32[]{:S(2)}, u32[]{:S(2)}) collective-permute-start(f32[3,1,8,8,128]{4,3,2,1,0:T(8,128)S(1)} %pad_maximum_fusion.3), channel_id=1, source_target_pairs={{0,1},{1,2},{2,3},{3,4},{4,5},{5,6},{6,7},{8,9},{9,10},{10,11},{11... | collective-permute-start | bytes 294920 | tf_op jit(solution)/shard_map/ppermute | solution.py:401
  40.1 1.9 collective-permute-start.3
  42.0 1.4 copy.18
  43.5 0.0 copy-done.2
  43.5 0.1 broadcast_in_dim.7
  43.5 0.7 reshape.57.rates_ref
  44.2 0.0 collective-permute-done.2
  44.2 3.3 %collective-permute-done.3 = f32[3,1,8,8,128]{4,3,2,1,0:T(8,128)S(1)} collective-permute-done((f32[3,1,8,8,128]{4,3,2,1,0:T(8,128)S(1)}, f32[3,1,8,8,128]{4,3,2,1,0:T(8,128)S(1)}, u32[]{:S(2)}, u32[]{:S(2)}) %collective-permute-start.3) | collective-permute-done | bytes 98336 | tf_op jit(solution)/shard_map/ppermute | solution.py:402
  47.5 0.7 pad_maximum_fusion.1
  48.2 0.0 collective-permute-done.6
  48.2 0.0 collective-permute-done.7
  48.2 3.5 %pad_maximum_fusion = bf16[3,3,1024,256]{3,2,1,0:T(8,128)(2,1)} fusion(bf16[3,1,1024,256]{3,2,1,0:T(8,128)(2,1)} %collective-permute-done.7, bf16[3,1,1024,256]{3,2,1,0:T(8,128)(2,1)S(1)} %constant_dynamic-update-slice_fusion, bf16[3,1,1024,256]{3,2,1,0:T(8,128)(2,1)S(1)} %collective-permute-done.6), kind=kLoop, calls=%fused_computation | loop fusion | flops 4718592 | bytes 9437184 | tf_op jit(solution)/shard_map/concatenate | solution.py:403
  51.7 115.4 %fragments.1 = (f32[9,8,1024]{2,1,0:T(8,128)}, f32[8,128]{1,0:T(8,128)}) custom-call(s32[48,64]{1,0:T(8,128)} %slot_ref.1, s32[48]{0:T(128)} %count_ref.1, f32[72,8,128]{2,1,0:T(8,128)} %bitcast.28, bf16[9216,256]{1,0:T(8,128)(2,1)} %bitcast.27, f32[64,48]{1,0:T(8,128)} %bitcast.33, bf16[2,256,768]{2,1,0:T(8,128)(2,1)} %wqkv_ref.1, ...), custom_call_target="tpu_custom_call" | custom-call | tf_op jit(solution)/shard_map/fragments/pallas_call | solution.py:361
  167.1 1.0 slice.35
  168.1 2.6 collective-permute-start.8
  170.8 1.3 collective-permute-start.9
  172.1 0.0 collective-permute-done.8
  172.1 3.6 %collective-permute-done.9 = bf16[3,1,3,1024]{3,0,2,1:T(4,128)(2,1)S(1)} collective-permute-done((bf16[3,1,3,1024]{3,0,2,1:T(4,128)(2,1)S(1)}, bf16[3,1,3,1024]{3,0,2,1:T(4,128)(2,1)S(1)}, u32[]{:S(2)}, u32[]{:S(2)}) %collective-permute-start.9) | collective-permute-done | bytes 18464 | tf_op jit(solution)/shard_map/ppermute | solution.py:402
  175.7 0.1 pad_maximum_fusion.6
  175.8 3.5 %collective-permute-start.10 = (bf16[3,5,1,1024]{3,0,2,1:T(4,128)(2,1)S(1)}, bf16[3,5,1,1024]{3,0,2,1:T(4,128)(2,1)S(1)}, u32[]{:S(2)}, u32[]{:S(2)}) collective-permute-start(bf16[3,5,1,1024]{3,0,2,1:T(4,128)(2,1)S(1)} %get-tuple-element.12), channel_id=1, source_target_pairs={{0,1},{1,2},{2,3},{3,4},{4,5},{5,6},{6,7},{8,9},{9,10},{10,11},{11... | collective-permute-start | bytes 92168 | tf_op jit(solution)/shard_map/ppermute | solution.py:401
  179.3 1.9 collective-permute-start.11
  181.9 8.1 %pair_tiles.1 = (f32[8,3,8,128]{3,2,1,0:T(8,128)}, f32[8,128]{1,0:T(8,128)}) custom-call(s32[2,128]{1,0:T(2,128)} %bitcast.36, s32[1]{0:T(128)} %bitcast.26.count_ref, f32[8,8,128]{2,1,0:T(8,128)} %get-tuple-element.16.own_ref, f32[72,8,128]{2,1,0:T(8,128)} %bitcast.29), custom_call_target="tpu_custom_call" | custom-call | tf_op jit(solution)/shard_map/pair_tiles/pallas_call | solution.py:108
  190.0 1.3 reduce_sum.42
  191.9 1.3 reduce_sum.41
  193.9 0.9 reduce_sum.40
  194.8 99.4 %psum.7 = f32[]{:T(128)} all-reduce(f32[]{:T(128)S(6)} %add.18), channel_id=1, replica_groups=mesh['brick'=16,'sub'=8] {'brick','sub'}, use_global_device_ids=true, to_apply=%region_4.5 | all-reduce | flops 1 | bytes 8 | tf_op jit(solution)/shard_map/psum | solution.py:443
  294.2 0.0 collective-permute-done.10
  294.2 0.0 collective-permute-done.11
  294.2 0.2 pad_maximum_fusion.2
  294.4 0.6 copy.19
  (7 shorter events, 0.2 us)
Async XLA Ops:
  0.6 26.0 %copy-start = (f32[3,1,1,1024]{3,2,1,0:T(1,128)S(1)}, f32[3,1,1,1024]{3,2,1,0:T(1,128)}, u32[]{:S(2)}) copy-start(f32[3,1,1,1024]{3,2,1,0:T(1,128)} %param.15) | copy-start | bytes 36868
  0.6 26.0 %copy-start.1 = (f32[1,1,1024]{2,1,0:T(1,128)S(1)}, f32[1,1,1024]{2,1,0:T(1,128)}, u32[]{:S(2)}) copy-start(f32[1,1,1024]{2,1,0:T(1,128)} %param.16) | copy-start | bytes 12292
  0.7 42.8 %copy-start.2 = (f32[2,8]{1,0:T(2,128)S(1)}, f32[2,8]{1,0:T(2,128)}, u32[]{:S(2)}) copy-start(f32[2,8]{1,0:T(2,128)} %param.25) | copy-start | bytes 196
  0.7 15.0 %collective-permute-start.4 = (bf16[1,1,1024,256]{3,2,1,0:T(8,128)(2,1)}, bf16[1,1,1024,256]{3,2,1,0:T(8,128)(2,1)S(1)}, u32[]{:S(2)}, u32[]{:S(2)}) collective-permute-start(bf16[1,1,1024,256]{3,2,1,0:T(8,128)(2,1)} %param.14), channel_id=1, source_target_pairs={{0,8},{8,16},{16,24},{24,32},{32,40},{40,48},{48,56},{56,64},{64,7... | collective-permute-start | bytes 1572872 | tf_op jit(solution)/shard_map/ppermute | solution.py:401
  4.8 14.6 %collective-permute-start.5 = (bf16[1,1,1024,256]{3,2,1,0:T(8,128)(2,1)}, bf16[1,1,1024,256]{3,2,1,0:T(8,128)(2,1)S(1)}, u32[]{:S(2)}, u32[]{:S(2)}) collective-permute-start(bf16[1,1,1024,256]{3,2,1,0:T(8,128)(2,1)} %param.14), channel_id=1, source_target_pairs={{8,0},{16,8},{24,16},{32,24},{40,32},{48,40},{56,48},{64,56},{72,6... | collective-permute-start | bytes 1572872 | tf_op jit(solution)/shard_map/ppermute | solution.py:402
  19.4 28.8 %collective-permute-start.6 = (bf16[3,1,1024,256]{3,2,1,0:T(8,128)(2,1)S(1)}, bf16[3,1,1024,256]{3,2,1,0:T(8,128)(2,1)S(1)}, u32[]{:S(2)}, u32[]{:S(2)}) collective-permute-start(bf16[3,1,1024,256]{3,2,1,0:T(8,128)(2,1)S(1)} %constant_dynamic-update-slice_fusion), channel_id=1, source_target_pairs={{0,1},{1,2},{2,3},{3,4},{4,5},{5,6},{6,7},{8,9},{9,10},{10,11},{11... | collective-permute-start | bytes 4718600 | tf_op jit(solution)/shard_map/ppermute | solution.py:401
  24.7 23.5 %collective-permute-start.7 = (bf16[3,1,1024,256]{3,2,1,0:T(8,128)(2,1)S(1)}, bf16[3,1,1024,256]{3,2,1,0:T(8,128)(2,1)}, u32[]{:S(2)}, u32[]{:S(2)}) collective-permute-start(bf16[3,1,1024,256]{3,2,1,0:T(8,128)(2,1)S(1)} %constant_dynamic-update-slice_fusion), channel_id=1, source_target_pairs={{1,0},{2,1},{3,2},{4,3},{5,4},{6,5},{7,6},{9,8},{10,9},{11,10},{12... | collective-permute-start | bytes 4718600 | tf_op jit(solution)/shard_map/ppermute | solution.py:402
  27.3 4.4 %collective-permute-start = (f32[1,1,8,8,128]{4,3,2,1,0:T(8,128)S(1)}, f32[1,1,8,8,128]{4,3,2,1,0:T(8,128)S(1)}, u32[]{:S(2)}, u32[]{:S(2)}) collective-permute-start(f32[1,1,8,8,128]{4,3,2,1,0:T(8,128)S(1)} %get-tuple-element.17), channel_id=1, source_target_pairs={{0,8},{8,16},{16,24},{24,32},{32,40},{40,48},{48,56},{56,64},{64,7... | collective-permute-start | bytes 98312 | tf_op jit(solution)/shard_map/ppermute | solution.py:401
  30.4 4.7 %collective-permute-start.1 = (f32[1,1,8,8,128]{4,3,2,1,0:T(8,128)S(1)}, f32[1,1,8,8,128]{4,3,2,1,0:T(8,128)S(1)}, u32[]{:S(2)}, u32[]{:S(2)}) collective-permute-start(f32[1,1,8,8,128]{4,3,2,1,0:T(8,128)S(1)} %get-tuple-element.17), channel_id=1, source_target_pairs={{8,0},{16,8},{24,16},{32,24},{40,32},{48,40},{56,48},{64,56},{72,6... | collective-permute-start | bytes 98312 | tf_op jit(solution)/shard_map/ppermute | solution.py:402
  35.0 9.2 %collective-permute-start.2 = (f32[3,1,8,8,128]{4,3,2,1,0:T(8,128)S(1)}, f32[3,1,8,8,128]{4,3,2,1,0:T(8,128)S(1)}, u32[]{:S(2)}, u32[]{:S(2)}) collective-permute-start(f32[3,1,8,8,128]{4,3,2,1,0:T(8,128)S(1)} %pad_maximum_fusion.3), channel_id=1, source_target_pairs={{0,1},{1,2},{2,3},{3,4},{4,5},{5,6},{6,7},{8,9},{9,10},{10,11},{11... | collective-permute-start | bytes 294920 | tf_op jit(solution)/shard_map/ppermute | solution.py:401
  40.1 7.4 %collective-permute-start.3 = (f32[3,1,8,8,128]{4,3,2,1,0:T(8,128)S(1)}, f32[3,1,8,8,128]{4,3,2,1,0:T(8,128)S(1)}, u32[]{:S(2)}, u32[]{:S(2)}) collective-permute-start(f32[3,1,8,8,128]{4,3,2,1,0:T(8,128)S(1)} %pad_maximum_fusion.3), channel_id=1, source_target_pairs={{1,0},{2,1},{3,2},{4,3},{5,4},{6,5},{7,6},{9,8},{10,9},{11,10},{12... | collective-permute-start | bytes 294920 | tf_op jit(solution)/shard_map/ppermute | solution.py:402
  168.1 3.9 %collective-permute-start.8 = (bf16[3,1,3,1024]{3,0,2,1:T(4,128)(2,1)S(1)}, bf16[3,1,3,1024]{3,0,2,1:T(4,128)(2,1)S(1)}, u32[]{:S(2)}, u32[]{:S(2)}) collective-permute-start(bf16[3,1,3,1024]{3,0,2,1:T(4,128)(2,1)S(1)} %get-tuple-element.14), channel_id=1, source_target_pairs={{0,8},{8,16},{16,24},{24,32},{32,40},{40,48},{48,56},{56,64},{64,7... | collective-permute-start | bytes 55304 | tf_op jit(solution)/shard_map/ppermute | solution.py:401
  170.8 4.9 %collective-permute-start.9 = (bf16[3,1,3,1024]{3,0,2,1:T(4,128)(2,1)S(1)}, bf16[3,1,3,1024]{3,0,2,1:T(4,128)(2,1)S(1)}, u32[]{:S(2)}, u32[]{:S(2)}) collective-permute-start(bf16[3,1,3,1024]{3,0,2,1:T(4,128)(2,1)S(1)} %get-tuple-element.15), channel_id=1, source_target_pairs={{8,0},{16,8},{24,16},{32,24},{40,32},{48,40},{56,48},{64,56},{72,6... | collective-permute-start | bytes 55304 | tf_op jit(solution)/shard_map/ppermute | solution.py:402
  175.8 118.4 %collective-permute-start.10 = (bf16[3,5,1,1024]{3,0,2,1:T(4,128)(2,1)S(1)}, bf16[3,5,1,1024]{3,0,2,1:T(4,128)(2,1)S(1)}, u32[]{:S(2)}, u32[]{:S(2)}) collective-permute-start(bf16[3,5,1,1024]{3,0,2,1:T(4,128)(2,1)S(1)} %get-tuple-element.12), channel_id=1, source_target_pairs={{0,1},{1,2},{2,3},{3,4},{4,5},{5,6},{6,7},{8,9},{9,10},{10,11},{11... | collective-permute-start | bytes 92168 | tf_op jit(solution)/shard_map/ppermute | solution.py:401
  179.3 114.9 %collective-permute-start.11 = (bf16[3,5,1,1024]{3,0,2,1:T(4,128)(2,1)S(1)}, bf16[3,5,1,1024]{3,0,2,1:T(4,128)(2,1)S(1)}, u32[]{:S(2)}, u32[]{:S(2)}) collective-permute-start(bf16[3,5,1,1024]{3,0,2,1:T(4,128)(2,1)S(1)} %get-tuple-element.13), channel_id=1, source_target_pairs={{1,0},{2,1},{3,2},{4,3},{5,4},{6,5},{7,6},{9,8},{10,9},{11,10},{12... | collective-permute-start | bytes 92168 | tf_op jit(solution)/shard_map/ppermute | solution.py:402

commit v2 on v1

v2 whole, which is shorter than its diff:
```python
import math

import jax
import jax.numpy as jnp
from jax import lax
from jax.experimental import pallas as pl
from jax.experimental.pallas import tpu as pltpu
from jax.sharding import PartitionSpec as P

F = 256
HEADS = 8
LAYERS = 2
SLOTS = 64
TILE = 128
GROUP = 8
ROWS = GROUP * SLOTS
QUAD = 128

NORM_EPS = 1e-05
PAIR_SOFTEN = 0.01
SCREEN_RATE = 0.1
COULOMB_UNIT = 14.4
CHARGE_SOFTEN = 1.0
FAR = 1e30
GAUSS = 2.0 * SCREEN_RATE / math.sqrt(math.pi)
ERFC_P = 0.6
ERFC_C = (
    0.33858295223558404,
    0.33681896467541816,
    0.2948193558779553,
    0.06093701313639673,
    0.3109940554359323,
    -0.6781244471753995,
    0.4339317702022656,
    -0.0979638654555287,
)
MIB = 1024 * 1024


def dot(a, b):
    return lax.dot_general(a, b, (((1,), (0,)), ((), ())), preferred_element_type=jnp.float32)


def dot_nt(a, b):
    return lax.dot_general(a, b, (((1,), (1,)), ((), ())), preferred_element_type=jnp.float32)


def dot_tn(a, b):
    return lax.dot_general(a, b, (((0,), (0,)), ((), ())), preferred_element_type=jnp.float32)


def recip(x):
    return pl.reciprocal(x, approx=True)


def pair_body(pairs_ref, count_ref, own_ref, near_ref, force_ref, energy_ref, own_cols, total):
    own_tiles = own_ref.shape[0]
    total[...] = jnp.zeros_like(total)
    energy_ref[...] = jnp.zeros_like(energy_ref)
    for t in range(own_tiles):
        cols = jnp.transpose(own_ref[t])
        for c in range(4):
            own_cols[t, c] = jnp.broadcast_to(cols[:, c : c + 1], (TILE, TILE))
    chunk = 32
    lane = lax.broadcasted_iota(jnp.int32, (chunk, TILE), 1)
    row = lax.broadcasted_iota(jnp.int32, (chunk, TILE), 0)
    rel = lane - row

    def one_pair(p, carry):
        own = pairs_ref[0, p]
        near = pairs_ref[1, p]
        n = near_ref[near]
        xj, yj, zj, qj = (n[c : c + 1, :] for c in range(4))
        same = jnp.where(near - 4 * own_tiles == own, 0, 4 * TILE)
        en = jnp.zeros((8, TILE), jnp.float32)
        for start in range(0, TILE, chunk):
            at = pl.ds(start, chunk)
            dx = own_cols[own, 0, at, :] - xj
            dy = own_cols[own, 1, at, :] - yj
            dz = own_cols[own, 2, at, :] - zj
            qq = jnp.where(rel == same + start, 0.0, own_cols[own, 3, at, :] * qj)
            s = dx * dx + dy * dy + dz * dz + CHARGE_SOFTEN
            s = jnp.minimum(s, 1e6)
            rinv = lax.rsqrt(s)
            t = recip(1.0 + (ERFC_P * SCREEN_RATE) * (s * rinv))
            g = ERFC_C[-1]
            for coef in ERFC_C[-2::-1]:
                g = g * t + coef
            gauss = qq * jnp.exp2((-SCREEN_RATE * SCREEN_RATE * math.log2(math.e)) * s)
            screened = (g * t) * rinv
            en += jnp.sum((gauss * screened).reshape(chunk // 8, 8, TILE), axis=0)
            w = (gauss * (screened + GAUSS)) * (rinv * rinv)
            total[own, 0, at, :] += w * dx
            total[own, 1, at, :] += w * dy
            total[own, 2, at, :] += w * dz
        energy_ref[...] += en
        return carry

    lax.fori_loop(0, count_ref[0], one_pair, 0)
    for t in range(own_tiles):
        for c in range(3):
            force_ref[c, t : t + 1, :] = jnp.sum(
                jnp.transpose(total[t, c]), axis=0, keepdims=True
            )


def solvent_pairs(own8, near8, pairs, count):
    tiles = own8.shape[0]
    smem = pl.BlockSpec(memory_space=pltpu.SMEM)
    vmem = pl.BlockSpec(memory_space=pltpu.VMEM)
    return pl.pallas_call(
        pair_body,
        out_shape=(
            jax.ShapeDtypeStruct((3, tiles, TILE), jnp.float32),
            jax.ShapeDtypeStruct((8, TILE), jnp.float32),
        ),
        in_specs=[smem, smem, vmem, vmem],
        out_specs=(vmem, vmem),
        scratch_shapes=[
            pltpu.VMEM((tiles, 4, TILE, TILE), jnp.float32),
            pltpu.VMEM((tiles, 3, TILE, TILE), jnp.float32),
        ],
        compiler_params=pltpu.CompilerParams(vmem_limit_bytes=16 * MIB),
        name="pair_tiles",
    )(pairs, count, own8, near8)


def norm_parts(hidden):
    centre = jnp.mean(hidden, axis=-1, keepdims=True)
    shifted = hidden - centre
    spread = jnp.mean(shifted * shifted, axis=-1, keepdims=True)
    scale = lax.rsqrt(spread + NORM_EPS)
    return shifted * scale, scale


def norm_back(grad, gain, unit, scale):
    g = grad * gain
    mean_g = jnp.mean(g, axis=-1, keepdims=True)
    mean_gu = jnp.mean(g * unit, axis=-1, keepdims=True)
    return scale * (g - mean_g - unit * mean_gu)


def bf16(x):
    return x.astype(jnp.bfloat16)


def fragment_body(
    order_ref,
    slot_ref,
    near_ref,
    feat_ref,
    cap_ref,
    wqkv_ref,
    wout_ref,
    gains_ref,
    span_ref,
    span_cols_ref,
    wread_ref,
    wen_ref,
    force_ref,
    energy_ref,
    table,
    slots,
    slot_force,
    bins,
):
    tiles = near_ref.shape[0]
    frags = order_ref.shape[0]

    def widen(i, carry):
        for k in range(8):
            at = pl.multiple_of(i * 8 * TILE + k * TILE, TILE)
            both = feat_ref[pl.ds(at, TILE), :].astype(jnp.float32)
            table[0, pl.ds(at, TILE), :] = both[:, :QUAD]
            table[1, pl.ds(at, TILE), :] = both[:, QUAD:]
            n = jnp.transpose(near_ref[i * 8 + k])
            table[2, pl.ds(at, TILE), :] = jnp.concatenate(
                [n, jnp.zeros((TILE, TILE - 8), jnp.float32)], axis=1
            )
        return carry

    lax.fori_loop(0, tiles // 8, widen, 0)
    slot_force[...] = jnp.zeros_like(slot_force)
    energy_ref[...] = jnp.zeros_like(energy_ref)

    def fill(i, state):
        low, high, made = state
        big = order_ref[jnp.minimum(low, frags - 1)]
        small = order_ref[jnp.maximum(high, 0)]
        big_live, small_live = big >> 6, small >> 6
        start = (big_live + 7) & -8
        fits = start + ((small_live + 7) & -8) <= SLOTS
        both = jnp.logical_and(low < high, fits)
        bins[0, made] = big & 63
        bins[1, made] = small & 63
        bins[2, made] = big_live
        bins[3, made] = jnp.where(both, start, SLOTS)
        bins[4, made] = jnp.where(both, small_live, 0)
        one = jnp.where(low <= high, 1, 0)
        return low + one, high - jnp.where(both, 1, 0), made + one

    _, _, made = lax.fori_loop(0, frags, fill, (0, frags - 1, 0))
    for k in range(GROUP - 1):
        bins[0, made + k] = 0
        bins[1, made + k] = 0
        bins[2, made + k] = 0
        bins[3, made + k] = SLOTS
        bins[4, made + k] = 0

    lane = lax.broadcasted_iota(jnp.int32, (1, QUAD), 1)
    head_mask = [(lane // 32 == h).astype(jnp.bfloat16) for h in range(4)]
    head_pick = [lane // 32 == h for h in range(4)]
    slot_row = lax.broadcasted_iota(jnp.int32, (SLOTS, QUAD), 0)
    slot_lane = lax.broadcasted_iota(jnp.int32, (SLOTS, QUAD), 1) % SLOTS

    def spread_heads(x):
        return jnp.concatenate([x * head_mask[h] for h in range(4)], axis=0)

    def fold_heads(x):
        out = jnp.where(head_pick[0], x[0:SLOTS], 0.0)
        for h in range(1, 4):
            out = jnp.where(head_pick[h], x[h * SLOTS : (h + 1) * SLOTS], out)
        return out

    half = 0.5 / math.sqrt(32.0)
    units = [(f, quad) for f in range(GROUP) for quad in range(2)]

    def rows_of(f):
        return slice(f * SLOTS, (f + 1) * SLOTS)

    def one_block(b, carry):
        info = []
        for f in range(GROUP):
            big, small, first, start, second = (bins[c, b * GROUP + f] for c in range(5))
            bases = [
                pl.multiple_of(
                    jnp.where(k * 8 < start, big * SLOTS, small * SLOTS - start) + k * 8, 8
                )
                for k in range(SLOTS // 8)
            ]
            info.append((first, start, second, bases))

        for f in range(GROUP):
            for k, base in enumerate(info[f][3]):
                for j in range(8):
                    r = slot_ref[base + j]
                    at = f * SLOTS + k * 8 + j
                    for c in range(3):
                        slots[c, at : at + 1, :] = table[c, pl.ds(r, 1), :]

        atom_rows = jnp.transpose(slots[2])
        dists, inverses, offsets, weights = [], [], [], []
        for f in range(GROUP):
            first, start, second, bases = info[f]
            col = slots[2, rows_of(f), :]
            row = atom_rows[0:8, rows_of(f)]
            row = jnp.concatenate([row, row], axis=1)
            off = [col[:, c : c + 1] - row[c : c + 1, :] for c in range(3)]
            square = off[0] * off[0] + off[1] * off[1] + off[2] * off[2] + PAIR_SOFTEN
            inverse = lax.rsqrt(square)

            def owner(i, dead):
                late = jnp.logical_and(i >= start, i < start + second)
                return jnp.where(i < first, 1, jnp.where(late, 2, dead))

            mine = owner(slot_row, 0)
            dists.append(jnp.where(mine == owner(slot_lane, -1), square * inverse, FAR))
            inverses.append(inverse)
            offsets.append(off)
            cap = jnp.concatenate([cap_ref[pl.ds(base, 8), :] for base in bases], axis=0)
            weights.append(jnp.where(mine > 0, cap, 0.0))
        dist2 = [jnp.concatenate([d, d], axis=1) for d in dists]
        weight = jnp.concatenate(weights, axis=0)

        def attention(layer, project):
            def part(f, quad, which):
                at = which * F + quad * QUAD
                return project[rows_of(f), at : at + QUAD]

            qs = [part(f, quad, 0) for f, quad in units]
            kbs = [spread_heads(part(f, quad, 1)) for f, quad in units]
            vbs = [spread_heads(part(f, quad, 2)) for f, quad in units]
            scores = [dot_nt(q, kb) for q, kb in zip(qs, kbs)]
            atts, by_dist, by_score = [], [], []
            for (f, quad), score in zip(units, scores):
                u = score * half
                th = jnp.tanh(u)
                silu = u + u * th
                span = span_ref[layer : layer + 1, quad * 256 : (quad + 1) * 256]
                damp = recip(dist2[f] + span)
                att = silu * damp
                atts.append(bf16(att))
                by_dist.append(att * damp)
                if layer == 1:
                    by_score.append(damp * ((1.0 + th) + (silu - silu * th)))
            span_cols = span_cols_ref[layer : layer + 1, :]
            message = [dot(att, vb) for att, vb in zip(atts, vbs)]
            message = jnp.concatenate(
                [jnp.concatenate(message[2 * f : 2 * f + 2], axis=1) for f in range(GROUP)], axis=0
            )
            return bf16(message * span_cols), (qs, kbs, vbs, atts, by_dist, by_score)

        gain = [gains_ref[i : i + 1, :] for i in range(LAYERS + 1)]
        h0 = jnp.concatenate([slots[0], slots[1]], axis=1)
        unit0, _ = norm_parts(h0)
        project0 = bf16(dot(bf16(unit0 * gain[0]), wqkv_ref[0]))
        message0, kept0 = attention(0, project0)
        h1 = h0 + dot(message0, wout_ref[0])
        unit1, scale1 = norm_parts(h1)
        project1 = bf16(dot(bf16(unit1 * gain[1]), wqkv_ref[1]))
        message1, kept1 = attention(1, project1)
        h2 = h1 + dot(message1, wout_ref[1])
        unit2, scale2 = norm_parts(h2)
        u = 0.5 * dot(bf16(unit2 * gain[2]), wread_ref[...])
        th = jnp.tanh(u)
        silu = u + u * th
        weighted = weight * wen_ref[...]
        energy_ref[...] += jnp.sum((weighted * silu).reshape(ROWS // 8, 8, QUAD), axis=0)

        dread = bf16((0.5 * weighted) * ((1.0 + th) + (silu - silu * th)))
        dh2 = norm_back(dot_nt(dread, wread_ref[...]), gain[2], unit2, scale2)
        dmsg1 = bf16(dot_nt(bf16(dh2), wout_ref[1]) * span_cols_ref[1:2, :])
        qs, kbs, vbs, atts, by_dist, by_score = kept1
        dms = [dmsg1[rows_of(f), quad * QUAD : (quad + 1) * QUAD] for f, quad in units]
        datts = [dot_nt(dm, vb) for dm, vb in zip(dms, vbs)]
        dvs = [bf16(fold_heads(dot_tn(att, dm))) for att, dm in zip(atts, dms)]
        dss = [bf16(datt * slope) for datt, slope in zip(datts, by_score)]
        dqs = [bf16(dot(ds, kb) * half) for ds, kb in zip(dss, kbs)]
        dks = [bf16(fold_heads(dot_tn(ds, q)) * half) for ds, q in zip(dss, qs)]
        pulls = [datt * slope for datt, slope in zip(datts, by_dist)]
        dproject = jnp.concatenate(
            [
                jnp.concatenate(
                    [x[2 * f + quad] for x in (dqs, dks, dvs) for quad in range(2)], axis=1
                )
                for f in range(GROUP)
            ],
            axis=0,
        )
        dh1 = dh2 + norm_back(dot_nt(dproject, wqkv_ref[1]), gain[1], unit1, scale1)
        dmsg0 = bf16(dot_nt(bf16(dh1), wout_ref[0]) * span_cols_ref[0:1, :])
        datts = [
            dot_nt(dmsg0[rows_of(f), quad * QUAD : (quad + 1) * QUAD], vb)
            for (f, quad), vb in zip(units, kept0[2])
        ]
        pulls = [old + datt * slope for old, datt, slope in zip(pulls, datts, kept0[4])]
        force_rows = []
        for f in range(GROUP):
            pull = pulls[2 * f] + pulls[2 * f + 1]
            pull = (pull[:, :QUAD] + pull[:, QUAD:]) * inverses[f]
            pull = pull[:, :SLOTS] + pull[:, SLOTS:]
            pull = pull + jnp.transpose(pull)
            for c in range(3):
                force_rows.append(
                    -jnp.sum(pull * offsets[f][c][:, :SLOTS], axis=0, keepdims=True)
                )
        packed = jnp.concatenate(
            [
                jnp.concatenate([force_rows[3 * f + c] for f in range(GROUP)], axis=1)
                for c in range(3)
            ]
            + [jnp.zeros((5, ROWS), jnp.float32)],
            axis=0,
        )
        slot_force[:, 8:16] = jnp.transpose(packed)

        for f in range(GROUP):
            for k, base in enumerate(info[f][3]):
                rs = [slot_ref[base + j] for j in range(8)]
                old = [table[2, pl.ds(r, 1), :] for r in rs]
                for j in range(8):
                    at = f * SLOTS + k * 8 + j
                    table[2, pl.ds(rs[j], 1), :] = old[j] + slot_force[at : at + 1, :]
        return carry

    lax.fori_loop(0, (made + GROUP - 1) // GROUP, one_block, 0)

    pick = (
        lax.broadcasted_iota(jnp.int32, (16, TILE), 0) + 8
        == lax.broadcasted_iota(jnp.int32, (16, TILE), 1)
    ).astype(jnp.bfloat16)
    for i in range(tiles // 8):
        rows = dot_nt(pick, bf16(table[2, i * 1024 : (i + 1) * 1024, :]))
        for c in range(3):
            for k in range(8):
                force_ref[i, c, k : k + 1, :] = rows[c : c + 1, k * TILE : (k + 1) * TILE]


def fragment_model(near8, near_features, slot_index, atom_count, cap_weight, weights):
    w_qkv, w_out, gains, rates, w_read, w_energy = weights
    tiles = near8.shape[0]
    frags = atom_count.shape[0]
    smem = pl.BlockSpec(memory_space=pltpu.SMEM)
    vmem = pl.BlockSpec(memory_space=pltpu.VMEM)
    ids = jnp.arange(frags, dtype=jnp.int32)
    key = atom_count * 64 + ids
    place = jnp.sum(key[None, :] > key[:, None], axis=1)
    order = jnp.sum(jnp.where(place[None, :] == ids[:, None], key[None, :], 0), axis=1)
    spans = 1.0 / rates
    force, energy = pl.pallas_call(
        fragment_body,
        out_shape=(
            jax.ShapeDtypeStruct((tiles // 8, 3, 8, TILE), jnp.float32),
            jax.ShapeDtypeStruct((8, TILE), jnp.float32),
        ),
        in_specs=[smem, smem] + [vmem] * 10,
        out_specs=(vmem, vmem),
        scratch_shapes=[
            pltpu.VMEM((3, tiles * TILE, TILE), jnp.float32),
            pltpu.VMEM((3, ROWS, TILE), jnp.float32),
            pltpu.VMEM((ROWS, TILE), jnp.float32),
            pltpu.SMEM((5, frags + GROUP + 1), jnp.int32),
        ],
        compiler_params=pltpu.CompilerParams(vmem_limit_bytes=56 * MIB),
        name="fragments",
    )(
        order,
        slot_index.reshape(-1),
        near8,
        near_features,
        jnp.broadcast_to(cap_weight.reshape(-1, 1), (frags * SLOTS, TILE)),
        w_qkv,
        w_out,
        gains,
        jnp.repeat(spans, SLOTS, axis=1),
        jnp.repeat(spans, F // HEADS, axis=1),
        w_read,
        w_energy.reshape(1, -1),
    )
    return force, energy


def home_body(
    force_ref,
    pair_ref,
    frag_energy_ref,
    pair_energy_ref,
    out_ref,
    energy_ref,
    landing,
    by_sub,
    by_brick,
    force_send,
    force_recv,
    sub_send,
    sub_recv,
    brick_send,
    brick_recv,
):
    bricks, subs = by_brick.shape[0], by_sub.shape[0]
    brick, sub = lax.axis_index("brick"), lax.axis_index("sub")
    mesh_id = pl.DeviceIdType.MESH
    around = [(u, v) for u in (-1, 0, 1) for v in (-1, 0, 1) if (u, v) != (0, 0)]

    def inside(u, v):
        b, s = brick + u, sub + v
        return (b >= 0) & (b < bricks) & (s >= 0) & (s < subs)

    sub_peers = [(brick, lax.rem(sub + d, subs)) for d in range(1, subs)]
    brick_peers = [(lax.rem(brick + d, bricks), sub) for d in range(1, bricks)]

    barrier = pltpu.get_barrier_semaphore()
    for peer in sub_peers + brick_peers:
        pl.semaphore_signal(barrier, inc=1, device_id=peer, device_id_type=mesh_id)
    corners = [(u, v) for u, v in around if u != 0 and v != 0]
    for u, v in corners:

        @pl.when(inside(u, v))
        def _(u=u, v=v):
            pl.semaphore_signal(
                barrier, inc=1, device_id=(brick + u, sub + v), device_id_type=mesh_id
            )

    beside = [
        jnp.where(at > 0, 1, 0) + jnp.where(at < size - 1, 1, 0)
        for at, size in ((brick, bricks), (sub, subs))
    ]
    pl.semaphore_wait(barrier, subs + bricks - 2 + beside[0] * beside[1])

    def energy_copy(store, send, recv, k, slot, peer):
        return pltpu.make_async_remote_copy(
            src_ref=store.at[slot],
            dst_ref=store.at[slot],
            send_sem=send.at[k],
            recv_sem=recv.at[slot],
            device_id=peer,
            device_id_type=mesh_id,
        )

    by_sub[sub] = frag_energy_ref[...] + (0.5 * COULOMB_UNIT) * pair_energy_ref[...]
    for k, peer in enumerate(sub_peers):
        energy_copy(by_sub, sub_send, sub_recv, k, sub, peer).start()

    def force_copy(u, v):
        k = (u + 1) * 3 + v + 1
        return pltpu.make_async_remote_copy(
            src_ref=force_ref.at[k],
            dst_ref=landing.at[k],
            send_sem=force_send.at[k],
            recv_sem=force_recv.at[k],
            device_id=(brick + u, sub + v),
            device_id_type=mesh_id,
        )

    for u, v in around:

        @pl.when(inside(u, v))
        def _(u=u, v=v):
            force_copy(u, v).start()

    for k, peer in enumerate(sub_peers):
        energy_copy(by_sub, sub_send, sub_recv, k, peer[1], peer).wait_recv()
    by_brick[brick] = jnp.sum(by_sub[...], axis=0)
    for k, peer in enumerate(brick_peers):
        energy_copy(by_brick, brick_send, brick_recv, k, brick, peer).start()

    out_ref[...] = force_ref[4] + COULOMB_UNIT * pair_ref[...]
    for u, v in around:
        @pl.when(inside(-u, -v))
        def _(u=u, v=v):
            force_copy(u, v).wait_recv()
            out_ref[...] += landing[(u + 1) * 3 + v + 1]

    for k, peer in enumerate(brick_peers):
        energy_copy(by_brick, brick_send, brick_recv, k, peer[0], peer).wait_recv()
    energy_ref[0, 0] = jnp.sum(jnp.sum(by_brick[...], axis=0))

    for u, v in around:

        @pl.when(inside(u, v))
        def _(u=u, v=v):
            force_copy(u, v).wait_send()

    for k, peer in enumerate(sub_peers):
        energy_copy(by_sub, sub_send, sub_recv, k, sub, peer).wait_send()
    for k, peer in enumerate(brick_peers):
        energy_copy(by_brick, brick_send, brick_recv, k, brick, peer).wait_send()


def bring_home(row_force, pair_force, frag_energy, pair_energy):
    bricks, subs = lax.axis_size("brick"), lax.axis_size("sub")
    vmem = pl.BlockSpec(memory_space=pltpu.VMEM)
    block = row_force.shape[1:]
    dma = pltpu.SemaphoreType.DMA
    return pl.pallas_call(
        home_body,
        out_shape=(
            jax.ShapeDtypeStruct(block, jnp.float32),
            jax.ShapeDtypeStruct((1, 1), jnp.float32),
        ),
        in_specs=[vmem] * 4,
        out_specs=(vmem, pl.BlockSpec(memory_space=pltpu.SMEM)),
        scratch_shapes=[
            pltpu.VMEM((9,) + block, jnp.float32),
            pltpu.VMEM((subs, 8, TILE), jnp.float32),
            pltpu.VMEM((bricks, 8, TILE), jnp.float32),
            dma((9,)),
            dma((9,)),
            dma((subs,)),
            dma((subs,)),
            dma((bricks,)),
            dma((bricks,)),
        ],
        compiler_params=pltpu.CompilerParams(collective_id=1, has_side_effects=True),
        name="bring_home",
    )(row_force, pair_force, frag_energy, pair_energy)


def with_halo(x, sides, width):
    for axis, dim in sides:
        devices, length = (lax.axis_size(axis), x.shape[dim])
        up = [(i, (i + 1) % devices) for i in range(devices - 1)]
        down = [(j, i) for i, j in up]
        last = lax.slice_in_dim(x, length - width, length, axis=dim)
        initial = lax.slice_in_dim(x, 0, width, axis=dim)
        before = lax.ppermute(last, axis, up)
        after = lax.ppermute(initial, axis, down)
        x = jnp.concatenate([before, x, after], axis=dim)
    return x


def body(
    atom_features,
    positions,
    charges,
    slot_index,
    atom_count,
    cap_weight,
    tile_pairs,
    tile_count,
    w_qkv,
    w_out,
    gains,
    rates,
    w_read,
    w_energy,
):
    own_size = atom_features.shape[2]
    own_tiles = own_size // TILE
    own8 = jnp.concatenate([positions.reshape(3, -1), charges.reshape(1, -1)], axis=0)
    own8 = jnp.pad(own8, ((0, 4), (0, 0))).reshape(8, own_tiles, TILE).transpose(1, 0, 2)
    near8 = with_halo(own8[None, None], (("brick", 0), ("sub", 1)), 1).reshape(-1, 8, TILE)
    near_features = with_halo(atom_features, (("brick", 0), ("sub", 1)), 1)
    pair_force, pair_energy = solvent_pairs(
        own8, near8, tile_pairs.reshape(2, -1), tile_count.reshape(1)
    )
    row_force, frag_energy = fragment_model(
        near8,
        near_features.reshape(-1, F),
        slot_index,
        atom_count,
        cap_weight,
        (w_qkv, w_out, gains, rates, w_read, w_energy),
    )
    forces, energy = bring_home(row_force, pair_force, frag_energy, pair_energy)
    return forces.reshape(3, 1, 1, own_size), energy.reshape(())


def solution(mesh):
    in_specs = (
        P("brick", "sub", None, None),
        P(None, "brick", "sub", None),
        P("brick", "sub", None),
        P(("brick", "sub"), None),
        P(("brick", "sub")),
        P(("brick", "sub"), None),
        P(None, "brick", "sub", None),
        P("brick", "sub"),
        P(),
        P(),
        P(),
        P(),
        P(),
        P(),
    )
    out_specs = (P(None, "brick", "sub", None), P())
    return jax.shard_map(body, mesh=mesh, in_specs=in_specs, out_specs=out_specs, check_vma=False)
```

time: 296 us -> 135 us (0.46)
  blocking collectives: 99.4 us -> 0 us
  Pallas kernels: 123 us -> 77.6 us
  starting transfers between devices: 33.3 us -> 24 us
  waiting for transfers between devices: 22.4 us -> 17.8 us
  other arithmetic: 8.65 us -> 4.37 us
    psum x1 -> x0, blocking collectives: 99.4 us -> none  [body(): energy_sum = lax.psum(ml_energy + mm_energy, ('brick', 'sub'))]
    pallas_call x1, Pallas kernels: 115 us -> 45.7 us  [fragment_model(): pl.pallas_call(fragment_body, out_shape=(jax.ShapeDtypeStruct((tiles // 8...]
    pallas_call x1 -> x2, Pallas kernels: 8.12 us -> 31.8 us  [the longest x1 24.8 us: bring_home(): pl.pallas_call(home_body, out_shape=(jax.ShapeDtypeStruct(block, jnp.floa...]
    ppermute x6 -> x4, starting transfers between devices: 23.7 us -> 17.6 us  [with_halo(): before = lax.ppermute(last, axis, up)]
    ppermute x6 -> x4, waiting for transfers between devices: 12.9 us -> 7.23 us  [with_halo(): after = lax.ppermute(initial, axis, down)]
    ppermute x6 -> x4, starting transfers between devices: 9.64 us -> 6.43 us  [with_halo(): after = lax.ppermute(initial, axis, down)]
    ppermute x6 -> x4, waiting for transfers between devices: 9.57 us -> 10.6 us  [with_halo(): before = lax.ppermute(last, axis, up)]
  transfers between devices with their start and end apart: 12 -> 8, of which waited for: 5 -> 5; matrix products, arithmetic and copies ran while one was open for 3% -> 3% of each run, Pallas kernels for 3% -> 5%
where the time goes in v2:
time: 135 us
  Pallas kernels  77.6 us (57%)
  starting transfers between devices  24 us (18%)
  waiting for transfers between devices  17.8 us (13%)
  local copies, waits for them, and re-layouts  7.57 us (6%)
  other arithmetic  4.37 us (3%)
  between operations  3.21 us (2%)
    pallas_call x1, Pallas kernels, fragment_model(): pl.pallas_call(fragment_body, out_shape=(jax.ShapeDtypeStruct((tiles // 8...  45.7 us
    pallas_call x1, Pallas kernels, bring_home(): pl.pallas_call(home_body, out_shape=(jax.ShapeDtypeStruct(block, jnp.floa...  24.8 us
    ppermute x4, starting transfers between devices, with_halo(): before = lax.ppermute(last, axis, up)  17.6 us
    ppermute x4, waiting for transfers between devices, with_halo(): before = lax.ppermute(last, axis, up)  10.6 us
    ppermute x4, waiting for transfers between devices, with_halo(): after = lax.ppermute(initial, axis, down)  7.23 us
    pallas_call x1, Pallas kernels, solvent_pairs(): pl.pallas_call(pair_body, out_shape=(jax.ShapeDtypeStruct((3, tiles, TILE...  7.06 us
    ppermute x4, starting transfers between devices, with_halo(): after = lax.ppermute(initial, axis, down)  6.43 us
    unnamed x24, local copies, waits for them, and re-layouts  3.64 us
  transfers between devices with their start and end apart: 8, of which 5 were waited for; matrix products, arithmetic and copies ran while one was open for 3% of the time, Pallas kernels for 5%

profile of v2, /device:TPU:1, one launch (start us, length us, event | category | flops | bytes accessed | tf_op | source)
XLA Modules:
  0.0 134.5 jit_solution(18276171901324988696)
XLA Ops:
  0.6 0.0 copy-start.6
  0.6 0.0 copy-start.7
  0.7 0.0 copy-start.9
  0.7 0.0 copy-start.8
  0.7 0.0 copy-start.4
  0.7 0.0 copy-start.5
  0.7 4.1 %collective-permute-start.4 = (bf16[1,1,1024,256]{3,2,1,0:T(8,128)(2,1)}, bf16[1,1,1024,256]{3,2,1,0:T(8,128)(2,1)S(1)}, u32[]{:S(2)}, u32[]{:S(2)}) collective-permute-start(bf16[1,1,1024,256]{3,2,1,0:T(8,128)(2,1)} %param.14), channel_id=1, source_target_pairs={{0,8},{8,16},{16,24},{24,32},{32,40},{40,48},{48,56},{56,64},{64,7... | collective-permute-start | bytes 1572872 | tf_op jit(solution)/shard_map/ppermute | solution.py:576
  4.8 1.3 collective-permute-start.5
  6.1 9.6 %collective-permute-done.4 = bf16[1,1,1024,256]{3,2,1,0:T(8,128)(2,1)S(1)} collective-permute-done((bf16[1,1,1024,256]{3,2,1,0:T(8,128)(2,1)}, bf16[1,1,1024,256]{3,2,1,0:T(8,128)(2,1)S(1)}, u32[]{:S(2)}, u32[]{:S(2)}) %collective-permute-start.4) | collective-permute-done | bytes 524320 | tf_op jit(solution)/shard_map/ppermute | solution.py:576
  15.7 0.0 copy-start.3
  15.7 1.1 constant_dynamic-update-slice_fusion.1
  16.8 2.6 %collective-permute-done.5 = bf16[1,1,1024,256]{3,2,1,0:T(8,128)(2,1)S(1)} collective-permute-done((bf16[1,1,1024,256]{3,2,1,0:T(8,128)(2,1)}, bf16[1,1,1024,256]{3,2,1,0:T(8,128)(2,1)S(1)}, u32[]{:S(2)}, u32[]{:S(2)}) %collective-permute-start.5) | collective-permute-done | bytes 524320 | tf_op jit(solution)/shard_map/ppermute | solution.py:577
  19.4 5.3 %collective-permute-start.6 = (bf16[3,1,1024,256]{3,2,1,0:T(8,128)(2,1)S(1)}, bf16[3,1,1024,256]{3,2,1,0:T(8,128)(2,1)S(1)}, u32[]{:S(2)}, u32[]{:S(2)}) collective-permute-start(bf16[3,1,1024,256]{3,2,1,0:T(8,128)(2,1)S(1)} %constant_dynamic-update-slice_fusion), channel_id=1, source_target_pairs={{0,1},{1,2},{2,3},{3,4},{4,5},{5,6},{6,7},{8,9},{9,10},{10,11},{11... | collective-permute-start | bytes 4718600 | tf_op jit(solution)/shard_map/ppermute | solution.py:576
  24.7 1.9 %collective-permute-start.7 = (bf16[3,1,1024,256]{3,2,1,0:T(8,128)(2,1)S(1)}, bf16[3,1,1024,256]{3,2,1,0:T(8,128)(2,1)}, u32[]{:S(2)}, u32[]{:S(2)}) collective-permute-start(bf16[3,1,1024,256]{3,2,1,0:T(8,128)(2,1)S(1)} %constant_dynamic-update-slice_fusion), channel_id=1, source_target_pairs={{1,0},{2,1},{3,2},{4,3},{5,4},{6,5},{7,6},{9,8},{10,9},{11,10},{12... | collective-permute-start | bytes 4718600 | tf_op jit(solution)/shard_map/ppermute | solution.py:577
  26.7 0.0 copy-done.6
  26.7 0.0 copy-done.7
  26.7 3.1 %collective-permute-start = (f32[1,1,8,8,128]{4,3,2,1,0:T(8,128)S(1)}, f32[1,1,8,8,128]{4,3,2,1,0:T(8,128)S(1)}, u32[]{:S(2)}, u32[]{:S(2)}) collective-permute-start(f32[1,1,8,8,128]{4,3,2,1,0:T(8,128)S(1)} %get-tuple-element.21), channel_id=1, source_target_pairs={{0,8},{8,16},{16,24},{24,32},{32,40},{40,48},{48,56},{56,64},{64,7... | collective-permute-start | bytes 98312 | tf_op jit(solution)/shard_map/ppermute | solution.py:576
  29.8 1.3 collective-permute-start.1
  31.1 0.0 copy-done.9
  31.1 0.0 copy-done.8
  31.2 0.2 convert_reduce_fusion
  31.3 0.1 broadcast_in_dim.35
  31.4 0.7 reshape.54.span_ref
  32.1 0.1 broadcast_in_dim.36
  32.2 0.7 reshape.55.span_cols_ref
  32.8 0.0 copy-done.4
  32.8 0.1 broadcast_in_dim.33
  32.9 0.7 reshape.48.slot_ref
  34.2 0.0 collective-permute-done
  34.2 0.2 collective-permute-done.1
  34.5 5.1 %collective-permute-start.2 = (f32[3,1,8,8,128]{4,3,2,1,0:T(8,128)S(1)}, f32[3,1,8,8,128]{4,3,2,1,0:T(8,128)S(1)}, u32[]{:S(2)}, u32[]{:S(2)}) collective-permute-start(f32[3,1,8,8,128]{4,3,2,1,0:T(8,128)S(1)} %pad_maximum_fusion.2), channel_id=1, source_target_pairs={{0,1},{1,2},{2,3},{3,4},{4,5},{5,6},{6,7},{8,9},{9,10},{10,11},{11... | collective-permute-start | bytes 294920 | tf_op jit(solution)/shard_map/ppermute | solution.py:576
  39.6 1.9 %collective-permute-start.3 = (f32[3,1,8,8,128]{4,3,2,1,0:T(8,128)S(1)}, f32[3,1,8,8,128]{4,3,2,1,0:T(8,128)S(1)}, u32[]{:S(2)}, u32[]{:S(2)}) collective-permute-start(f32[3,1,8,8,128]{4,3,2,1,0:T(8,128)S(1)} %pad_maximum_fusion.2), channel_id=1, source_target_pairs={{1,0},{2,1},{3,2},{4,3},{5,4},{6,5},{7,6},{9,8},{10,9},{11,10},{12... | collective-permute-start | bytes 294920 | tf_op jit(solution)/shard_map/ppermute | solution.py:577
  41.5 0.6 select_reduce_fusion.order_ref
  42.1 1.0 collective-permute-done.2
  43.1 4.4 %collective-permute-done.3 = f32[3,1,8,8,128]{4,3,2,1,0:T(8,128)S(1)} collective-permute-done((f32[3,1,8,8,128]{4,3,2,1,0:T(8,128)S(1)}, f32[3,1,8,8,128]{4,3,2,1,0:T(8,128)S(1)}, u32[]{:S(2)}, u32[]{:S(2)}) %collective-permute-start.3) | collective-permute-done | bytes 98336 | tf_op jit(solution)/shard_map/ppermute | solution.py:577
  47.5 0.0 copy-start
  47.6 0.0 copy-done.3
  47.6 7.1 %pair_tiles.1 = (f32[3,8,128]{2,1,0:T(8,128)S(1)}, f32[8,128]{1,0:T(8,128)S(1)}) custom-call(s32[2,128]{1,0:T(2,128)S(1)} %bitcast.21, s32[1]{0:T(128)} %bitcast.18.count_ref, f32[8,8,128]{2,1,0:T(8,128)S(1)} %get-tuple-element.20.own_ref, f32[72,8,128]{2,1,0:T(8,128)S(1)} %bitcast.19), custom_call_target="tpu_custom_call" | custom-call | tf_op jit(solution)/shard_map/pair_tiles/pallas_call | solution.py:111
  54.6 0.6 copy-done.1
  55.2 0.6 copy-done.2
  55.8 0.0 collective-permute-done.6
  55.8 0.0 collective-permute-done.7
  55.8 3.5 %pad_maximum_fusion = bf16[3,3,1024,256]{3,2,1,0:T(8,128)(2,1)} fusion(bf16[3,1,1024,256]{3,2,1,0:T(8,128)(2,1)} %collective-permute-done.7, bf16[3,1,1024,256]{3,2,1,0:T(8,128)(2,1)S(1)} %constant_dynamic-update-slice_fusion, bf16[3,1,1024,256]{3,2,1,0:T(8,128)(2,1)S(1)} %collective-permute-done.6), kind=kLoop, calls=%fused_computation | loop fusion | flops 4718592 | bytes 9437184 | tf_op jit(solution)/shard_map/concatenate | solution.py:578
  59.3 0.0 copy-done
  59.3 1.7 %broadcast_in_dim.34.cap_ref = f32[3072,128]{1,0:T(8,128)} broadcast(f32[3072]{0:T(1024)S(1)} %broadcast_in_dim.33), dimensions={0} | broadcast | bytes 1585152 | tf_op jit(solution)/shard_map/broadcast_in_dim | solution.py:421
  61.0 45.7 %fragments.1 = (f32[9,3,8,128]{3,2,1,0:T(8,128)}, f32[8,128]{1,0:T(8,128)}) custom-call(s32[48]{0:T(128)} %select_reduce_fusion.order_ref, s32[3072]{0:T(1024)} %reshape.48.slot_ref, f32[72,8,128]{2,1,0:T(8,128)} %bitcast.20, bf16[9216,256]{1,0:T(8,128)(2,1)} %bitcast.22, f32[3072,128]{1,0:T(8,128)} %broadcast_in_dim.34.cap_ref, ...), custom_call_target="tpu_custom_call" | custom-call | tf_op jit(solution)/shard_map/fragments/pallas_call | solution.py:400
  106.8 24.8 %bring_home.1 = (f32[3,8,128]{2,1,0:T(8,128)}, f32[1,1]{1,0:T(1,128)}) custom-call(f32[9,3,8,128]{3,2,1,0:T(8,128)} %get-tuple-element.8.force_ref, f32[3,8,128]{2,1,0:T(8,128)} %copy-done.1, f32[8,128]{1,0:T(8,128)} %get-tuple-element.10.frag_energy_ref, f32[8,128]{1,0:T(8,128)} %copy-done.2), custom_call_target="tpu_custom_call" | custom-call | tf_op jit(solution)/shard_map/bring_home/pallas_call | solution.py:545
  131.6 1.3 copy.27
  (11 shorter events, 0.1 us)
Async XLA Ops:
  0.6 26.0 %copy-start.6 = (f32[3,1,1,1024]{3,2,1,0:T(1,128)S(1)}, f32[3,1,1,1024]{3,2,1,0:T(1,128)}, u32[]{:S(2)}) copy-start(f32[3,1,1,1024]{3,2,1,0:T(1,128)} %param.15) | copy-start | bytes 36868
  0.6 26.0 %copy-start.7 = (f32[1,1,1024]{2,1,0:T(1,128)S(1)}, f32[1,1,1024]{2,1,0:T(1,128)}, u32[]{:S(2)}) copy-start(f32[1,1,1024]{2,1,0:T(1,128)} %param.16) | copy-start | bytes 12292
  0.7 30.5 %copy-start.9 = (s32[48]{0:T(128)S(1)}, s32[48]{0:T(128)}, u32[]{:S(2)}) copy-start(s32[48]{0:T(128)} %param.18) | copy-start | bytes 580
  0.7 30.5 %copy-start.8 = (f32[2,8]{1,0:T(2,128)S(1)}, f32[2,8]{1,0:T(2,128)}, u32[]{:S(2)}) copy-start(f32[2,8]{1,0:T(2,128)} %param.25) | copy-start | bytes 196
  0.7 32.1 %copy-start.4 = (f32[48,64]{1,0:T(8,128)S(1)}, f32[48,64]{1,0:T(8,128)}, u32[]{:S(2)}) copy-start(f32[48,64]{1,0:T(8,128)} %param.19) | copy-start | bytes 36868
  0.7 32.2 %copy-start.5 = (s32[48,64]{1,0:T(8,128)S(1)}, s32[48,64]{1,0:T(8,128)}, u32[]{:S(2)}) copy-start(s32[48,64]{1,0:T(8,128)} %param.17) | copy-start | bytes 36868
  0.7 15.0 %collective-permute-start.4 = (bf16[1,1,1024,256]{3,2,1,0:T(8,128)(2,1)}, bf16[1,1,1024,256]{3,2,1,0:T(8,128)(2,1)S(1)}, u32[]{:S(2)}, u32[]{:S(2)}) collective-permute-start(bf16[1,1,1024,256]{3,2,1,0:T(8,128)(2,1)} %param.14), channel_id=1, source_target_pairs={{0,8},{8,16},{16,24},{24,32},{32,40},{40,48},{48,56},{56,64},{64,7... | collective-permute-start | bytes 1572872 | tf_op jit(solution)/shard_map/ppermute | solution.py:576
  4.8 14.6 %collective-permute-start.5 = (bf16[1,1,1024,256]{3,2,1,0:T(8,128)(2,1)}, bf16[1,1,1024,256]{3,2,1,0:T(8,128)(2,1)S(1)}, u32[]{:S(2)}, u32[]{:S(2)}) collective-permute-start(bf16[1,1,1024,256]{3,2,1,0:T(8,128)(2,1)} %param.14), channel_id=1, source_target_pairs={{8,0},{16,8},{24,16},{32,24},{40,32},{48,40},{56,48},{64,56},{72,6... | collective-permute-start | bytes 1572872 | tf_op jit(solution)/shard_map/ppermute | solution.py:577
  15.7 31.9 %copy-start.3 = (s32[2,1,1,128]{3,2,1,0:T(1,128)S(1)}, s32[2,1,1,128]{3,2,1,0:T(1,128)}, u32[]{:S(2)}) copy-start(s32[2,1,1,128]{3,2,1,0:T(1,128)} %param.20) | copy-start | bytes 3076
  19.4 36.4 %collective-permute-start.6 = (bf16[3,1,1024,256]{3,2,1,0:T(8,128)(2,1)S(1)}, bf16[3,1,1024,256]{3,2,1,0:T(8,128)(2,1)S(1)}, u32[]{:S(2)}, u32[]{:S(2)}) collective-permute-start(bf16[3,1,1024,256]{3,2,1,0:T(8,128)(2,1)S(1)} %constant_dynamic-update-slice_fusion), channel_id=1, source_target_pairs={{0,1},{1,2},{2,3},{3,4},{4,5},{5,6},{6,7},{8,9},{9,10},{10,11},{11... | collective-permute-start | bytes 4718600 | tf_op jit(solution)/shard_map/ppermute | solution.py:576
  24.7 31.1 %collective-permute-start.7 = (bf16[3,1,1024,256]{3,2,1,0:T(8,128)(2,1)S(1)}, bf16[3,1,1024,256]{3,2,1,0:T(8,128)(2,1)}, u32[]{:S(2)}, u32[]{:S(2)}) collective-permute-start(bf16[3,1,1024,256]{3,2,1,0:T(8,128)(2,1)S(1)} %constant_dynamic-update-slice_fusion), channel_id=1, source_target_pairs={{1,0},{2,1},{3,2},{4,3},{5,4},{6,5},{7,6},{9,8},{10,9},{11,10},{12... | collective-permute-start | bytes 4718600 | tf_op jit(solution)/shard_map/ppermute | solution.py:577
  26.7 7.5 %collective-permute-start = (f32[1,1,8,8,128]{4,3,2,1,0:T(8,128)S(1)}, f32[1,1,8,8,128]{4,3,2,1,0:T(8,128)S(1)}, u32[]{:S(2)}, u32[]{:S(2)}) collective-permute-start(f32[1,1,8,8,128]{4,3,2,1,0:T(8,128)S(1)} %get-tuple-element.21), channel_id=1, source_target_pairs={{0,8},{8,16},{16,24},{24,32},{32,40},{40,48},{48,56},{56,64},{64,7... | collective-permute-start | bytes 98312 | tf_op jit(solution)/shard_map/ppermute | solution.py:576
  29.8 4.7 %collective-permute-start.1 = (f32[1,1,8,8,128]{4,3,2,1,0:T(8,128)S(1)}, f32[1,1,8,8,128]{4,3,2,1,0:T(8,128)S(1)}, u32[]{:S(2)}, u32[]{:S(2)}) collective-permute-start(f32[1,1,8,8,128]{4,3,2,1,0:T(8,128)S(1)} %get-tuple-element.21), channel_id=1, source_target_pairs={{8,0},{16,8},{24,16},{32,24},{40,32},{48,40},{56,48},{64,56},{72,6... | collective-permute-start | bytes 98312 | tf_op jit(solution)/shard_map/ppermute | solution.py:577
  34.5 8.6 %collective-permute-start.2 = (f32[3,1,8,8,128]{4,3,2,1,0:T(8,128)S(1)}, f32[3,1,8,8,128]{4,3,2,1,0:T(8,128)S(1)}, u32[]{:S(2)}, u32[]{:S(2)}) collective-permute-start(f32[3,1,8,8,128]{4,3,2,1,0:T(8,128)S(1)} %pad_maximum_fusion.2), channel_id=1, source_target_pairs={{0,1},{1,2},{2,3},{3,4},{4,5},{5,6},{6,7},{8,9},{9,10},{10,11},{11... | collective-permute-start | bytes 294920 | tf_op jit(solution)/shard_map/ppermute | solution.py:576
  39.6 8.0 %collective-permute-start.3 = (f32[3,1,8,8,128]{4,3,2,1,0:T(8,128)S(1)}, f32[3,1,8,8,128]{4,3,2,1,0:T(8,128)S(1)}, u32[]{:S(2)}, u32[]{:S(2)}) collective-permute-start(f32[3,1,8,8,128]{4,3,2,1,0:T(8,128)S(1)} %pad_maximum_fusion.2), channel_id=1, source_target_pairs={{1,0},{2,1},{3,2},{4,3},{5,4},{6,5},{7,6},{9,8},{10,9},{11,10},{12... | collective-permute-start | bytes 294920 | tf_op jit(solution)/shard_map/ppermute | solution.py:577
  47.5 11.8 %copy-start = (f32[3,3,8,8,128]{4,3,2,1,0:T(8,128)}, f32[3,3,8,8,128]{4,3,2,1,0:T(8,128)S(1)}, u32[]{:S(2)}) copy-start(f32[3,3,8,8,128]{4,3,2,1,0:T(8,128)S(1)} %pad_maximum_fusion.1) | copy-start | bytes 884740
  54.6 0.6 copy-start.1
  55.2 0.6 copy-start.2

commit v3 on v2

--- a/solution.py
+++ b/solution.py
@@ -162,15 +162,16 @@
     table,
     slots,
     slot_force,
+    caps,
     bins,
 ):
     tiles = near_ref.shape[0]
-    frags = order_ref.shape[0]
+    frags = cap_ref.shape[0]
 
     def widen(i, carry):
         for k in range(8):
             at = pl.multiple_of(i * 8 * TILE + k * TILE, TILE)
-            both = feat_ref[pl.ds(at, TILE), :].astype(jnp.float32)
+            both = feat_ref[i, k * TILE : (k + 1) * TILE, :].astype(jnp.float32)
             table[0, pl.ds(at, TILE), :] = both[:, :QUAD]
             table[1, pl.ds(at, TILE), :] = both[:, QUAD:]
             n = jnp.transpose(near_ref[i * 8 + k])
@@ -181,25 +182,34 @@
 
     lax.fori_loop(0, tiles // 8, widen, 0)
     slot_force[...] = jnp.zeros_like(slot_force)
+    slots[0, :TILE, :] = jnp.zeros((TILE, TILE), jnp.float32)
+    slots[0, :frags, :SLOTS] = cap_ref[...]
+    cols = jnp.transpose(slots[0, :TILE, :])
+    for f in range(frags):
+        caps[f * SLOTS : (f + 1) * SLOTS, :] = jnp.broadcast_to(
+            cols[:SLOTS, f : f + 1], (SLOTS, TILE)
+        )
     energy_ref[...] = jnp.zeros_like(energy_ref)
 
-    def fill(i, state):
-        low, high, made = state
-        big = order_ref[jnp.minimum(low, frags - 1)]
+    high = frags - 1
+    made = 0
+    runs = [order_ref[frags + k] for k in range(5)]
+    for k in range(frags):
+        fits = (
+            ((k >= runs[0]) & (k < runs[1]))
+            | ((k >= runs[2]) & (k < runs[3]))
+            | (k >= runs[4])
+        )
+        both = fits & (k < high)
+        big = order_ref[k]
         small = order_ref[jnp.maximum(high, 0)]
-        big_live, small_live = big >> 6, small >> 6
-        start = (big_live + 7) & -8
-        fits = start + ((small_live + 7) & -8) <= SLOTS
-        both = jnp.logical_and(low < high, fits)
-        bins[0, made] = big & 63
-        bins[1, made] = small & 63
-        bins[2, made] = big_live
-        bins[3, made] = jnp.where(both, start, SLOTS)
-        bins[4, made] = jnp.where(both, small_live, 0)
-        one = jnp.where(low <= high, 1, 0)
-        return low + one, high - jnp.where(both, 1, 0), made + one
-
-    _, _, made = lax.fori_loop(0, frags, fill, (0, frags - 1, 0))
+        bins[0, k] = big & 63
+        bins[1, k] = small & 63
+        bins[2, k] = big >> 6
+        bins[3, k] = jnp.where(both, ((big >> 6) + 7) & -8, SLOTS)
+        bins[4, k] = jnp.where(both, small >> 6, 0)
+        made = jnp.where(k <= high, k + 1, made)
+        high = high - jnp.where(both, 1, 0)
     for k in range(GROUP - 1):
         bins[0, made + k] = 0
         bins[1, made + k] = 0
@@ -267,7 +277,7 @@
             dists.append(jnp.where(mine == owner(slot_lane, -1), square * inverse, FAR))
             inverses.append(inverse)
             offsets.append(off)
-            cap = jnp.concatenate([cap_ref[pl.ds(base, 8), :] for base in bases], axis=0)
+            cap = jnp.concatenate([caps[pl.ds(base, 8), :] for base in bases], axis=0)
             weights.append(jnp.where(mine > 0, cap, 0.0))
         dist2 = [jnp.concatenate([d, d], axis=1) for d in dists]
         weight = jnp.concatenate(weights, axis=0)
@@ -396,6 +406,13 @@
     key = atom_count * 64 + ids
     place = jnp.sum(key[None, :] > key[:, None], axis=1)
     order = jnp.sum(jnp.where(place[None, :] == ids[:, None], key[None, :], 0), axis=1)
+    eighths = (atom_count + 7) // 8
+    alone = jnp.sum((eighths >= 7).astype(jnp.int32))
+    n6, n5, n3, n2 = (jnp.sum((eighths == k).astype(jnp.int32)) for k in (6, 5, 3, 2))
+    with6 = jnp.minimum(n6, n2)
+    with5 = jnp.minimum(n5, n2 - with6 + n3)
+    runs = [alone, alone + with6, alone + n6, alone + n6 + with5, alone + n6 + n5]
+    order = jnp.concatenate([order, jnp.stack(runs)])
     spans = 1.0 / rates
     force, energy = pl.pallas_call(
         fragment_body,
@@ -409,6 +426,7 @@
             pltpu.VMEM((3, tiles * TILE, TILE), jnp.float32),
             pltpu.VMEM((3, ROWS, TILE), jnp.float32),
             pltpu.VMEM((ROWS, TILE), jnp.float32),
+            pltpu.VMEM((frags * SLOTS, TILE), jnp.float32),
             pltpu.SMEM((5, frags + GROUP + 1), jnp.int32),
         ],
         compiler_params=pltpu.CompilerParams(vmem_limit_bytes=56 * MIB),
@@ -418,7 +436,7 @@
         slot_index.reshape(-1),
         near8,
         near_features,
-        jnp.broadcast_to(cap_weight.reshape(-1, 1), (frags * SLOTS, TILE)),
+        cap_weight,
         w_qkv,
         w_out,
         gains,
@@ -566,17 +584,220 @@
     )(row_force, pair_force, frag_energy, pair_energy)
 
 
-def with_halo(x, sides, width):
-    for axis, dim in sides:
-        devices, length = (lax.axis_size(axis), x.shape[dim])
-        up = [(i, (i + 1) % devices) for i in range(devices - 1)]
-        down = [(j, i) for i, j in up]
-        last = lax.slice_in_dim(x, length - width, length, axis=dim)
-        initial = lax.slice_in_dim(x, 0, width, axis=dim)
-        before = lax.ppermute(last, axis, up)
-        after = lax.ppermute(initial, axis, down)
-        x = jnp.concatenate([before, x, after], axis=dim)
-    return x
+AROUND = [(u, v) for u in (-1, 0, 1) for v in (-1, 0, 1) if (u, v) != (0, 0)]
+CHUNKS = 4
+
+
+def block_of(u, v):
+    return (u + 1) * 3 + v + 1
+
+
+def halo_body(
+    own_ref,
+    feat_ref,
+    near_ref,
+    near_feat_ref,
+    atom_send,
+    atom_recv,
+    side_send,
+    side_recv,
+    ahead_send,
+    ahead_recv,
+    corner_send,
+    corner_recv,
+    local_sem,
+):
+    bricks, subs = lax.axis_size("brick"), lax.axis_size("sub")
+    brick, sub = lax.axis_index("brick"), lax.axis_index("sub")
+    mesh_id = pl.DeviceIdType.MESH
+    rows = feat_ref.shape[0]
+    tiles = own_ref.shape[0]
+    part = rows // CHUNKS
+
+    def inside(u, v):
+        b, s = brick + u, sub + v
+        return (b >= 0) & (b < bricks) & (s >= 0) & (s < subs)
+
+    barrier = pltpu.get_barrier_semaphore()
+    for u, v in AROUND:
+
+        @pl.when(inside(u, v))
+        def _(u=u, v=v):
+            pl.semaphore_signal(
+                barrier, inc=1, device_id=(brick + u, sub + v), device_id_type=mesh_id
+            )
+
+    beside = [
+        jnp.where(at > 0, 1, 0) + jnp.where(at < size - 1, 1, 0)
+        for at, size in ((brick, bricks), (sub, subs))
+    ]
+    pl.semaphore_wait(barrier, beside[0] + beside[1] + beside[0] * beside[1])
+
+    def atom_copy(u, v):
+        k = block_of(-u, -v)
+        return pltpu.make_async_remote_copy(
+            src_ref=own_ref,
+            dst_ref=near_ref.at[pl.ds(k * tiles, tiles)],
+            send_sem=atom_send.at[k],
+            recv_sem=atom_recv.at[k],
+            device_id=(brick + u, sub + v),
+            device_id_type=mesh_id,
+        )
+
+    def ahead_copy(u, c):
+        i = (u + 1) // 2
+        return pltpu.make_async_remote_copy(
+            src_ref=feat_ref.at[pl.ds(c * part, part)],
+            dst_ref=near_feat_ref.at[block_of(-u, 0), pl.ds(c * part, part)],
+            send_sem=ahead_send.at[i, c],
+            recv_sem=ahead_recv.at[i, c],
+            device_id=(brick + u, sub),
+            device_id_type=mesh_id,
+        )
+
+    def side_copy(v):
+        i = (v + 1) // 2
+        return pltpu.make_async_remote_copy(
+            src_ref=feat_ref,
+            dst_ref=near_feat_ref.at[block_of(0, -v)],
+            send_sem=side_send.at[i],
+            recv_sem=side_recv.at[i],
+            device_id=(brick, sub + v),
+            device_id_type=mesh_id,
+        )
+
+    def corner_copy(w, v, c):
+        i = (w + 1) + (v + 1) // 2
+        at = pl.ds(c * part, part)
+        return pltpu.make_async_remote_copy(
+            src_ref=near_feat_ref.at[block_of(w, 0), at],
+            dst_ref=near_feat_ref.at[block_of(w, -v), at],
+            send_sem=corner_send.at[i, c],
+            recv_sem=corner_recv.at[i, c],
+            device_id=(brick, sub + v),
+            device_id_type=mesh_id,
+        )
+
+    for u, v in AROUND:
+
+        @pl.when(inside(u, v))
+        def _(u=u, v=v):
+            atom_copy(u, v).start()
+
+    for c in range(CHUNKS):
+        for u in (-1, 1):
+
+            @pl.when(inside(u, 0))
+            def _(u=u, c=c):
+                ahead_copy(u, c).start()
+
+        if c == 0:
+            for v in (-1, 1):
+
+                @pl.when(inside(0, v))
+                def _(v=v):
+                    side_copy(v).start()
+
+    local = pltpu.make_async_copy(feat_ref, near_feat_ref.at[block_of(0, 0)], local_sem)
+    local.start()
+    near_ref[pl.ds(block_of(0, 0) * tiles, tiles)] = own_ref[...]
+    for u, v in AROUND:
+        k = block_of(u, v)
+
+        @pl.when(jnp.logical_not(inside(u, v)))
+        def _(k=k):
+            near_ref[pl.ds(k * tiles, tiles)] = jnp.zeros_like(own_ref)
+
+    def forward(c):
+        for w in (-1, 1):
+
+            @pl.when(inside(w, 0))
+            def _(w=w):
+                ahead_copy(-w, c).wait_recv()
+                for v in (-1, 1):
+
+                    @pl.when(inside(0, v))
+                    def _(w=w, v=v):
+                        corner_copy(w, v, c).start()
+
+    for c in range(CHUNKS):
+        forward(c)
+
+    for u, v in AROUND:
+
+        @pl.when(inside(-u, -v))
+        def _(u=u, v=v):
+            atom_copy(u, v).wait_recv()
+
+    for v in (-1, 1):
+
+        @pl.when(inside(0, -v))
+        def _(v=v):
+            side_copy(v).wait_recv()
+
+    for w in (-1, 1):
+        for v in (-1, 1):
+
+            @pl.when(inside(w, -v))
+            def _(w=w, v=v):
+                for c in range(CHUNKS):
+                    corner_copy(w, v, c).wait_recv()
+
+    local.wait()
+    for u, v in AROUND:
+
+        @pl.when(inside(u, v))
+        def _(u=u, v=v):
+            atom_copy(u, v).wait_send()
+
+    for u in (-1, 1):
+
+        @pl.when(inside(u, 0))
+        def _(u=u):
+            for c in range(CHUNKS):
+                ahead_copy(u, c).wait_send()
+
+    for v in (-1, 1):
+
+        @pl.when(inside(0, v))
+        def _(v=v):
+            side_copy(v).wait_send()
+
+    for w in (-1, 1):
+        for v in (-1, 1):
+
+            @pl.when(inside(w, v))
+            def _(w=w, v=v):
+                for c in range(CHUNKS):
+                    corner_copy(w, v, c).wait_send()
+
+
+def halo(own8, features):
+    vmem = pl.BlockSpec(memory_space=pltpu.VMEM)
+    hbm = pl.BlockSpec(memory_space=pl.ANY)
+    dma = pltpu.SemaphoreType.DMA
+    return pl.pallas_call(
+        halo_body,
+        out_shape=(
+            jax.ShapeDtypeStruct((9 * own8.shape[0],) + own8.shape[1:], own8.dtype),
+            jax.ShapeDtypeStruct((9,) + features.shape, features.dtype),
+        ),
+        in_specs=[vmem, hbm],
+        out_specs=(vmem, hbm),
+        scratch_shapes=[
+            dma((9,)),
+            dma((9,)),
+            dma((2,)),
+            dma((2,)),
+            dma((2, CHUNKS)),
+            dma((2, CHUNKS)),
+            dma((4, CHUNKS)),
+            dma((4, CHUNKS)),
+            dma(()),
+        ],
+        compiler_params=pltpu.CompilerParams(collective_id=2, has_side_effects=True),
+        name="halo",
+    )(own8, features)
 
 
 def body(
@@ -599,14 +820,13 @@
     own_tiles = own_size // TILE
     own8 = jnp.concatenate([positions.reshape(3, -1), charges.reshape(1, -1)], axis=0)
     own8 = jnp.pad(own8, ((0, 4), (0, 0))).reshape(8, own_tiles, TILE).transpose(1, 0, 2)
-    near8 = with_halo(own8[None, None], (("brick", 0), ("sub", 1)), 1).reshape(-1, 8, TILE)
-    near_features = with_halo(atom_features, (("brick", 0), ("sub", 1)), 1)
+    near8, near_features = halo(own8, atom_features.reshape(own_size, -1))
     pair_force, pair_energy = solvent_pairs(
         own8, near8, tile_pairs.reshape(2, -1), tile_count.reshape(1)
     )
     row_force, frag_energy = fragment_model(
         near8,
-        near_features.reshape(-1, F),
+        near_features,
         slot_index,
         atom_count,
         cap_weight,

time: 135 us -> 129 us (0.956)
  Pallas kernels: 77.6 us -> 107 us
  starting transfers between devices: 24 us -> 0 us
  waiting for transfers between devices: 17.8 us -> 0 us
  between operations: 3.21 us -> 8.84 us
  local copies, waits for them, and re-layouts: 7.57 us -> 9.74 us
    pallas_call x0 -> x1, Pallas kernels: none -> 25.3 us  [halo(): pl.pallas_call(halo_body, out_shape=(jax.ShapeDtypeStruct((9 * own8.shape...]
    ppermute x8 -> x0, starting transfers between devices: 24 us -> none  [the longest x4 17.6 us: with_halo(): before = lax.ppermute(last, axis, up)]
    ppermute x8 -> x0, waiting for transfers between devices: 17.8 us -> none  [the longest x4 10.6 us: with_halo(): before = lax.ppermute(last, axis, up)]
    pallas_call x1, Pallas kernels: 24.8 us -> 38 us  [bring_home(): pl.pallas_call(home_body, out_shape=(jax.ShapeDtypeStruct(block, jnp.floa...]
    pallas_call x1, Pallas kernels: 45.7 us -> 37.5 us  [fragment_model(): pl.pallas_call(fragment_body, out_shape=(jax.ShapeDtypeStruct((tiles // 8...]
    concatenate x3 -> x0, other arithmetic: 3.54 us -> none  [with_halo(): x = jnp.concatenate([before, x, after], axis=dim)]
    unnamed x24 -> x12, local copies, waits for them, and re-layouts: 3.64 us -> 5.58 us
    broadcast_in_dim x2 -> x0, local copies, waits for them, and re-layouts: 1.74 us -> none  [fragment_model(): jnp.broadcast_to(cap_weight.reshape(-1, 1), (frags * SLOTS, TILE))]
  transfers between devices with their start and end apart: 8 -> 0, of which waited for: 5 -> 0; matrix products, arithmetic and copies ran while one was open for 3% -> 0% of each run, Pallas kernels for 5% -> 0%
where the time goes in v3:
time: 129 us
  Pallas kernels  107 us (83%)
  local copies, waits for them, and re-layouts  9.74 us (8%)
  between operations  8.84 us (7%)
  other arithmetic  3.7 us (3%)
    pallas_call x1, Pallas kernels, bring_home(): pl.pallas_call(home_body, out_shape=(jax.ShapeDtypeStruct(block, jnp.floa...  38 us
    pallas_call x1, Pallas kernels, fragment_model(): pl.pallas_call(fragment_body, out_shape=(jax.ShapeDtypeStruct((tiles // 8...  37.5 us
    pallas_call x1, Pallas kernels, halo(): pl.pallas_call(halo_body, out_shape=(jax.ShapeDtypeStruct((9 * own8.shape...  25.3 us
    pallas_call x1, Pallas kernels, solvent_pairs(): pl.pallas_call(pair_body, out_shape=(jax.ShapeDtypeStruct((3, tiles, TILE...  5.7 us
    unnamed x12, local copies, waits for them, and re-layouts  5.58 us

profile of v3, /device:TPU:1, one launch (start us, length us, event | category | flops | bytes accessed | tf_op | source)
XLA Modules:
  0.0 128.8 jit_solution(8731032194713962362)
XLA Ops:
  1.3 0.7 broadcast_divide_fusion
  2.0 0.7 and_select_fusion
  2.6 0.2 convert_reduce_fusion
  2.8 0.1 select_reduce_fusion
  2.9 0.8 fusion.5
  9.4 1.3 concatenate.6.order_ref
  10.7 0.1 broadcast_in_dim.23
  10.7 0.7 reshape.49.span_cols_ref
  11.4 0.1 broadcast_in_dim.22
  11.5 0.7 reshape.48.span_ref
  12.1 1.4 %reshape.43.slot_ref = s32[3072]{0:T(1024)} reshape(s32[48,64]{1,0:T(8,128)} %param.17) | data formatting | bytes 24576 | tf_op jit(solution)/shard_map/reshape | solution.py:436
  13.6 0.7 copy.21
  14.3 1.3 %fusion.own_ref = f32[8,8,128]{2,1,0:T(8,128)} fusion(f32[1,1024]{1,0:T(1,128)} %bitcast.24, f32[3,1024]{1,0:T(4,128)S(1)} %bitcast.22), kind=kLoop, calls=%fused_computation.1 | loop fusion | flops 32768 | bytes 49152 | tf_op jit(solution)/shard_map/transpose | solution.py:822
  15.6 25.3 %halo.1 = (f32[72,8,128]{2,1,0:T(8,128)}, bf16[9,1024,256]{2,1,0:T(8,128)(2,1)}) custom-call(f32[8,8,128]{2,1,0:T(8,128)} %fusion.own_ref, bf16[1024,256]{1,0:T(8,128)(2,1)} %bitcast.21), custom_call_target="tpu_custom_call" | custom-call | tf_op jit(solution)/shard_map/halo/pallas_call | solution.py:779
  40.9 0.0 copy-start
  40.9 1.0 copy-done
  41.9 0.0 copy-start.1
  41.9 0.8 copy-done.1
  42.6 0.0 copy-start.4
  42.6 0.7 copy-done.4
  43.3 5.7 %pair_tiles.1 = (f32[3,8,128]{2,1,0:T(8,128)S(1)}, f32[8,128]{1,0:T(8,128)S(1)}) custom-call(s32[2,128]{1,0:T(2,128)S(1)} %bitcast.20, s32[1]{0:T(128)} %bitcast.19.count_ref, f32[8,8,128]{2,1,0:T(8,128)S(1)} %copy-done.1, f32[72,8,128]{2,1,0:T(8,128)S(1)} %copy-done), custom_call_target="tpu_custom_call" | custom-call | tf_op jit(solution)/shard_map/pair_tiles/pallas_call | solution.py:111
  49.0 0.0 copy-start.2
  49.0 0.6 copy-done.2
  49.6 0.0 copy-start.3
  49.6 0.6 copy-done.3
  50.2 37.5 %fragments.1 = (f32[9,3,8,128]{3,2,1,0:T(8,128)}, f32[8,128]{1,0:T(8,128)}) custom-call(s32[53]{0:T(128)} %concatenate.6.order_ref, s32[3072]{0:T(1024)} %reshape.43.slot_ref, f32[72,8,128]{2,1,0:T(8,128)} %get-tuple-element.10.near_ref, bf16[9,1024,256]{2,1,0:T(8,128)(2,1)} %get-tuple-element.11.feat_ref, f32[48,64]{1,0:T(8,128)} %cap_ref.1, ...), custom_call_target="tpu_custom_call" | custom-call | tf_op jit(solution)/shard_map/fragments/pallas_call | solution.py:417
  87.7 38.0 %bring_home.1 = (f32[3,8,128]{2,1,0:T(8,128)}, f32[1,1]{1,0:T(1,128)}) custom-call(f32[9,3,8,128]{3,2,1,0:T(8,128)} %get-tuple-element.12.force_ref, f32[3,8,128]{2,1,0:T(8,128)} %copy-done.2, f32[8,128]{1,0:T(8,128)} %get-tuple-element.14.frag_energy_ref, f32[8,128]{1,0:T(8,128)} %copy-done.3), custom_call_target="tpu_custom_call" | custom-call | tf_op jit(solution)/shard_map/bring_home/pallas_call | solution.py:563
  125.7 1.3 %copy.25 = f32[3,1,1,1024]{3,2,1,0:T(1,128)} copy(f32[3,1,1,1024]{3,2,1,0:T(1,128)} %bitcast.23) | data formatting | bytes 24576
Async XLA Ops:
  40.9 1.0 copy-start
  41.9 0.8 copy-start.1
  42.6 0.7 copy-start.4
  49.0 0.6 copy-start.2
  49.6 0.6 copy-start.3

commit v4 on v3

--- a/solution.py
+++ b/solution.py
@@ -53,78 +53,6 @@
     return pl.reciprocal(x, approx=True)
 
 
-def pair_body(pairs_ref, count_ref, own_ref, near_ref, force_ref, energy_ref, own_cols, total):
-    own_tiles = own_ref.shape[0]
-    total[...] = jnp.zeros_like(total)
-    energy_ref[...] = jnp.zeros_like(energy_ref)
-    for t in range(own_tiles):
-        cols = jnp.transpose(own_ref[t])
-        for c in range(4):
-            own_cols[t, c] = jnp.broadcast_to(cols[:, c : c + 1], (TILE, TILE))
-    chunk = 32
-    lane = lax.broadcasted_iota(jnp.int32, (chunk, TILE), 1)
-    row = lax.broadcasted_iota(jnp.int32, (chunk, TILE), 0)
-    rel = lane - row
-
-    def one_pair(p, carry):
-        own = pairs_ref[0, p]
-        near = pairs_ref[1, p]
-        n = near_ref[near]
-        xj, yj, zj, qj = (n[c : c + 1, :] for c in range(4))
-        same = jnp.where(near - 4 * own_tiles == own, 0, 4 * TILE)
-        en = jnp.zeros((8, TILE), jnp.float32)
-        for start in range(0, TILE, chunk):
-            at = pl.ds(start, chunk)
-            dx = own_cols[own, 0, at, :] - xj
-            dy = own_cols[own, 1, at, :] - yj
-            dz = own_cols[own, 2, at, :] - zj
-            qq = jnp.where(rel == same + start, 0.0, own_cols[own, 3, at, :] * qj)
-            s = dx * dx + dy * dy + dz * dz + CHARGE_SOFTEN
-            s = jnp.minimum(s, 1e6)
-            rinv = lax.rsqrt(s)
-            t = recip(1.0 + (ERFC_P * SCREEN_RATE) * (s * rinv))
-            g = ERFC_C[-1]
-            for coef in ERFC_C[-2::-1]:
-                g = g * t + coef
-            gauss = qq * jnp.exp2((-SCREEN_RATE * SCREEN_RATE * math.log2(math.e)) * s)
-            screened = (g * t) * rinv
-            en += jnp.sum((gauss * screened).reshape(chunk // 8, 8, TILE), axis=0)
-            w = (gauss * (screened + GAUSS)) * (rinv * rinv)
-            total[own, 0, at, :] += w * dx
-            total[own, 1, at, :] += w * dy
-            total[own, 2, at, :] += w * dz
-        energy_ref[...] += en
-        return carry
-
-    lax.fori_loop(0, count_ref[0], one_pair, 0)
-    for t in range(own_tiles):
-        for c in range(3):
-            force_ref[c, t : t + 1, :] = jnp.sum(
-                jnp.transpose(total[t, c]), axis=0, keepdims=True
-            )
-
-
-def solvent_pairs(own8, near8, pairs, count):
-    tiles = own8.shape[0]
-    smem = pl.BlockSpec(memory_space=pltpu.SMEM)
-    vmem = pl.BlockSpec(memory_space=pltpu.VMEM)
-    return pl.pallas_call(
-        pair_body,
-        out_shape=(
-            jax.ShapeDtypeStruct((3, tiles, TILE), jnp.float32),
-            jax.ShapeDtypeStruct((8, TILE), jnp.float32),
-        ),
-        in_specs=[smem, smem, vmem, vmem],
-        out_specs=(vmem, vmem),
-        scratch_shapes=[
-            pltpu.VMEM((tiles, 4, TILE, TILE), jnp.float32),
-            pltpu.VMEM((tiles, 3, TILE, TILE), jnp.float32),
-        ],
-        compiler_params=pltpu.CompilerParams(vmem_limit_bytes=16 * MIB),
-        name="pair_tiles",
-    )(pairs, count, own8, near8)
-
-
 def norm_parts(hidden):
     centre = jnp.mean(hidden, axis=-1, keepdims=True)
     shifted = hidden - centre
@@ -145,16 +73,15 @@
 
 
 def fragment_body(
-    order_ref,
+    count_ref,
     slot_ref,
+    rate_ref,
     near_ref,
     feat_ref,
     cap_ref,
     wqkv_ref,
     wout_ref,
     gains_ref,
-    span_ref,
-    span_cols_ref,
     wread_ref,
     wen_ref,
     force_ref,
@@ -163,6 +90,9 @@
     slots,
     slot_force,
     caps,
+    span_ref,
+    span_cols_ref,
+    order_ref,
     bins,
 ):
     tiles = near_ref.shape[0]
@@ -182,18 +112,39 @@
 
     lax.fori_loop(0, tiles // 8, widen, 0)
     slot_force[...] = jnp.zeros_like(slot_force)
+    head = lax.broadcasted_iota(jnp.int32, (1, HEADS * SLOTS), 1) // SLOTS
+    head_col = lax.broadcasted_iota(jnp.int32, (1, F), 1) // (F // HEADS)
+    for layer in range(LAYERS):
+        wide = jnp.ones((1, HEADS * SLOTS), jnp.float32)
+        cols = jnp.ones((1, F), jnp.float32)
+        for h in range(HEADS):
+            wide = jnp.where(head == h, rate_ref[layer, h], wide)
+            cols = jnp.where(head_col == h, rate_ref[layer, h], cols)
+        span_ref[layer : layer + 1, :] = 1.0 / wide
+        span_cols_ref[layer : layer + 1, :] = 1.0 / cols
     slots[0, :TILE, :] = jnp.zeros((TILE, TILE), jnp.float32)
     slots[0, :frags, :SLOTS] = cap_ref[...]
     cols = jnp.transpose(slots[0, :TILE, :])
     for f in range(frags):
-        caps[f * SLOTS : (f + 1) * SLOTS, :] = jnp.broadcast_to(
+        caps[f] = jnp.broadcast_to(
             cols[:SLOTS, f : f + 1], (SLOTS, TILE)
         )
     energy_ref[...] = jnp.zeros_like(energy_ref)
 
+    ends = {9: 0}
+    made = 0
+    for size in range(8, 1, -1):
+        for k in range(frags):
+            live = count_ref[k]
+            order_ref[made] = live * 64 + k
+            made += jnp.where((live + 7) >> 3 == size, 1, 0)
+        ends[size] = made
+    n6, n5, n3, n2 = (ends[k] - ends[k + 1] for k in (6, 5, 3, 2))
+    with6 = jnp.minimum(n6, n2)
+    with5 = jnp.minimum(n5, n2 - with6 + n3)
+    runs = [ends[7], ends[7] + with6, ends[6], ends[6] + with5, ends[5]]
     high = frags - 1
     made = 0
-    runs = [order_ref[frags + k] for k in range(5)]
     for k in range(frags):
         fits = (
             ((k >= runs[0]) & (k < runs[1]))
@@ -242,18 +193,17 @@
         info = []
         for f in range(GROUP):
             big, small, first, start, second = (bins[c, b * GROUP + f] for c in range(5))
-            bases = [
-                pl.multiple_of(
-                    jnp.where(k * 8 < start, big * SLOTS, small * SLOTS - start) + k * 8, 8
-                )
-                for k in range(SLOTS // 8)
-            ]
+            bases = []
+            for k in range(SLOTS // 8):
+                early = k * 8 < start
+                at = pl.multiple_of(k * 8 - jnp.where(early, 0, start), 8)
+                bases.append((jnp.where(early, big, small), at))
             info.append((first, start, second, bases))
 
         for f in range(GROUP):
-            for k, base in enumerate(info[f][3]):
+            for k, (frag, first) in enumerate(info[f][3]):
                 for j in range(8):
-                    r = slot_ref[base + j]
+                    r = slot_ref[frag, first + j]
                     at = f * SLOTS + k * 8 + j
                     for c in range(3):
                         slots[c, at : at + 1, :] = table[c, pl.ds(r, 1), :]
@@ -277,7 +227,7 @@
             dists.append(jnp.where(mine == owner(slot_lane, -1), square * inverse, FAR))
             inverses.append(inverse)
             offsets.append(off)
-            cap = jnp.concatenate([caps[pl.ds(base, 8), :] for base in bases], axis=0)
+            cap = jnp.concatenate([caps[frag, pl.ds(at, 8), :] for frag, at in bases], axis=0)
             weights.append(jnp.where(mine > 0, cap, 0.0))
         dist2 = [jnp.concatenate([d, d], axis=1) for d in dists]
         weight = jnp.concatenate(weights, axis=0)
@@ -375,8 +325,8 @@
         slot_force[:, 8:16] = jnp.transpose(packed)
 
         for f in range(GROUP):
-            for k, base in enumerate(info[f][3]):
-                rs = [slot_ref[base + j] for j in range(8)]
+            for k, (frag, first) in enumerate(info[f][3]):
+                rs = [slot_ref[frag, first + j] for j in range(8)]
                 old = [table[2, pl.ds(r, 1), :] for r in rs]
                 for j in range(8):
                     at = f * SLOTS + k * 8 + j
@@ -402,46 +352,36 @@
     frags = atom_count.shape[0]
     smem = pl.BlockSpec(memory_space=pltpu.SMEM)
     vmem = pl.BlockSpec(memory_space=pltpu.VMEM)
-    ids = jnp.arange(frags, dtype=jnp.int32)
-    key = atom_count * 64 + ids
-    place = jnp.sum(key[None, :] > key[:, None], axis=1)
-    order = jnp.sum(jnp.where(place[None, :] == ids[:, None], key[None, :], 0), axis=1)
-    eighths = (atom_count + 7) // 8
-    alone = jnp.sum((eighths >= 7).astype(jnp.int32))
-    n6, n5, n3, n2 = (jnp.sum((eighths == k).astype(jnp.int32)) for k in (6, 5, 3, 2))
-    with6 = jnp.minimum(n6, n2)
-    with5 = jnp.minimum(n5, n2 - with6 + n3)
-    runs = [alone, alone + with6, alone + n6, alone + n6 + with5, alone + n6 + n5]
-    order = jnp.concatenate([order, jnp.stack(runs)])
-    spans = 1.0 / rates
     force, energy = pl.pallas_call(
         fragment_body,
         out_shape=(
             jax.ShapeDtypeStruct((tiles // 8, 3, 8, TILE), jnp.float32),
             jax.ShapeDtypeStruct((8, TILE), jnp.float32),
         ),
-        in_specs=[smem, smem] + [vmem] * 10,
+        in_specs=[smem, smem, smem] + [vmem] * 8,
         out_specs=(vmem, vmem),
         scratch_shapes=[
             pltpu.VMEM((3, tiles * TILE, TILE), jnp.float32),
             pltpu.VMEM((3, ROWS, TILE), jnp.float32),
             pltpu.VMEM((ROWS, TILE), jnp.float32),
-            pltpu.VMEM((frags * SLOTS, TILE), jnp.float32),
+            pltpu.VMEM((frags, SLOTS, TILE), jnp.float32),
+            pltpu.VMEM((LAYERS, HEADS * SLOTS), jnp.float32),
+            pltpu.VMEM((LAYERS, F), jnp.float32),
+            pltpu.SMEM((frags + 1,), jnp.int32),
             pltpu.SMEM((5, frags + GROUP + 1), jnp.int32),
         ],
         compiler_params=pltpu.CompilerParams(vmem_limit_bytes=56 * MIB),
         name="fragments",
     )(
-        order,
-        slot_index.reshape(-1),
+        atom_count,
+        slot_index,
+        rates,
         near8,
         near_features,
         cap_weight,
         w_qkv,
         w_out,
         gains,
-        jnp.repeat(spans, SLOTS, axis=1),
-        jnp.repeat(spans, F // HEADS, axis=1),
         w_read,
         w_energy.reshape(1, -1),
     )
@@ -505,7 +445,7 @@
             device_id_type=mesh_id,
         )
 
-    by_sub[sub] = frag_energy_ref[...] + (0.5 * COULOMB_UNIT) * pair_energy_ref[...]
+    by_sub[sub] = frag_energy_ref[...] + pair_energy_ref[...]
     for k, peer in enumerate(sub_peers):
         energy_copy(by_sub, sub_send, sub_recv, k, sub, peer).start()
 
@@ -532,7 +472,7 @@
     for k, peer in enumerate(brick_peers):
         energy_copy(by_brick, brick_send, brick_recv, k, brick, peer).start()
 
-    out_ref[...] = force_ref[4] + COULOMB_UNIT * pair_ref[...]
+    out_ref[...] = force_ref[4] + pair_ref[...]
     for u, v in around:
         @pl.when(inside(-u, -v))
         def _(u=u, v=v):
@@ -579,7 +519,9 @@
             dma((bricks,)),
             dma((bricks,)),
         ],
-        compiler_params=pltpu.CompilerParams(collective_id=1, has_side_effects=True),
+        compiler_params=pltpu.CompilerParams(
+            collective_id=1, has_side_effects=True, vmem_limit_bytes=56 * MIB
+        ),
         name="bring_home",
     )(row_force, pair_force, frag_energy, pair_energy)
 
@@ -588,15 +530,31 @@
 CHUNKS = 4
 
 
+STEP_PAIRS = 16
+
+
+def three_parts(x):
+    a = bf16(x).astype(jnp.float32)
+    b = bf16(x - a).astype(jnp.float32)
+    return [a, b, x - a - b, jnp.zeros_like(x)]
+
+
 def block_of(u, v):
     return (u + 1) * 3 + v + 1
 
 
 def halo_body(
-    own_ref,
+    pairs_ref,
+    count_ref,
+    pos_ref,
+    charge_ref,
+    own_list_ref,
     feat_ref,
     near_ref,
     near_feat_ref,
+    pair_force_ref,
+    pair_energy_ref,
+    parts,
     atom_send,
     atom_recv,
     side_send,
@@ -611,8 +569,15 @@
     brick, sub = lax.axis_index("brick"), lax.axis_index("sub")
     mesh_id = pl.DeviceIdType.MESH
     rows = feat_ref.shape[0]
-    tiles = own_ref.shape[0]
+    tiles = charge_ref.shape[0]
     part = rows // CHUNKS
+    centre = block_of(0, 0) * tiles
+
+    near_ref[pl.ds(centre, tiles)] = jnp.zeros((tiles, 8, TILE), jnp.float32)
+    for t in range(tiles):
+        for c in range(3):
+            near_ref[centre + t, c : c + 1, :] = pos_ref[c, t : t + 1, :]
+        near_ref[centre + t, 3:4, :] = charge_ref[t : t + 1, :]
 
     def inside(u, v):
         b, s = brick + u, sub + v
@@ -636,7 +601,7 @@
     def atom_copy(u, v):
         k = block_of(-u, -v)
         return pltpu.make_async_remote_copy(
-            src_ref=own_ref,
+            src_ref=near_ref.at[pl.ds(centre, tiles)],
             dst_ref=near_ref.at[pl.ds(k * tiles, tiles)],
             send_sem=atom_send.at[k],
             recv_sem=atom_recv.at[k],
@@ -700,13 +665,12 @@
 
     local = pltpu.make_async_copy(feat_ref, near_feat_ref.at[block_of(0, 0)], local_sem)
     local.start()
-    near_ref[pl.ds(block_of(0, 0) * tiles, tiles)] = own_ref[...]
     for u, v in AROUND:
         k = block_of(u, v)
 
         @pl.when(jnp.logical_not(inside(u, v)))
         def _(k=k):
-            near_ref[pl.ds(k * tiles, tiles)] = jnp.zeros_like(own_ref)
+            near_ref[pl.ds(k * tiles, tiles)] = jnp.zeros((tiles, 8, TILE), jnp.float32)
 
     def forward(c):
         for w in (-1, 1):
@@ -720,14 +684,69 @@
                     def _(w=w, v=v):
                         corner_copy(w, v, c).start()
 
-    for c in range(CHUNKS):
-        forward(c)
-
     for u, v in AROUND:
 
         @pl.when(inside(-u, -v))
         def _(u=u, v=v):
             atom_copy(u, v).wait_recv()
+
+    spread = (
+        lax.broadcasted_iota(jnp.int32, (32, 4 * TILE), 0) % 8
+        == lax.broadcasted_iota(jnp.int32, (32, 4 * TILE), 1) // TILE
+    ).astype(jnp.bfloat16)
+    chunk = 32
+    rel = lax.broadcasted_iota(jnp.int32, (chunk, TILE), 1) - lax.broadcasted_iota(
+        jnp.int32, (chunk, TILE), 0
+    )
+
+    def one_pair(p, carry):
+        own = pairs_ref[0, p]
+        near = pairs_ref[1, p]
+        o = near_ref[centre + own]
+        xi, yi, zi, qi = (o[c : c + 1, :] for c in range(4))
+        cols = dot_tn(bf16(jnp.concatenate(three_parts(near_ref[near]), axis=0)), spread)
+        same = jnp.where(near == own + centre, 0, 4 * TILE)
+        sums = [jnp.zeros((8, TILE), jnp.float32) for _ in range(4)]
+        for start in range(0, TILE, chunk):
+            xj, yj, zj, qj = (
+                cols[start : start + chunk, c * TILE : (c + 1) * TILE] for c in range(4)
+            )
+            dx, dy, dz = xi - xj, yi - yj, zi - zj
+            qq = jnp.where(rel == same + start, 0.0, qi * qj)
+            square = dx * dx + dy * dy + dz * dz + CHARGE_SOFTEN
+            square = jnp.minimum(square, 1e6)
+            rinv = lax.rsqrt(square)
+            t = recip(1.0 + (ERFC_P * SCREEN_RATE) * (square * rinv))
+            g = ERFC_C[-1]
+            for coef in ERFC_C[-2::-1]:
+                g = g * t + coef
+            gauss = qq * jnp.exp2((-SCREEN_RATE * SCREEN_RATE * math.log2(math.e)) * square)
+            screened = (g * t) * rinv
+            w = (gauss * (screened + GAUSS)) * (rinv * rinv)
+            for k, term in enumerate((w * dx, w * dy, w * dz, gauss * screened)):
+                sums[k] += jnp.sum(term.reshape(chunk // 8, 8, TILE), axis=0)
+        for k in range(4):
+            parts[k, pl.ds(p, 1), :] = jnp.sum(sums[k], axis=0, keepdims=True)
+        return carry
+
+    pairs = own_list_ref.shape[1]
+    done = 0
+    for c in range(CHUNKS):
+        forward(c)
+        upto = (c + 1) * STEP_PAIRS if c < CHUNKS - 1 else pairs
+        lax.fori_loop(done, upto, one_pair, 0)
+        done = upto
+
+    pick = (
+        (own_list_ref[0:1, :] == lax.broadcasted_iota(jnp.int32, (16, pairs), 0))
+        & (lax.broadcasted_iota(jnp.int32, (16, pairs), 1) < count_ref[0, 0])
+    ).astype(jnp.bfloat16)
+    for k in range(4):
+        whole = sum(dot(pick, bf16(x)) for x in three_parts(parts[k])[:3])[:tiles]
+        if k < 3:
+            pair_force_ref[k] = COULOMB_UNIT * whole
+        else:
+            pair_energy_ref[...] = (0.5 * COULOMB_UNIT) * whole
 
     for v in (-1, 1):
 
@@ -772,19 +791,24 @@
                     corner_copy(w, v, c).wait_send()
 
 
-def halo(own8, features):
+def halo(positions, charges, features, pairs, count):
+    tiles = charges.shape[0]
+    smem = pl.BlockSpec(memory_space=pltpu.SMEM)
     vmem = pl.BlockSpec(memory_space=pltpu.VMEM)
     hbm = pl.BlockSpec(memory_space=pl.ANY)
     dma = pltpu.SemaphoreType.DMA
     return pl.pallas_call(
         halo_body,
         out_shape=(
-            jax.ShapeDtypeStruct((9 * own8.shape[0],) + own8.shape[1:], own8.dtype),
+            jax.ShapeDtypeStruct((9 * tiles, 8, TILE), jnp.float32),
             jax.ShapeDtypeStruct((9,) + features.shape, features.dtype),
+            jax.ShapeDtypeStruct((3, tiles, TILE), jnp.float32),
+            jax.ShapeDtypeStruct((tiles, TILE), jnp.float32),
         ),
-        in_specs=[vmem, hbm],
-        out_specs=(vmem, hbm),
+        in_specs=[smem, smem, vmem, vmem, vmem, hbm],
+        out_specs=(vmem, hbm, vmem, vmem),
         scratch_shapes=[
+            pltpu.VMEM((4, pairs.shape[1], TILE), jnp.float32),
             dma((9,)),
             dma((9,)),
             dma((2,)),
@@ -795,9 +819,11 @@
             dma((4, CHUNKS)),
             dma(()),
         ],
-        compiler_params=pltpu.CompilerParams(collective_id=2, has_side_effects=True),
+        compiler_params=pltpu.CompilerParams(
+            collective_id=2, has_side_effects=True, vmem_limit_bytes=56 * MIB
+        ),
         name="halo",
-    )(own8, features)
+    )(pairs, count, positions, charges, pairs, features)
 
 
 def body(
@@ -818,11 +844,12 @@
 ):
     own_size = atom_features.shape[2]
     own_tiles = own_size // TILE
-    own8 = jnp.concatenate([positions.reshape(3, -1), charges.reshape(1, -1)], axis=0)
-    own8 = jnp.pad(own8, ((0, 4), (0, 0))).reshape(8, own_tiles, TILE).transpose(1, 0, 2)
-    near8, near_features = halo(own8, atom_features.reshape(own_size, -1))
-    pair_force, pair_energy = solvent_pairs(
-        own8, near8, tile_pairs.reshape(2, -1), tile_count.reshape(1)
+    near8, near_features, pair_force, pair_energy = halo(
+        positions.reshape(3, own_tiles, TILE),
+        charges.reshape(own_tiles, TILE),
+        atom_features.reshape(own_size, -1),
+        tile_pairs.reshape(2, -1),
+        tile_count,
     )
     row_force, frag_energy = fragment_model(
         near8,

time: 129 us -> 125 us (0.969)
  Pallas kernels: 107 us -> 121 us
  local copies, waits for them, and re-layouts: 9.74 us -> 1.31 us
  between operations: 8.84 us -> 3.03 us
  other arithmetic: 3.7 us -> 0 us
    pallas_call x2 -> x1, Pallas kernels: 31 us -> 54.2 us  [halo(): pl.pallas_call(halo_body, out_shape=(jax.ShapeDtypeStruct((9 * tiles, 8,...]
    pallas_call x1, Pallas kernels: 38 us -> 25 us  [bring_home(): pl.pallas_call(home_body, out_shape=(jax.ShapeDtypeStruct(block, jnp.floa...]
    unnamed x12 -> x1, local copies, waits for them, and re-layouts: 5.58 us -> 1.31 us
    pallas_call x1, Pallas kernels: 37.5 us -> 41.5 us  [fragment_model(): pl.pallas_call(fragment_body, out_shape=(jax.ShapeDtypeStruct((tiles // 8...]
    reshape x3 -> x0, local copies, waits for them, and re-layouts: 2.74 us -> none  [the longest x1 1.41 us: fragment_model(): slot_index.reshape(-1)]
    transpose x1 -> x0, other arithmetic: 1.3 us -> none  [body(): jnp.pad(own8, ((0, 4), (0, 0))).reshape(8, own_tiles, TILE)]
where the time goes in v4:
time: 125 us
  Pallas kernels  121 us (97%)
  between operations  3.03 us (2%)
  local copies, waits for them, and re-layouts  1.31 us (1%)
    pallas_call x1, Pallas kernels, halo(): pl.pallas_call(halo_body, out_shape=(jax.ShapeDtypeStruct((9 * tiles, 8,...  54.2 us
    pallas_call x1, Pallas kernels, fragment_model(): pl.pallas_call(fragment_body, out_shape=(jax.ShapeDtypeStruct((tiles // 8...  41.5 us
    pallas_call x1, Pallas kernels, bring_home(): pl.pallas_call(home_body, out_shape=(jax.ShapeDtypeStruct(block, jnp.floa...  25 us

profile of v4, /device:TPU:1, one launch (start us, length us, event | category | flops | bytes accessed | tf_op | source)
XLA Modules:
  0.0 125.0 jit_solution(7828942105161463425)
XLA Ops:
  1.3 54.2 %halo.1 = (f32[72,8,128]{2,1,0:T(8,128)}, bf16[9,1024,256]{2,1,0:T(8,128)(2,1)}, f32[3,8,128]{2,1,0:T(8,128)}, f32[8,128]{1,0:T(8,128)}) custom-call(s32[2,128]{1,0:T(2,128)} %bitcast.11, s32[1,1]{1,0:T(1,128)S(6)} %copy.20.count_ref, f32[3,8,128]{2,1,0:T(8,128)} %bitcast.9, f32[8,128]{1,0:T(8,128)} %bitcast.10, s32[2,128]{1,0:T(2,128)} %bitcast.12, ...), custom_call_target="tpu_custom_call" | custom-call | tf_op jit(solution)/shard_map/halo/pallas_call | solution.py:800
  55.5 41.5 %fragments.1 = (f32[9,3,8,128]{3,2,1,0:T(8,128)}, f32[8,128]{1,0:T(8,128)}) custom-call(s32[48]{0:T(128)} %count_ref.2, s32[48,64]{1,0:T(8,128)} %slot_ref.1, f32[2,8]{1,0:T(2,128)} %rate_ref.1, f32[72,8,128]{2,1,0:T(8,128)} %get-tuple-element.10.near_ref, bf16[9,1024,256]{2,1,0:T(8,128)(2,1)} %get-tuple-element.11.feat_ref, f32[48,64]{1,0:T(8,128)} %cap_ref.1, ...), custom_call_target="tpu_custom_call" | custom-call | tf_op jit(solution)/shard_map/fragments/pallas_call | solution.py:355
  97.0 25.0 %bring_home.1 = (f32[3,8,128]{2,1,0:T(8,128)}, f32[1,1]{1,0:T(1,128)}) custom-call(f32[9,3,8,128]{3,2,1,0:T(8,128)} %get-tuple-element.12.force_ref, f32[3,8,128]{2,1,0:T(8,128)} %get-tuple-element.13.pair_ref, f32[8,128]{1,0:T(8,128)} %get-tuple-element.14.frag_energy_ref, f32[8,128]{1,0:T(8,128)} %get-tuple-element.15.pair_energy_ref), custom_call_target="tpu_custom_call" | custom-call | tf_op jit(solution)/shard_map/bring_home/pallas_call | solution.py:503
  121.9 1.3 %copy.21 = f32[3,1,1,1024]{3,2,1,0:T(1,128)} copy(f32[3,1,1,1024]{3,2,1,0:T(1,128)} %bitcast.8) | data formatting | bytes 24576

commit v5 on v4

--- a/solution.py
+++ b/solution.py
@@ -87,6 +87,7 @@
     force_ref,
     energy_ref,
     table,
+    forces,
     slots,
     slot_force,
     caps,
@@ -108,6 +109,7 @@
             table[2, pl.ds(at, TILE), :] = jnp.concatenate(
                 [n, jnp.zeros((TILE, TILE - 8), jnp.float32)], axis=1
             )
+            forces[pl.ds(at, TILE), :] = jnp.zeros((TILE, TILE), jnp.float32)
         return carry
 
     lax.fori_loop(0, tiles // 8, widen, 0)
@@ -126,9 +128,9 @@
     slots[0, :frags, :SLOTS] = cap_ref[...]
     cols = jnp.transpose(slots[0, :TILE, :])
     for f in range(frags):
-        caps[f] = jnp.broadcast_to(
-            cols[:SLOTS, f : f + 1], (SLOTS, TILE)
-        )
+        wide = jnp.broadcast_to(cols[:SLOTS, f : f + 1], (SLOTS, TILE))
+        for k in range(SLOTS // 8):
+            caps[k, f] = wide[k * 8 : (k + 1) * 8]
     energy_ref[...] = jnp.zeros_like(energy_ref)
 
     ends = {9: 0}
@@ -161,7 +163,7 @@
         bins[4, k] = jnp.where(both, small >> 6, 0)
         made = jnp.where(k <= high, k + 1, made)
         high = high - jnp.where(both, 1, 0)
-    for k in range(GROUP - 1):
+    for k in range(2 * GROUP - 1):
         bins[0, made + k] = 0
         bins[1, made + k] = 0
         bins[2, made + k] = 0
@@ -189,30 +191,43 @@
     def rows_of(f):
         return slice(f * SLOTS, (f + 1) * SLOTS)
 
+    def eighths(which):
+        big, small, start = (bins[c, which] for c in (0, 1, 3))
+        start = start >> 3
+        for k in range(SLOTS // 8):
+            early = k < start
+            yield k, jnp.where(early, big, small), k - jnp.where(early, 0, start)
+
+    def gather(b):
+        for f in range(GROUP):
+            for k, frag, part in eighths(b * GROUP + f):
+                rs = [slot_ref[part, frag, j] for j in range(8)]
+                at = f * SLOTS + k * 8
+                for j in range(8):
+                    for c in range(3):
+                        slots[c, at + j : at + j + 1, :] = table[c, pl.ds(rs[j], 1), :]
+
+    def scatter(b):
+        for f in range(GROUP):
+            for k, frag, part in eighths(b * GROUP + f):
+                rs = [slot_ref[part, frag, j] for j in range(8)]
+                old = [forces[pl.ds(r, 1), :] for r in rs]
+                for j in range(8):
+                    at = f * SLOTS + k * 8 + j
+                    forces[pl.ds(rs[j], 1), :] = old[j] + slot_force[at : at + 1, :]
+
     def one_block(b, carry):
-        info = []
-        for f in range(GROUP):
-            big, small, first, start, second = (bins[c, b * GROUP + f] for c in range(5))
-            bases = []
-            for k in range(SLOTS // 8):
-                early = k * 8 < start
-                at = pl.multiple_of(k * 8 - jnp.where(early, 0, start), 8)
-                bases.append((jnp.where(early, big, small), at))
-            info.append((first, start, second, bases))
-
-        for f in range(GROUP):
-            for k, (frag, first) in enumerate(info[f][3]):
-                for j in range(8):
-                    r = slot_ref[frag, first + j]
-                    at = f * SLOTS + k * 8 + j
-                    for c in range(3):
-                        slots[c, at : at + 1, :] = table[c, pl.ds(r, 1), :]
-
-        atom_rows = jnp.transpose(slots[2])
+        info = [tuple(bins[c, b * GROUP + f] for c in (2, 3, 4)) for f in range(GROUP)]
+        h0 = jnp.concatenate([slots[0], slots[1]], axis=1)
+        atoms = slots[2]
+        gather(b + 1)
+        scatter(jnp.maximum(b - 1, 0))
+
+        atom_rows = jnp.transpose(atoms)
         dists, inverses, offsets, weights = [], [], [], []
         for f in range(GROUP):
-            first, start, second, bases = info[f]
-            col = slots[2, rows_of(f), :]
+            first, start, second = info[f]
+            col = atoms[rows_of(f), :]
             row = atom_rows[0:8, rows_of(f)]
             row = jnp.concatenate([row, row], axis=1)
             off = [col[:, c : c + 1] - row[c : c + 1, :] for c in range(3)]
@@ -227,7 +242,7 @@
             dists.append(jnp.where(mine == owner(slot_lane, -1), square * inverse, FAR))
             inverses.append(inverse)
             offsets.append(off)
-            cap = jnp.concatenate([caps[frag, pl.ds(at, 8), :] for frag, at in bases], axis=0)
+            cap = jnp.concatenate([caps[part, frag] for _, frag, part in eighths(b * GROUP + f)], axis=0)
             weights.append(jnp.where(mine > 0, cap, 0.0))
         dist2 = [jnp.concatenate([d, d], axis=1) for d in dists]
         weight = jnp.concatenate(weights, axis=0)
@@ -261,7 +276,6 @@
             return bf16(message * span_cols), (qs, kbs, vbs, atts, by_dist, by_score)
 
         gain = [gains_ref[i : i + 1, :] for i in range(LAYERS + 1)]
-        h0 = jnp.concatenate([slots[0], slots[1]], axis=1)
         unit0, _ = norm_parts(h0)
         project0 = bf16(dot(bf16(unit0 * gain[0]), wqkv_ref[0]))
         message0, kept0 = attention(0, project0)
@@ -322,31 +336,26 @@
             + [jnp.zeros((5, ROWS), jnp.float32)],
             axis=0,
         )
-        slot_force[:, 8:16] = jnp.transpose(packed)
-
-        for f in range(GROUP):
-            for k, (frag, first) in enumerate(info[f][3]):
-                rs = [slot_ref[frag, first + j] for j in range(8)]
-                old = [table[2, pl.ds(r, 1), :] for r in rs]
-                for j in range(8):
-                    at = f * SLOTS + k * 8 + j
-                    table[2, pl.ds(rs[j], 1), :] = old[j] + slot_force[at : at + 1, :]
+        slot_force[:, 0:8] = jnp.transpose(packed)
         return carry
 
-    lax.fori_loop(0, (made + GROUP - 1) // GROUP, one_block, 0)
+    gather(0)
+    groups = (made + GROUP - 1) // GROUP
+    lax.fori_loop(0, groups, one_block, 0)
+    scatter(groups - 1)
 
     pick = (
-        lax.broadcasted_iota(jnp.int32, (16, TILE), 0) + 8
+        lax.broadcasted_iota(jnp.int32, (16, TILE), 0)
         == lax.broadcasted_iota(jnp.int32, (16, TILE), 1)
     ).astype(jnp.bfloat16)
     for i in range(tiles // 8):
-        rows = dot_nt(pick, bf16(table[2, i * 1024 : (i + 1) * 1024, :]))
+        rows = dot_nt(pick, bf16(forces[i * 1024 : (i + 1) * 1024, :]))
         for c in range(3):
             for k in range(8):
                 force_ref[i, c, k : k + 1, :] = rows[c : c + 1, k * TILE : (k + 1) * TILE]
 
 
-def fragment_model(near8, near_features, slot_index, atom_count, cap_weight, weights):
+def fragment_model(near8, near_features, slot_rows, atom_count, cap_weight, weights):
     w_qkv, w_out, gains, rates, w_read, w_energy = weights
     tiles = near8.shape[0]
     frags = atom_count.shape[0]
@@ -362,19 +371,20 @@
         out_specs=(vmem, vmem),
         scratch_shapes=[
             pltpu.VMEM((3, tiles * TILE, TILE), jnp.float32),
+            pltpu.VMEM((tiles * TILE, TILE), jnp.float32),
             pltpu.VMEM((3, ROWS, TILE), jnp.float32),
             pltpu.VMEM((ROWS, TILE), jnp.float32),
-            pltpu.VMEM((frags, SLOTS, TILE), jnp.float32),
+            pltpu.VMEM((SLOTS // 8, frags, 8, TILE), jnp.float32),
             pltpu.VMEM((LAYERS, HEADS * SLOTS), jnp.float32),
             pltpu.VMEM((LAYERS, F), jnp.float32),
             pltpu.SMEM((frags + 1,), jnp.int32),
-            pltpu.SMEM((5, frags + GROUP + 1), jnp.int32),
+            pltpu.SMEM((5, frags + 2 * GROUP), jnp.int32),
         ],
         compiler_params=pltpu.CompilerParams(vmem_limit_bytes=56 * MIB),
         name="fragments",
     )(
         atom_count,
-        slot_index,
+        slot_rows,
         rates,
         near8,
         near_features,
@@ -549,12 +559,16 @@
     pos_ref,
     charge_ref,
     own_list_ref,
+    slot_ref,
     feat_ref,
     near_ref,
     near_feat_ref,
     pair_force_ref,
     pair_energy_ref,
+    rows_ref,
     parts,
+    cols_a,
+    cols_b,
     atom_send,
     atom_recv,
     side_send,
@@ -573,6 +587,8 @@
     part = rows // CHUNKS
     centre = block_of(0, 0) * tiles
 
+    for k in range(SLOTS // 8):
+        rows_ref[k] = slot_ref[:, k * 8 : (k + 1) * 8]
     near_ref[pl.ds(centre, tiles)] = jnp.zeros((tiles, 8, TILE), jnp.float32)
     for t in range(tiles):
         for c in range(3):
@@ -699,17 +715,21 @@
         jnp.int32, (chunk, TILE), 0
     )
 
-    def one_pair(p, carry):
+    def spread_near(cols, first):
+        for k in range(4):
+            near = pairs_ref[1, jnp.minimum(first + k, pairs - 1)]
+            cols[k] = dot_tn(bf16(jnp.concatenate(three_parts(near_ref[near]), axis=0)), spread)
+
+    def one_pair(p, cols, k):
         own = pairs_ref[0, p]
         near = pairs_ref[1, p]
         o = near_ref[centre + own]
         xi, yi, zi, qi = (o[c : c + 1, :] for c in range(4))
-        cols = dot_tn(bf16(jnp.concatenate(three_parts(near_ref[near]), axis=0)), spread)
         same = jnp.where(near == own + centre, 0, 4 * TILE)
         sums = [jnp.zeros((8, TILE), jnp.float32) for _ in range(4)]
         for start in range(0, TILE, chunk):
             xj, yj, zj, qj = (
-                cols[start : start + chunk, c * TILE : (c + 1) * TILE] for c in range(4)
+                cols[k, start : start + chunk, c * TILE : (c + 1) * TILE] for c in range(4)
             )
             dx, dy, dz = xi - xj, yi - yj, zi - zj
             qq = jnp.where(rel == same + start, 0.0, qi * qj)
@@ -723,18 +743,28 @@
             gauss = qq * jnp.exp2((-SCREEN_RATE * SCREEN_RATE * math.log2(math.e)) * square)
             screened = (g * t) * rinv
             w = (gauss * (screened + GAUSS)) * (rinv * rinv)
-            for k, term in enumerate((w * dx, w * dy, w * dz, gauss * screened)):
-                sums[k] += jnp.sum(term.reshape(chunk // 8, 8, TILE), axis=0)
+            for c, term in enumerate((w * dx, w * dy, w * dz, gauss * screened)):
+                sums[c] += jnp.sum(term.reshape(chunk // 8, 8, TILE), axis=0)
+        for c in range(4):
+            parts[c, pl.ds(p, 1), :] = jnp.sum(sums[c], axis=0, keepdims=True)
+
+    def eight_pairs(i, carry):
+        p = 8 * i
+        spread_near(cols_b, p + 4)
         for k in range(4):
-            parts[k, pl.ds(p, 1), :] = jnp.sum(sums[k], axis=0, keepdims=True)
+            one_pair(p + k, cols_a, k)
+        spread_near(cols_a, p + 8)
+        for k in range(4):
+            one_pair(p + 4 + k, cols_b, k)
         return carry
 
     pairs = own_list_ref.shape[1]
+    spread_near(cols_a, 0)
     done = 0
     for c in range(CHUNKS):
         forward(c)
         upto = (c + 1) * STEP_PAIRS if c < CHUNKS - 1 else pairs
-        lax.fori_loop(done, upto, one_pair, 0)
+        lax.fori_loop(done // 8, upto // 8, eight_pairs, 0)
         done = upto
 
     pick = (
@@ -791,7 +821,7 @@
                     corner_copy(w, v, c).wait_send()
 
 
-def halo(positions, charges, features, pairs, count):
+def halo(positions, charges, features, pairs, count, slot_index):
     tiles = charges.shape[0]
     smem = pl.BlockSpec(memory_space=pltpu.SMEM)
     vmem = pl.BlockSpec(memory_space=pltpu.VMEM)
@@ -804,11 +834,14 @@
             jax.ShapeDtypeStruct((9,) + features.shape, features.dtype),
             jax.ShapeDtypeStruct((3, tiles, TILE), jnp.float32),
             jax.ShapeDtypeStruct((tiles, TILE), jnp.float32),
+            jax.ShapeDtypeStruct((SLOTS // 8, slot_index.shape[0], 8), jnp.int32),
         ),
-        in_specs=[smem, smem, vmem, vmem, vmem, hbm],
-        out_specs=(vmem, hbm, vmem, vmem),
+        in_specs=[smem, smem, vmem, vmem, vmem, vmem, hbm],
+        out_specs=(vmem, hbm, vmem, vmem, vmem),
         scratch_shapes=[
             pltpu.VMEM((4, pairs.shape[1], TILE), jnp.float32),
+            pltpu.VMEM((4, TILE, 4 * TILE), jnp.float32),
+            pltpu.VMEM((4, TILE, 4 * TILE), jnp.float32),
             dma((9,)),
             dma((9,)),
             dma((2,)),
@@ -823,7 +856,7 @@
             collective_id=2, has_side_effects=True, vmem_limit_bytes=56 * MIB
         ),
         name="halo",
-    )(pairs, count, positions, charges, pairs, features)
+    )(pairs, count, positions, charges, pairs, slot_index, features)
 
 
 def body(
@@ -844,17 +877,18 @@
 ):
     own_size = atom_features.shape[2]
     own_tiles = own_size // TILE
-    near8, near_features, pair_force, pair_energy = halo(
+    near8, near_features, pair_force, pair_energy, slot_rows = halo(
         positions.reshape(3, own_tiles, TILE),
         charges.reshape(own_tiles, TILE),
         atom_features.reshape(own_size, -1),
         tile_pairs.reshape(2, -1),
         tile_count,
+        slot_index,
     )
     row_force, frag_energy = fragment_model(
         near8,
         near_features,
-        slot_index,
+        slot_rows,
         atom_count,
         cap_weight,
         (w_qkv, w_out, gains, rates, w_read, w_energy),

time: 125 us -> 101 us (0.81)
  Pallas kernels: 121 us -> 96.4 us
    pallas_call x1, Pallas kernels: 54.2 us -> 33.1 us  [halo(): pl.pallas_call(halo_body, out_shape=(jax.ShapeDtypeStruct((9 * tiles, 8,...]
    pallas_call x1, Pallas kernels: 25 us -> 16.9 us  [bring_home(): pl.pallas_call(home_body, out_shape=(jax.ShapeDtypeStruct(block, jnp.floa...]
    pallas_call x1, Pallas kernels: 41.5 us -> 46.3 us  [fragment_model(): pl.pallas_call(fragment_body, out_shape=(jax.ShapeDtypeStruct((tiles // 8...]
where the time goes in v5:
time: 101 us
  Pallas kernels  96.4 us (95%)
  between operations  3.03 us (3%)
  local copies, waits for them, and re-layouts  1.31 us (1%)
    pallas_call x1, Pallas kernels, fragment_model(): pl.pallas_call(fragment_body, out_shape=(jax.ShapeDtypeStruct((tiles // 8...  46.3 us
    pallas_call x1, Pallas kernels, halo(): pl.pallas_call(halo_body, out_shape=(jax.ShapeDtypeStruct((9 * tiles, 8,...  33.1 us
    pallas_call x1, Pallas kernels, bring_home(): pl.pallas_call(home_body, out_shape=(jax.ShapeDtypeStruct(block, jnp.floa...  16.9 us

profile of v5, /device:TPU:1, one launch (start us, length us, event | category | flops | bytes accessed | tf_op | source)
XLA Modules:
  0.0 100.7 jit_solution(10230457975293881907)
XLA Ops:
  1.3 33.1 %halo.1 = (f32[72,8,128]{2,1,0:T(8,128)}, bf16[9,1024,256]{2,1,0:T(8,128)(2,1)}, f32[3,8,128]{2,1,0:T(8,128)}, f32[8,128]{1,0:T(8,128)}, s32[8,48,8]{2,1,0:T(8,128)}) custom-call(s32[2,128]{1,0:T(2,128)} %bitcast.11, s32[1,1]{1,0:T(1,128)S(6)} %copy.20.count_ref, f32[3,8,128]{2,1,0:T(8,128)} %bitcast.9, f32[8,128]{1,0:T(8,128)} %bitcast.10, ...), custom_call_target="tpu_custom_call" | custom-call | tf_op jit(solution)/shard_map/halo/pallas_call | solution.py:830
  34.4 46.3 %fragments.1 = (f32[9,3,8,128]{3,2,1,0:T(8,128)}, f32[8,128]{1,0:T(8,128)}) custom-call(s32[48]{0:T(128)} %count_ref.2, s32[8,48,8]{2,1,0:T(8,128)} %get-tuple-element.11.slot_ref, f32[2,8]{1,0:T(2,128)} %rate_ref.1, f32[72,8,128]{2,1,0:T(8,128)} %get-tuple-element.12.near_ref, bf16[9,1024,256]{2,1,0:T(8,128)(2,1)} %get-tuple-element.13.feat_ref, ...), custom_call_target="tpu_custom_call" | custom-call | tf_op jit(solution)/shard_map/fragments/pallas_call | solution.py:364
  80.7 16.9 %bring_home.1 = (f32[3,8,128]{2,1,0:T(8,128)}, f32[1,1]{1,0:T(1,128)}) custom-call(f32[9,3,8,128]{3,2,1,0:T(8,128)} %get-tuple-element.14.force_ref, f32[3,8,128]{2,1,0:T(8,128)} %get-tuple-element.15.pair_ref, f32[8,128]{1,0:T(8,128)} %get-tuple-element.16.frag_energy_ref, f32[8,128]{1,0:T(8,128)} %get-tuple-element.17.pair_energy_ref), custom_call_target="tpu_custom_call" | custom-call | tf_op jit(solution)/shard_map/bring_home/pallas_call | solution.py:513
  97.6 1.3 %copy.21 = f32[3,1,1,1024]{3,2,1,0:T(1,128)} copy(f32[3,1,1,1024]{3,2,1,0:T(1,128)} %bitcast.8) | data formatting | bytes 24576

commit v6 on v5

--- a/solution.py
+++ b/solution.py
@@ -94,15 +94,29 @@
     span_ref,
     span_cols_ref,
     order_ref,
+    tally,
     bins,
+    landed,
+    landed_sem,
 ):
     tiles = near_ref.shape[0]
     frags = cap_ref.shape[0]
 
+    def eighth_of(f):
+        return (f % (frags // 2)) * (2 * SLOTS // 8) + f // (frags // 2) * (SLOTS // 8)
+
+
+    def feature_copy(i):
+        return pltpu.make_async_copy(feat_ref.at[i], landed.at[i], landed_sem.at[i])
+
+    for i in range(tiles // 8):
+        feature_copy(i).start()
+
     def widen(i, carry):
+        feature_copy(i).wait()
         for k in range(8):
             at = pl.multiple_of(i * 8 * TILE + k * TILE, TILE)
-            both = feat_ref[i, k * TILE : (k + 1) * TILE, :].astype(jnp.float32)
+            both = landed[i, k * TILE : (k + 1) * TILE, :].astype(jnp.float32)
             table[0, pl.ds(at, TILE), :] = both[:, :QUAD]
             table[1, pl.ds(at, TILE), :] = both[:, QUAD:]
             n = jnp.transpose(near_ref[i * 8 + k])
@@ -112,7 +126,6 @@
             forces[pl.ds(at, TILE), :] = jnp.zeros((TILE, TILE), jnp.float32)
         return carry
 
-    lax.fori_loop(0, tiles // 8, widen, 0)
     slot_force[...] = jnp.zeros_like(slot_force)
     head = lax.broadcasted_iota(jnp.int32, (1, HEADS * SLOTS), 1) // SLOTS
     head_col = lax.broadcasted_iota(jnp.int32, (1, F), 1) // (F // HEADS)
@@ -130,17 +143,24 @@
     for f in range(frags):
         wide = jnp.broadcast_to(cols[:SLOTS, f : f + 1], (SLOTS, TILE))
         for k in range(SLOTS // 8):
-            caps[k, f] = wide[k * 8 : (k + 1) * 8]
+            caps[eighth_of(f) + k] = wide[k * 8 : (k + 1) * 8]
     energy_ref[...] = jnp.zeros_like(energy_ref)
 
+    for size in range(16):
+        tally[size] = 0
+    for k in range(frags):
+        size = (count_ref[k] + 7) >> 3
+        tally[size] = tally[size] + 1
     ends = {9: 0}
-    made = 0
     for size in range(8, 1, -1):
-        for k in range(frags):
-            live = count_ref[k]
-            order_ref[made] = live * 64 + k
-            made += jnp.where((live + 7) >> 3 == size, 1, 0)
-        ends[size] = made
+        ends[size] = ends[size + 1] + tally[size]
+        tally[size] = ends[size + 1]
+    for k in range(frags):
+        live = count_ref[k]
+        size = (live + 7) >> 3
+        at = tally[size]
+        order_ref[at] = live * 512 + eighth_of(k)
+        tally[size] = at + 1
     n6, n5, n3, n2 = (ends[k] - ends[k + 1] for k in (6, 5, 3, 2))
     with6 = jnp.minimum(n6, n2)
     with5 = jnp.minimum(n5, n2 - with6 + n3)
@@ -156,11 +176,11 @@
         both = fits & (k < high)
         big = order_ref[k]
         small = order_ref[jnp.maximum(high, 0)]
-        bins[0, k] = big & 63
-        bins[1, k] = small & 63
-        bins[2, k] = big >> 6
-        bins[3, k] = jnp.where(both, ((big >> 6) + 7) & -8, SLOTS)
-        bins[4, k] = jnp.where(both, small >> 6, 0)
+        bins[0, k] = big & 511
+        bins[1, k] = small & 511
+        bins[2, k] = big >> 9
+        bins[3, k] = jnp.where(both, ((big >> 9) + 7) & -8, SLOTS)
+        bins[4, k] = jnp.where(both, small >> 9, 0)
         made = jnp.where(k <= high, k + 1, made)
         high = high - jnp.where(both, 1, 0)
     for k in range(2 * GROUP - 1):
@@ -195,13 +215,12 @@
         big, small, start = (bins[c, which] for c in (0, 1, 3))
         start = start >> 3
         for k in range(SLOTS // 8):
-            early = k < start
-            yield k, jnp.where(early, big, small), k - jnp.where(early, 0, start)
+            yield k, jnp.where(k < start, big, small - start) + k
 
     def gather(b):
         for f in range(GROUP):
-            for k, frag, part in eighths(b * GROUP + f):
-                rs = [slot_ref[part, frag, j] for j in range(8)]
+            for k, part in eighths(b * GROUP + f):
+                rs = [slot_ref[part * 8 + j] for j in range(8)]
                 at = f * SLOTS + k * 8
                 for j in range(8):
                     for c in range(3):
@@ -209,8 +228,8 @@
 
     def scatter(b):
         for f in range(GROUP):
-            for k, frag, part in eighths(b * GROUP + f):
-                rs = [slot_ref[part, frag, j] for j in range(8)]
+            for k, part in eighths(b * GROUP + f):
+                rs = [slot_ref[part * 8 + j] for j in range(8)]
                 old = [forces[pl.ds(r, 1), :] for r in rs]
                 for j in range(8):
                     at = f * SLOTS + k * 8 + j
@@ -242,7 +261,7 @@
             dists.append(jnp.where(mine == owner(slot_lane, -1), square * inverse, FAR))
             inverses.append(inverse)
             offsets.append(off)
-            cap = jnp.concatenate([caps[part, frag] for _, frag, part in eighths(b * GROUP + f)], axis=0)
+            cap = jnp.concatenate([caps[part] for _, part in eighths(b * GROUP + f)], axis=0)
             weights.append(jnp.where(mine > 0, cap, 0.0))
         dist2 = [jnp.concatenate([d, d], axis=1) for d in dists]
         weight = jnp.concatenate(weights, axis=0)
@@ -339,6 +358,7 @@
         slot_force[:, 0:8] = jnp.transpose(packed)
         return carry
 
+    lax.fori_loop(0, tiles // 8, widen, 0)
     gather(0)
     groups = (made + GROUP - 1) // GROUP
     lax.fori_loop(0, groups, one_block, 0)
@@ -367,24 +387,27 @@
             jax.ShapeDtypeStruct((tiles // 8, 3, 8, TILE), jnp.float32),
             jax.ShapeDtypeStruct((8, TILE), jnp.float32),
         ),
-        in_specs=[smem, smem, smem] + [vmem] * 8,
+        in_specs=[smem, smem, smem, vmem, pl.BlockSpec(memory_space=pl.ANY)] + [vmem] * 6,
         out_specs=(vmem, vmem),
         scratch_shapes=[
             pltpu.VMEM((3, tiles * TILE, TILE), jnp.float32),
             pltpu.VMEM((tiles * TILE, TILE), jnp.float32),
             pltpu.VMEM((3, ROWS, TILE), jnp.float32),
             pltpu.VMEM((ROWS, TILE), jnp.float32),
-            pltpu.VMEM((SLOTS // 8, frags, 8, TILE), jnp.float32),
+            pltpu.VMEM((SLOTS // 8 * frags, 8, TILE), jnp.float32),
             pltpu.VMEM((LAYERS, HEADS * SLOTS), jnp.float32),
             pltpu.VMEM((LAYERS, F), jnp.float32),
-            pltpu.SMEM((frags + 1,), jnp.int32),
+            pltpu.SMEM((frags,), jnp.int32),
+            pltpu.SMEM((16,), jnp.int32),
             pltpu.SMEM((5, frags + 2 * GROUP), jnp.int32),
+            pltpu.VMEM(near_features.shape, near_features.dtype),
+            pltpu.SemaphoreType.DMA((tiles // 8,)),
         ],
         compiler_params=pltpu.CompilerParams(vmem_limit_bytes=56 * MIB),
         name="fragments",
     )(
         atom_count,
-        slot_rows,
+        slot_rows.reshape(-1),
         rates,
         near8,
         near_features,
@@ -587,8 +610,8 @@
     part = rows // CHUNKS
     centre = block_of(0, 0) * tiles
 
-    for k in range(SLOTS // 8):
-        rows_ref[k] = slot_ref[:, k * 8 : (k + 1) * 8]
+    rows_ref[:, :SLOTS] = slot_ref[: rows_ref.shape[0]]
+    rows_ref[:, SLOTS:] = slot_ref[rows_ref.shape[0] :]
     near_ref[pl.ds(centre, tiles)] = jnp.zeros((tiles, 8, TILE), jnp.float32)
     for t in range(tiles):
         for c in range(3):
@@ -711,9 +734,6 @@
         == lax.broadcasted_iota(jnp.int32, (32, 4 * TILE), 1) // TILE
     ).astype(jnp.bfloat16)
     chunk = 32
-    rel = lax.broadcasted_iota(jnp.int32, (chunk, TILE), 1) - lax.broadcasted_iota(
-        jnp.int32, (chunk, TILE), 0
-    )
 
     def spread_near(cols, first):
         for k in range(4):
@@ -725,28 +745,27 @@
         near = pairs_ref[1, p]
         o = near_ref[centre + own]
         xi, yi, zi, qi = (o[c : c + 1, :] for c in range(4))
-        same = jnp.where(near == own + centre, 0, 4 * TILE)
         sums = [jnp.zeros((8, TILE), jnp.float32) for _ in range(4)]
         for start in range(0, TILE, chunk):
             xj, yj, zj, qj = (
                 cols[k, start : start + chunk, c * TILE : (c + 1) * TILE] for c in range(4)
             )
             dx, dy, dz = xi - xj, yi - yj, zi - zj
-            qq = jnp.where(rel == same + start, 0.0, qi * qj)
             square = dx * dx + dy * dy + dz * dz + CHARGE_SOFTEN
-            square = jnp.minimum(square, 1e6)
             rinv = lax.rsqrt(square)
-            t = recip(1.0 + (ERFC_P * SCREEN_RATE) * (square * rinv))
+            t = rinv * recip(rinv + ERFC_P * SCREEN_RATE)
             g = ERFC_C[-1]
             for coef in ERFC_C[-2::-1]:
                 g = g * t + coef
-            gauss = qq * jnp.exp2((-SCREEN_RATE * SCREEN_RATE * math.log2(math.e)) * square)
+            gauss = qj * jnp.exp2((-SCREEN_RATE * SCREEN_RATE * math.log2(math.e)) * square)
             screened = (g * t) * rinv
             w = (gauss * (screened + GAUSS)) * (rinv * rinv)
             for c, term in enumerate((w * dx, w * dy, w * dz, gauss * screened)):
                 sums[c] += jnp.sum(term.reshape(chunk // 8, 8, TILE), axis=0)
+        itself = jnp.where(near == own + centre, math.erfc(SCREEN_RATE), 0.0)
         for c in range(4):
-            parts[c, pl.ds(p, 1), :] = jnp.sum(sums[c], axis=0, keepdims=True)
+            row = jnp.sum(sums[c], axis=0, keepdims=True)
+            parts[c, pl.ds(p, 1), :] = qi * (row - itself * qi if c == 3 else row)
 
     def eight_pairs(i, carry):
         p = 8 * i
@@ -834,7 +853,7 @@
             jax.ShapeDtypeStruct((9,) + features.shape, features.dtype),
             jax.ShapeDtypeStruct((3, tiles, TILE), jnp.float32),
             jax.ShapeDtypeStruct((tiles, TILE), jnp.float32),
-            jax.ShapeDtypeStruct((SLOTS // 8, slot_index.shape[0], 8), jnp.int32),
+            jax.ShapeDtypeStruct((slot_index.shape[0] // 2, 2 * SLOTS), jnp.int32),
         ),
         in_specs=[smem, smem, vmem, vmem, vmem, vmem, hbm],
         out_specs=(vmem, hbm, vmem, vmem, vmem),

time: 101 us -> 97.9 us (0.969)
  Pallas kernels: 96.4 us -> 93.2 us
    pallas_call x1, Pallas kernels: 46.3 us -> 37.1 us  [fragment_model(): pl.pallas_call(fragment_body, out_shape=(jax.ShapeDtypeStruct((tiles // 8...]
    pallas_call x1, Pallas kernels: 16.9 us -> 24.3 us  [bring_home(): pl.pallas_call(home_body, out_shape=(jax.ShapeDtypeStruct(block, jnp.floa...]
    pallas_call x1, Pallas kernels: 33.1 us -> 31.9 us  [halo(): pl.pallas_call(halo_body, out_shape=(jax.ShapeDtypeStruct((9 * tiles, 8,...]
where the time goes in v6:
time: 97.9 us; the launch traced here: 97.6 us
  Pallas kernels  93.2 us (95%)
  between operations  3.07 us (3%)
  local copies, waits for them, and re-layouts  1.31 us (1%)
    pallas_call x1, Pallas kernels, fragment_model(): pl.pallas_call(fragment_body, out_shape=(jax.ShapeDtypeStruct((tiles // 8...  37.1 us
    pallas_call x1, Pallas kernels, halo(): pl.pallas_call(halo_body, out_shape=(jax.ShapeDtypeStruct((9 * tiles, 8,...  31.9 us
    pallas_call x1, Pallas kernels, bring_home(): pl.pallas_call(home_body, out_shape=(jax.ShapeDtypeStruct(block, jnp.floa...  24.3 us

profile of v6, /device:TPU:1, one launch (start us, length us, event | category | flops | bytes accessed | tf_op | source)
XLA Modules:
  0.0 97.6 jit_solution(10635443318997831293)
XLA Ops:
  1.3 31.9 %halo.1 = (f32[72,8,128]{2,1,0:T(8,128)}, bf16[9,1024,256]{2,1,0:T(8,128)(2,1)}, f32[3,8,128]{2,1,0:T(8,128)}, f32[8,128]{1,0:T(8,128)}, s32[24,128]{1,0:T(8,128)}) custom-call(s32[2,128]{1,0:T(2,128)} %bitcast.13, s32[1,1]{1,0:T(1,128)S(6)} %copy.20.count_ref, f32[3,8,128]{2,1,0:T(8,128)} %bitcast.10, f32[8,128]{1,0:T(8,128)} %bitcast.12, ...), custom_call_target="tpu_custom_call" | custom-call | tf_op jit(solution)/shard_map/halo/pallas_call | solution.py:849
  33.2 37.1 %fragments.1 = (f32[9,3,8,128]{3,2,1,0:T(8,128)}, f32[8,128]{1,0:T(8,128)}) custom-call(s32[48]{0:T(128)} %count_ref.2, s32[3072]{0:T(1024)} %bitcast.11, f32[2,8]{1,0:T(2,128)} %rate_ref.1, f32[72,8,128]{2,1,0:T(8,128)} %get-tuple-element.12.near_ref, bf16[9,1024,256]{2,1,0:T(8,128)(2,1)} %get-tuple-element.13.feat_ref, f32[48,64]{1,0:T(8,128)} %cap_ref.1, ...), custom_call_target="tpu_custom_call" | custom-call | tf_op jit(solution)/shard_map/fragments/pallas_call | solution.py:384
  70.2 24.3 %bring_home.1 = (f32[3,8,128]{2,1,0:T(8,128)}, f32[1,1]{1,0:T(1,128)}) custom-call(f32[9,3,8,128]{3,2,1,0:T(8,128)} %get-tuple-element.14.force_ref, f32[3,8,128]{2,1,0:T(8,128)} %get-tuple-element.15.pair_ref, f32[8,128]{1,0:T(8,128)} %get-tuple-element.16.frag_energy_ref, f32[8,128]{1,0:T(8,128)} %get-tuple-element.17.pair_energy_ref), custom_call_target="tpu_custom_call" | custom-call | tf_op jit(solution)/shard_map/bring_home/pallas_call | solution.py:536
  94.5 1.3 %copy.21 = f32[3,1,1,1024]{3,2,1,0:T(1,128)} copy(f32[3,1,1,1024]{3,2,1,0:T(1,128)} %bitcast.9) | data formatting | bytes 24576

commit v7 on v6

--- a/solution.py
+++ b/solution.py
@@ -117,12 +117,10 @@
         for k in range(8):
             at = pl.multiple_of(i * 8 * TILE + k * TILE, TILE)
             both = landed[i, k * TILE : (k + 1) * TILE, :].astype(jnp.float32)
-            table[0, pl.ds(at, TILE), :] = both[:, :QUAD]
-            table[1, pl.ds(at, TILE), :] = both[:, QUAD:]
             n = jnp.transpose(near_ref[i * 8 + k])
-            table[2, pl.ds(at, TILE), :] = jnp.concatenate(
-                [n, jnp.zeros((TILE, TILE - 8), jnp.float32)], axis=1
-            )
+            atoms = jnp.concatenate([n, jnp.zeros((TILE, TILE - 8), jnp.float32)], axis=1)
+            for c, part in enumerate((both[:, :QUAD], both[:, QUAD:], atoms)):
+                table[pl.ds(at * 4 + c, TILE, stride=4), :] = part
             forces[pl.ds(at, TILE), :] = jnp.zeros((TILE, TILE), jnp.float32)
         return carry
 
@@ -137,9 +135,9 @@
             cols = jnp.where(head_col == h, rate_ref[layer, h], cols)
         span_ref[layer : layer + 1, :] = 1.0 / wide
         span_cols_ref[layer : layer + 1, :] = 1.0 / cols
-    slots[0, :TILE, :] = jnp.zeros((TILE, TILE), jnp.float32)
-    slots[0, :frags, :SLOTS] = cap_ref[...]
-    cols = jnp.transpose(slots[0, :TILE, :])
+    slots[:TILE, :] = jnp.zeros((TILE, TILE), jnp.float32)
+    slots[:frags, :SLOTS] = cap_ref[...]
+    cols = jnp.transpose(slots[:TILE, :])
     for f in range(frags):
         wide = jnp.broadcast_to(cols[:SLOTS, f : f + 1], (SLOTS, TILE))
         for k in range(SLOTS // 8):
@@ -223,8 +221,8 @@
                 rs = [slot_ref[part * 8 + j] for j in range(8)]
                 at = f * SLOTS + k * 8
                 for j in range(8):
-                    for c in range(3):
-                        slots[c, at + j : at + j + 1, :] = table[c, pl.ds(rs[j], 1), :]
+                    row = pl.multiple_of(rs[j] * 4, 4)
+                    slots[4 * (at + j) : 4 * (at + j) + 4, :] = table[pl.ds(row, 4), :]
 
     def scatter(b):
         for f in range(GROUP):
@@ -234,13 +232,14 @@
                 for j in range(8):
                     at = f * SLOTS + k * 8 + j
                     forces[pl.ds(rs[j], 1), :] = old[j] + slot_force[at : at + 1, :]
+        return forces[pl.ds(rs[7], 1), :]
 
     def one_block(b, carry):
         info = [tuple(bins[c, b * GROUP + f] for c in (2, 3, 4)) for f in range(GROUP)]
-        h0 = jnp.concatenate([slots[0], slots[1]], axis=1)
-        atoms = slots[2]
+        h0 = jnp.concatenate([slots[pl.ds(c, ROWS, stride=4), :] for c in range(2)], axis=1)
+        atoms = slots[pl.ds(2, ROWS, stride=4), :]
         gather(b + 1)
-        scatter(jnp.maximum(b - 1, 0))
+        last = scatter(jnp.maximum(b - 1, 0))
 
         atom_rows = jnp.transpose(atoms)
         dists, inverses, offsets, weights = [], [], [], []
@@ -307,7 +306,7 @@
         u = 0.5 * dot(bf16(unit2 * gain[2]), wread_ref[...])
         th = jnp.tanh(u)
         silu = u + u * th
-        weighted = weight * wen_ref[...]
+        weighted = weight * (wen_ref[...] + 0.0 * last)
         energy_ref[...] += jnp.sum((weighted * silu).reshape(ROWS // 8, 8, QUAD), axis=0)
 
         dread = bf16((0.5 * weighted) * ((1.0 + th) + (silu - silu * th)))
@@ -390,9 +389,9 @@
         in_specs=[smem, smem, smem, vmem, pl.BlockSpec(memory_space=pl.ANY)] + [vmem] * 6,
         out_specs=(vmem, vmem),
         scratch_shapes=[
-            pltpu.VMEM((3, tiles * TILE, TILE), jnp.float32),
+            pltpu.VMEM((4 * tiles * TILE, TILE), jnp.float32),
             pltpu.VMEM((tiles * TILE, TILE), jnp.float32),
-            pltpu.VMEM((3, ROWS, TILE), jnp.float32),
+            pltpu.VMEM((4 * ROWS, TILE), jnp.float32),
             pltpu.VMEM((ROWS, TILE), jnp.float32),
             pltpu.VMEM((SLOTS // 8 * frags, 8, TILE), jnp.float32),
             pltpu.VMEM((LAYERS, HEADS * SLOTS), jnp.float32),
@@ -769,16 +768,17 @@
 
     def eight_pairs(i, carry):
         p = 8 * i
-        spread_near(cols_b, p + 4)
         for k in range(4):
             one_pair(p + k, cols_a, k)
         spread_near(cols_a, p + 8)
         for k in range(4):
             one_pair(p + 4 + k, cols_b, k)
+        spread_near(cols_b, p + 12)
         return carry
 
     pairs = own_list_ref.shape[1]
     spread_near(cols_a, 0)
+    spread_near(cols_b, 4)
     done = 0
     for c in range(CHUNKS):
         forward(c)

time: 97.9 us -> 96.2 us (0.983)
  Pallas kernels: 93.2 us -> 91.6 us
where the time goes in v7:
time: 96.2 us; the launch traced here: 95.9 us
  Pallas kernels  91.6 us (95%)
  between operations  3.07 us (3%)
  local copies, waits for them, and re-layouts  1.31 us (1%)
    pallas_call x1, Pallas kernels, fragment_model(): pl.pallas_call(fragment_body, out_shape=(jax.ShapeDtypeStruct((tiles // 8...  36.2 us
    pallas_call x1, Pallas kernels, halo(): pl.pallas_call(halo_body, out_shape=(jax.ShapeDtypeStruct((9 * tiles, 8,...  31.4 us
    pallas_call x1, Pallas kernels, bring_home(): pl.pallas_call(home_body, out_shape=(jax.ShapeDtypeStruct(block, jnp.floa...  23.9 us

profile of v7, /device:TPU:1, one launch (start us, length us, event | category | flops | bytes accessed | tf_op | source)
XLA Modules:
  0.0 95.9 jit_solution(9065985507794670794)
XLA Ops:
  1.3 31.4 %halo.1 = (f32[72,8,128]{2,1,0:T(8,128)}, bf16[9,1024,256]{2,1,0:T(8,128)(2,1)}, f32[3,8,128]{2,1,0:T(8,128)}, f32[8,128]{1,0:T(8,128)}, s32[24,128]{1,0:T(8,128)}) custom-call(s32[2,128]{1,0:T(2,128)} %bitcast.13, s32[1,1]{1,0:T(1,128)S(6)} %copy.20.count_ref, f32[3,8,128]{2,1,0:T(8,128)} %bitcast.10, f32[8,128]{1,0:T(8,128)} %bitcast.12, ...), custom_call_target="tpu_custom_call" | custom-call | tf_op jit(solution)/shard_map/halo/pallas_call | solution.py:849
  32.7 36.2 %fragments.1 = (f32[9,3,8,128]{3,2,1,0:T(8,128)}, f32[8,128]{1,0:T(8,128)}) custom-call(s32[48]{0:T(128)} %count_ref.2, s32[3072]{0:T(1024)} %bitcast.11, f32[2,8]{1,0:T(2,128)} %rate_ref.1, f32[72,8,128]{2,1,0:T(8,128)} %get-tuple-element.12.near_ref, bf16[9,1024,256]{2,1,0:T(8,128)(2,1)} %get-tuple-element.13.feat_ref, f32[48,64]{1,0:T(8,128)} %cap_ref.1, ...), custom_call_target="tpu_custom_call" | custom-call | tf_op jit(solution)/shard_map/fragments/pallas_call | solution.py:383
  68.9 23.9 %bring_home.1 = (f32[3,8,128]{2,1,0:T(8,128)}, f32[1,1]{1,0:T(1,128)}) custom-call(f32[9,3,8,128]{3,2,1,0:T(8,128)} %get-tuple-element.14.force_ref, f32[3,8,128]{2,1,0:T(8,128)} %get-tuple-element.15.pair_ref, f32[8,128]{1,0:T(8,128)} %get-tuple-element.16.frag_energy_ref, f32[8,128]{1,0:T(8,128)} %get-tuple-element.17.pair_energy_ref), custom_call_target="tpu_custom_call" | custom-call | tf_op jit(solution)/shard_map/bring_home/pallas_call | solution.py:535
  92.9 1.3 %copy.21 = f32[3,1,1,1024]{3,2,1,0:T(1,128)} copy(f32[3,1,1,1024]{3,2,1,0:T(1,128)} %bitcast.9) | data formatting | bytes 24576

commit v8 on v7

--- a/solution.py
+++ b/solution.py
@@ -780,11 +780,12 @@
     spread_near(cols_a, 0)
     spread_near(cols_b, 4)
     done = 0
-    for c in range(CHUNKS):
-        forward(c)
-        upto = (c + 1) * STEP_PAIRS if c < CHUNKS - 1 else pairs
+    for c in range(CHUNKS + 1):
+        upto = (c + 1) * STEP_PAIRS if c < CHUNKS else pairs
         lax.fori_loop(done // 8, upto // 8, eight_pairs, 0)
         done = upto
+        if c < CHUNKS:
+            forward(c)
 
     pick = (
         (own_list_ref[0:1, :] == lax.broadcasted_iota(jnp.int32, (16, pairs), 0))

time: 96.2 us -> 94.5 us (0.982)
  Pallas kernels: 91.6 us -> 89.9 us
    pallas_call x1, Pallas kernels: 36.2 us -> 43.2 us  [fragment_model(): pl.pallas_call(fragment_body, out_shape=(jax.ShapeDtypeStruct((tiles // 8...]
    pallas_call x1, Pallas kernels: 23.9 us -> 17.2 us  [bring_home(): pl.pallas_call(home_body, out_shape=(jax.ShapeDtypeStruct(block, jnp.floa...]
    pallas_call x1, Pallas kernels: 31.4 us -> 29.4 us  [halo(): pl.pallas_call(halo_body, out_shape=(jax.ShapeDtypeStruct((9 * tiles, 8,...]
where the time goes in v8:
time: 94.5 us; the launch traced here: 94.2 us
  Pallas kernels  89.9 us (95%)
  between operations  3.07 us (3%)
  local copies, waits for them, and re-layouts  1.31 us (1%)
    pallas_call x1, Pallas kernels, fragment_model(): pl.pallas_call(fragment_body, out_shape=(jax.ShapeDtypeStruct((tiles // 8...  43.2 us
    pallas_call x1, Pallas kernels, halo(): pl.pallas_call(halo_body, out_shape=(jax.ShapeDtypeStruct((9 * tiles, 8,...  29.4 us
    pallas_call x1, Pallas kernels, bring_home(): pl.pallas_call(home_body, out_shape=(jax.ShapeDtypeStruct(block, jnp.floa...  17.2 us

profile of v8, /device:TPU:1, one launch (start us, length us, event | category | flops | bytes accessed | tf_op | source)
XLA Modules:
  0.0 94.2 jit_solution(14405495810875947020)
XLA Ops:
  1.3 29.4 %halo.1 = (f32[72,8,128]{2,1,0:T(8,128)}, bf16[9,1024,256]{2,1,0:T(8,128)(2,1)}, f32[3,8,128]{2,1,0:T(8,128)}, f32[8,128]{1,0:T(8,128)}, s32[24,128]{1,0:T(8,128)}) custom-call(s32[2,128]{1,0:T(2,128)} %bitcast.13, s32[1,1]{1,0:T(1,128)S(6)} %copy.20.count_ref, f32[3,8,128]{2,1,0:T(8,128)} %bitcast.10, f32[8,128]{1,0:T(8,128)} %bitcast.12, ...), custom_call_target="tpu_custom_call" | custom-call | tf_op jit(solution)/shard_map/halo/pallas_call | solution.py:850
  30.7 43.2 %fragments.1 = (f32[9,3,8,128]{3,2,1,0:T(8,128)}, f32[8,128]{1,0:T(8,128)}) custom-call(s32[48]{0:T(128)} %count_ref.2, s32[3072]{0:T(1024)} %bitcast.11, f32[2,8]{1,0:T(2,128)} %rate_ref.1, f32[72,8,128]{2,1,0:T(8,128)} %get-tuple-element.12.near_ref, bf16[9,1024,256]{2,1,0:T(8,128)(2,1)} %get-tuple-element.13.feat_ref, f32[48,64]{1,0:T(8,128)} %cap_ref.1, ...), custom_call_target="tpu_custom_call" | custom-call | tf_op jit(solution)/shard_map/fragments/pallas_call | solution.py:383
  73.9 17.2 %bring_home.1 = (f32[3,8,128]{2,1,0:T(8,128)}, f32[1,1]{1,0:T(1,128)}) custom-call(f32[9,3,8,128]{3,2,1,0:T(8,128)} %get-tuple-element.14.force_ref, f32[3,8,128]{2,1,0:T(8,128)} %get-tuple-element.15.pair_ref, f32[8,128]{1,0:T(8,128)} %get-tuple-element.16.frag_energy_ref, f32[8,128]{1,0:T(8,128)} %get-tuple-element.17.pair_energy_ref), custom_call_target="tpu_custom_call" | custom-call | tf_op jit(solution)/shard_map/bring_home/pallas_call | solution.py:535
  91.2 1.3 %copy.21 = f32[3,1,1,1024]{3,2,1,0:T(1,128)} copy(f32[3,1,1,1024]{3,2,1,0:T(1,128)} %bitcast.9) | data formatting | bytes 24576

commit v9 on v8

--- a/solution.py
+++ b/solution.py
@@ -559,7 +559,7 @@
 
 
 AROUND = [(u, v) for u in (-1, 0, 1) for v in (-1, 0, 1) if (u, v) != (0, 0)]
-CHUNKS = 4
+CHUNKS = 2
 
 
 STEP_PAIRS = 16
@@ -735,7 +735,7 @@
     chunk = 32
 
     def spread_near(cols, first):
-        for k in range(4):
+        for k in range(8):
             near = pairs_ref[1, jnp.minimum(first + k, pairs - 1)]
             cols[k] = dot_tn(bf16(jnp.concatenate(three_parts(near_ref[near]), axis=0)), spread)
 
@@ -766,23 +766,23 @@
             row = jnp.sum(sums[c], axis=0, keepdims=True)
             parts[c, pl.ds(p, 1), :] = qi * (row - itself * qi if c == 3 else row)
 
-    def eight_pairs(i, carry):
-        p = 8 * i
-        for k in range(4):
+    def sixteen_pairs(i, carry):
+        p = 16 * i
+        for k in range(8):
             one_pair(p + k, cols_a, k)
-        spread_near(cols_a, p + 8)
-        for k in range(4):
-            one_pair(p + 4 + k, cols_b, k)
-        spread_near(cols_b, p + 12)
+        spread_near(cols_a, p + 16)
+        for k in range(8):
+            one_pair(p + 8 + k, cols_b, k)
+        spread_near(cols_b, p + 24)
         return carry
 
     pairs = own_list_ref.shape[1]
     spread_near(cols_a, 0)
-    spread_near(cols_b, 4)
+    spread_near(cols_b, 8)
     done = 0
     for c in range(CHUNKS + 1):
         upto = (c + 1) * STEP_PAIRS if c < CHUNKS else pairs
-        lax.fori_loop(done // 8, upto // 8, eight_pairs, 0)
+        lax.fori_loop(done // 16, upto // 16, sixteen_pairs, 0)
         done = upto
         if c < CHUNKS:
             forward(c)
@@ -860,8 +860,8 @@
         out_specs=(vmem, hbm, vmem, vmem, vmem),
         scratch_shapes=[
             pltpu.VMEM((4, pairs.shape[1], TILE), jnp.float32),
-            pltpu.VMEM((4, TILE, 4 * TILE), jnp.float32),
-            pltpu.VMEM((4, TILE, 4 * TILE), jnp.float32),
+            pltpu.VMEM((8, TILE, 4 * TILE), jnp.float32),
+            pltpu.VMEM((8, TILE, 4 * TILE), jnp.float32),
             dma((9,)),
             dma((9,)),
             dma((2,)),

time: 94.5 us -> 98.2 us (1.039)
  Pallas kernels: 89.9 us -> 93.6 us
    pallas_call x1, Pallas kernels: 17.2 us -> 24.8 us  [bring_home(): pl.pallas_call(home_body, out_shape=(jax.ShapeDtypeStruct(block, jnp.floa...]
    pallas_call x1, Pallas kernels: 43.2 us -> 36.2 us  [fragment_model(): pl.pallas_call(fragment_body, out_shape=(jax.ShapeDtypeStruct((tiles // 8...]
    pallas_call x1, Pallas kernels: 29.4 us -> 32.6 us  [halo(): pl.pallas_call(halo_body, out_shape=(jax.ShapeDtypeStruct((9 * tiles, 8,...]
where the time goes in v9:
time: 98.2 us; the launch traced here: 98 us
  Pallas kernels  93.6 us (95%)
  between operations  3.07 us (3%)
  local copies, waits for them, and re-layouts  1.31 us (1%)
    pallas_call x1, Pallas kernels, fragment_model(): pl.pallas_call(fragment_body, out_shape=(jax.ShapeDtypeStruct((tiles // 8...  36.2 us
    pallas_call x1, Pallas kernels, halo(): pl.pallas_call(halo_body, out_shape=(jax.ShapeDtypeStruct((9 * tiles, 8,...  32.6 us
    pallas_call x1, Pallas kernels, bring_home(): pl.pallas_call(home_body, out_shape=(jax.ShapeDtypeStruct(block, jnp.floa...  24.8 us

profile of v9, /device:TPU:1, one launch (start us, length us, event | category | flops | bytes accessed | tf_op | source)
XLA Modules:
  0.0 98.0 jit_solution(5715420867345652508)
XLA Ops:
  1.3 32.6 %halo.1 = (f32[72,8,128]{2,1,0:T(8,128)}, bf16[9,1024,256]{2,1,0:T(8,128)(2,1)}, f32[3,8,128]{2,1,0:T(8,128)}, f32[8,128]{1,0:T(8,128)}, s32[24,128]{1,0:T(8,128)}) custom-call(s32[2,128]{1,0:T(2,128)} %bitcast.13, s32[1,1]{1,0:T(1,128)S(6)} %copy.20.count_ref, f32[3,8,128]{2,1,0:T(8,128)} %bitcast.10, f32[8,128]{1,0:T(8,128)} %bitcast.12, ...), custom_call_target="tpu_custom_call" | custom-call | tf_op jit(solution)/shard_map/halo/pallas_call | solution.py:850
  33.8 36.2 %fragments.1 = (f32[9,3,8,128]{3,2,1,0:T(8,128)}, f32[8,128]{1,0:T(8,128)}) custom-call(s32[48]{0:T(128)} %count_ref.2, s32[3072]{0:T(1024)} %bitcast.11, f32[2,8]{1,0:T(2,128)} %rate_ref.1, f32[72,8,128]{2,1,0:T(8,128)} %get-tuple-element.12.near_ref, bf16[9,1024,256]{2,1,0:T(8,128)(2,1)} %get-tuple-element.13.feat_ref, f32[48,64]{1,0:T(8,128)} %cap_ref.1, ...), custom_call_target="tpu_custom_call" | custom-call | tf_op jit(solution)/shard_map/fragments/pallas_call | solution.py:383
  70.1 24.8 %bring_home.1 = (f32[3,8,128]{2,1,0:T(8,128)}, f32[1,1]{1,0:T(1,128)}) custom-call(f32[9,3,8,128]{3,2,1,0:T(8,128)} %get-tuple-element.14.force_ref, f32[3,8,128]{2,1,0:T(8,128)} %get-tuple-element.15.pair_ref, f32[8,128]{1,0:T(8,128)} %get-tuple-element.16.frag_energy_ref, f32[8,128]{1,0:T(8,128)} %get-tuple-element.17.pair_energy_ref), custom_call_target="tpu_custom_call" | custom-call | tf_op jit(solution)/shard_map/bring_home/pallas_call | solution.py:535
  94.9 1.3 %copy.21 = f32[3,1,1,1024]{3,2,1,0:T(1,128)} copy(f32[3,1,1,1024]{3,2,1,0:T(1,128)} %bitcast.9) | data formatting | bytes 24576
